TPU v7x, 128 devices: a whole 4x4x4 slice. The times are simulated.
128 devices in a mesh: dp: 4 (over x), fsdp: 32 (over y, z, core).
Axes of the slice: x: 4, y: 4, z: 4, core: 2. Of those that a mesh axis runs over, the one named last changes fastest.
Arguments:
- log_mel: bfloat16 [16384, 16, 128], P(('dp', 'fsdp')), may hold values from -10 to 10
- bucket_list: int32 [128, 128], P(('dp', 'fsdp')), may hold values from 0 to 127, each once within a row
- utterance_frames: int32 [512], P(('dp', 'fsdp')), may hold values from 256 to 512
- stem_weight: bfloat16 [16, 48], replicated, may hold values from -3 to 3
- first_gain: float32 [1536], replicated, may hold values from 0.5 to 1.5
- gate_proj: bfloat16 [1536, 3072], P('fsdp'), may hold values from -0.15625 to 0.15625
- conv_kernel: float32 [31, 1536], replicated, may hold values from -3 to 3
- second_gain: float32 [1536], replicated, may hold values from 0.5 to 1.5
- out_proj: bfloat16 [1536, 1536], P('fsdp'), may hold values from -0.15625 to 0.15625
- cotangent: bfloat16 [65536, 1536], P(('dp', 'fsdp')), may hold values from -0.125 to 0.125
Outputs:
- output: bfloat16 [65536, 1536], P(('dp', 'fsdp'))
- grad_gate: float32 [1536, 3072], P('fsdp')
- grad_out: float32 [1536, 1536], P('fsdp')
- grad_stem: float32 [16, 48], replicated
- grad_first: float32 [1536], replicated
- grad_conv: float32 [31, 1536], replicated
- grad_second: float32 [1536], replicated
Inputs may be any that keep to these rules, and one draw needn't show every extreme that they name: `bucket_list`: each row names each number once.
All inputs are finite; a program needn't handle non-finite values.
Results may differ from a plain program's by a relative error of at most 0.024.
Values may be sent and summed in bfloat16 or wider, within the bound.
No kernel may reach another device: no remote copies, remote signals or barrier semaphores. Data moves between devices by JAX's collectives and lax.ppermute only.
A program may use at most 320 MiB of HBM per device.

v0:
```python
from functools import partial

import jax
import jax.numpy as jnp
from jax import lax
from jax.sharding import PartitionSpec as P

PATCH = 4
UTT_TOK = 128


EPSILON = 1e-05


def norm_rows(values, gain):
    centre = jnp.mean(values, axis=-1, keepdims=True)
    centred = values - centre
    spread = jnp.mean(centred * centred, axis=-1, keepdims=True)
    return centred * lax.rsqrt(spread + EPSILON) * gain


def depthwise(blocks, conv_kernel):
    tap_count = conv_kernel.shape[0]
    half_width = tap_count // 2
    length = blocks.shape[1]
    padded = jnp.pad(blocks, ((0, 0), (half_width, half_width), (0, 0)))
    summed = jnp.zeros(blocks.shape, jnp.float32)
    for offset in range(tap_count):
        summed = summed + padded[:, offset : offset + length, :] * conv_kernel[offset]
    return summed


def middle(valid_mask, activated, conv_kernel, second_gain):
    features = conv_kernel.shape[1]
    gated = activated[:, :features] * jax.nn.sigmoid(activated[:, features:]) * valid_mask
    blocks = gated.reshape(-1, UTT_TOK, features)
    filtered = depthwise(blocks, conv_kernel).reshape(gated.shape)
    return jax.nn.silu(norm_rows(filtered, second_gain))


def token_mask(utterance_frames):
    positions = lax.broadcasted_iota(jnp.int32, (utterance_frames.shape[0], UTT_TOK), 1)
    limits = (utterance_frames // PATCH)[:, None]
    return (positions < limits).astype(jnp.float32).reshape(-1, 1)


def stem_sum(frames, stem_weight):
    rows = frames.shape[0]
    groups = frames.shape[1] // (PATCH * PATCH)
    split_in = frames.reshape(rows, PATCH, groups, PATCH)
    kernel = stem_weight.reshape(PATCH, PATCH, -1)
    summed = jnp.einsum("tigj,ijc->tgc", split_in, kernel, preferred_element_type=jnp.float32)
    return summed.reshape(rows, -1)


def stem_weight_grad(frames, pre_grad):
    rows = frames.shape[0]
    groups = frames.shape[1] // (PATCH * PATCH)
    split_in = frames.reshape(rows, PATCH, groups, PATCH)
    split_grad = pre_grad.reshape(rows, groups, -1)
    summed = jnp.einsum("tigj,tgc->ijc", split_in, split_grad, preferred_element_type=jnp.float32)
    return summed.reshape(PATCH * PATCH, -1)


def body(
    log_mel,
    bucket_list,
    utterance_frames,
    stem_weight,
    first_gain,
    gate_proj,
    conv_kernel,
    second_gain,
    out_proj,
    cotangent,
):
    slot_order = bucket_list[0]
    outgoing = jnp.take(log_mel, slot_order, axis=0)
    arrived = lax.all_to_all(outgoing, ("dp", "fsdp"), split_axis=0, concat_axis=0, tiled=True)
    token_rows = arrived.size // (PATCH * log_mel.shape[2])
    frames = arrived.reshape(token_rows, PATCH * log_mel.shape[2])
    valid_mask = token_mask(utterance_frames)
    mask_narrow = valid_mask.astype(jnp.bfloat16)
    stem_total = stem_sum(frames, stem_weight)
    embedded = jax.nn.silu(stem_total).astype(jnp.bfloat16) * mask_narrow
    embed_wide = embedded.astype(jnp.float32)
    normed = norm_rows(embed_wide, first_gain).astype(jnp.bfloat16)
    gate_full, out_full = (
        lax.all_gather(gate_proj, "fsdp", axis=0, tiled=True),
        lax.all_gather(out_proj, "fsdp", axis=0, tiled=True),
    )
    activated = jnp.dot(normed, gate_full, preferred_element_type=jnp.float32)
    swish_wide = middle(valid_mask, activated, conv_kernel, second_gain)
    swished = swish_wide.astype(jnp.bfloat16)
    mixed = jnp.dot(swished, out_full, preferred_element_type=jnp.float32)
    output = ((embed_wide + mixed) * valid_mask).astype(jnp.bfloat16)
    mix_grad = cotangent * mask_narrow
    swish_grad = lax.dot_general(
        mix_grad, out_full, (((1,), (1,)), ((), ())), preferred_element_type=jnp.float32
    )
    unused, middle_back = jax.vjp(partial(middle, valid_mask), activated, conv_kernel, second_gain)
    act_wide, conv_grad, second_grad = middle_back(swish_grad)
    act_grad = act_wide.astype(jnp.bfloat16)
    normed_grad = lax.dot_general(
        act_grad, gate_full, (((1,), (1,)), ((), ())), preferred_element_type=jnp.float32
    )
    unused, norm_back = jax.vjp(norm_rows, embed_wide, first_gain)
    embed_grad, first_grad = norm_back(normed_grad)
    embed_grad = (embed_grad + mix_grad.astype(jnp.float32)) * valid_mask
    unused, silu_back = jax.vjp(jax.nn.silu, stem_total)
    pre_grad = silu_back(embed_grad)[0].astype(jnp.bfloat16)
    stem_grad = stem_weight_grad(frames, pre_grad)
    gate_term = lax.dot_general(
        normed, act_grad, (((0,), (0,)), ((), ())), preferred_element_type=jnp.float32
    )
    out_term = lax.dot_general(
        swished, mix_grad, (((0,), (0,)), ((), ())), preferred_element_type=jnp.float32
    )
    portion = lax.psum_scatter(
        jnp.concatenate([gate_term, out_term], axis=1).astype(jnp.bfloat16),
        "fsdp",
        scatter_dimension=0,
        tiled=True,
    ).astype(jnp.float32)
    portion = lax.psum(portion.astype(jnp.bfloat16), "dp").astype(jnp.float32)
    gate_cols = gate_proj.shape[1]
    small = lax.psum((stem_grad, first_grad, conv_grad, second_grad), ("dp", "fsdp"))
    return (
        output,
        portion[:, :gate_cols],
        portion[:, gate_cols:],
        small[0],
        small[1],
        small[2],
        small[3],
    )


def solution(mesh):
    return jax.shard_map(
        body,
        mesh=mesh,
        in_specs=(
            P(("dp", "fsdp"), None, None),
            P(("dp", "fsdp"), None),
            P(("dp", "fsdp")),
            P(),
            P(),
            P("fsdp", None),
            P(),
            P(),
            P("fsdp", None),
            P(("dp", "fsdp"), None),
        ),
        out_specs=(P(("dp", "fsdp"), None), P("fsdp", None), P("fsdp", None), P(), P(), P(), P()),
        check_vma=False,
    )
```

profile of v0, /device:TPU:1, one launch (start us, length us, event | category | flops | bytes accessed | tf_op | source)
XLA Modules:
  0.0 545.8 jit_solution(12234877702823997050)
XLA Ops:
  7.3 0.7 all-gather.3.cloned.1.call-update
  8.0 0.7 all-gather.5.cloned.1.call-update
  8.7 0.7 fusion.40
  9.4 0.7 gather_fusion
  10.1 0.7 compare_and_fusion
  10.7 1.0 broadcast_select_fusion
  11.7 11.5 %all-to-all-start = ((bf16[128,16,128]{2,1,0:T(8,128)(2,1)}), bf16[128,16,128]{2,1,0:T(8,128)(2,1)S(1)}, u32[]{:S(2)}, u32[]{:S(2)}) async-start(bf16[128,16,128]{2,1,0:T(8,128)(2,1)} %broadcast_select_fusion), calls=%async_computation | async-start | bytes 1048576 | tf_op jit(solution)/shard_map/all_to_all | solution.py:79
  23.3 0.3 slice_reduce_fusion.30
  23.9 13.0 %all-to-all-done = bf16[128,16,128]{2,1,0:T(8,128)(2,1)S(1)} async-done(((bf16[128,16,128]{2,1,0:T(8,128)(2,1)}), bf16[128,16,128]{2,1,0:T(8,128)(2,1)S(1)}, u32[]{:S(2)}, u32[]{:S(2)}) %all-to-all-start) | async-done | bytes 524320 | tf_op jit(solution)/shard_map/all_to_all | solution.py:79
  36.9 36.9 %reshape_reshape.4 = bf16[512,4,32,4]{3,2,1,0:T(8,128)(2,1)} reshape(bf16[128,16,128]{2,1,0:T(8,128)(2,1)S(1)} %all-to-all-done) | data formatting | bytes 1048576 | tf_op jit(solution)/shard_map/reshape;reshape | solution.py:50
  73.9 18.8 %convert_reduce_fusion = (f32[512]{0:T(512)S(1)}, bf16[512,32,48]{0,2,1:T(8,128)(2,1)}, f32[512,32,48,1]{0,2,3,1:T(8,128)}) fusion(bf16[512]{0:T(512)(128)(2,1)S(1)} %get-tuple-element.120, bf16[4,4,48,1]{2,1,0,3:T(4,128)(2,1)S(1)} %bitcast.119, bf16[512,4,32,4]{3,2,1,0:T(8,128)(2,1)} %reshape_reshape.4), kind=kOutput, calls=%fused_computation.44 | convolution fusion | flops 31456768 | bytes 5247488 | tf_op jit(solution)/shard_map/tigj,ijc->tgc/dot_general | solution.py:52
  92.7 2.4 copy.24
  95.1 3.0 fusion.12
  98.1 2.0 fusion.29
  100.1 8.7 %fusion.46 = f32[512,3072]{1,0:T(8,128)S(1)} fusion(bf16[1536,3072]{1,0:T(8,128)(2,1)} %all-gather.3.cloned.1.call-done, bf16[512,1536]{1,0:T(8,128)(2,1)} %fusion.29, f32[1536]{0:T(1024)S(1)} %copy-done.14, f32[512]{0:T(512)S(1)} %fusion.39, f32[512]{0:T(512)S(1)} %broadcast_multiply_fusion.32), kind=kOutput, calls=%fused_computation.225 | convolution fusion | flops 4835770368 | bytes 17311744 | tf_op jit(solution)/shard_map/dot_general | solution.py:92
  108.8 0.8 multiply_multiply_fusion
  109.6 1.8 copy-done.2
  111.4 16.5 %fusion.50 = (f32[4,128]{1,0:T(4,128)S(1)}, f32[4,128,1536]{2,1,0:T(8,128)S(1)}) fusion(f32[1536]{0:T(1024)S(1)} %get-tuple-element.70, f32[1536]{0:T(1024)S(1)} %get-tuple-element.71, f32[1536]{0:T(1024)S(1)} %get-tuple-element.42, f32[1536]{0:T(1024)S(1)} %get-tuple-element.43, f32[1536]{0:T(1024)S(1)} %get-tuple-element.44, ...), kind=kLoop, calls=%fused_computation.228 | loop fusion | flops 48758272 | bytes 6483968 | tf_op jit(solution)/shard_map/reduce_sum | solution.py:16
  128.0 1.7 copy-done.7
  129.6 0.4 multiply_reduce_fusion.33
  130.1 7.5 %multiply_reduce_fusion = (f32[1536]{0:T(1024)S(1)}, f32[512]{0:T(512)S(1)}, f32[512,1536]{1,0:T(8,128)S(1)}) fusion(f32[4,128,1536]{2,1,0:T(8,128)} %copy-done.7, f32[512]{0:T(512)S(1)} %bitcast_rsqrt_fusion, f32[512]{0:T(512)S(1)} %get-tuple-element.117, f32[1536]{0:T(1024)S(1)} %copy-done.15, bf16[1536,1536]{1,0:T(8,128)(2,1)} %all-gather.5.cloned.1.call-done, ...), kind=kOutput, calls=%fused_computation.82 | convolution fusion | flops 2430072832 | bytes 12602368 | tf_op jit(solution)/shard_map/dot_general | solution.py:98
  137.7 3.0 fusion.49
  140.7 3.4 multiply_reduce_fusion.16
  144.2 13.4 %broadcast_multiply_fusion.1 = (f32[4,128,1536]{2,1,0:T(8,128)}, f32[4,128,1536]{2,1,0:T(8,128)}, f32[4,128,1536]{2,1,0:T(8,128)}, f32[4,128,1536]{2,1,0:T(8,128...) fusion(f32[4,128,1536]{2,1,0:T(8,128)S(1)} %bitcast.109, ...), kind=kLoop, calls=%fused_computation.127 | loop fusion | flops 10223616 | bytes 44120064 | tf_op jit(solution)/shard_map/transpose(jvp())/mul | solution.py:29
  157.5 18.1 %broadcast_multiply_fusion = (f32[4,128,1536]{2,1,0:T(8,128)}, f32[4,128,1536]{2,1,0:T(8,128)}, f32[4,128,1536]{2,1,0:T(8,128)}, f32[4,128,1536]{2,1,0:T(8,128)}...) fusion(f32[4,128,1536]{2,1,0:T(8,128)S(1)} %bitcast.110, ...), kind=kLoop, calls=%fused_computation.126 | loop fusion | flops 14155776 | bytes 59879424 | tf_op jit(solution)/shard_map/transpose(jvp())/mul | solution.py:29
  175.6 6.8 %convolution_convert_fusion.1 = bf16[1536,1536]{1,0:T(8,128)(2,1)} fusion(bf16[512,1536]{1,0:T(8,128)(2,1)} %get-tuple-element.85, bf16[512,1536]{1,0:T(8,128)(2,1)} %param.19, bf16[512]{0:T(512)(128)(2,1)S(1)} %get-tuple-element.120), kind=kOutput, calls=%fused_computation.35 | convolution fusion | flops 2419064832 | bytes 7865344 | tf_op jit(solution)/shard_map/dot_general | solution.py:116
  182.5 26.4 %pad_add_fusion = f32[4,158,1536]{2,1,0:T(8,128)S(1)} fusion(f32[4,128,1536]{2,1,0:T(8,128)} %get-tuple-element.93, f32[4,128,1536]{2,1,0:T(8,128)} %get-tuple-element.94, f32[4,128,1536]{2,1,0:T(8,128)} %get-tuple-element.95, f32[4,128,1536]{2,1,0:T(8,128)} %get-tuple-element.96, f32[4,128,1536]{2,1,0:T(8,128)} %get-tuple-element.97, ...), kind=kLoop, calls=%fused_computation.42 | loop fusion | flops 23298048 | bytes 82526208 | tf_op jit(solution)/shard_map/transpose(jvp())/add_any | solution.py:29
  208.9 7.5 %pad_add_fusion.1 = f32[4,128,1536]{2,1,0:T(8,128)S(1)} fusion(f32[4,128,1536]{2,1,0:T(8,128)} %get-tuple-element.87, f32[4,128,1536]{2,1,0:T(8,128)} %get-tuple-element.88, f32[4,128,1536]{2,1,0:T(8,128)} %get-tuple-element.89, f32[4,128,1536]{2,1,0:T(8,128)} %get-tuple-element.90, f32[4,128,1536]{2,1,0:T(8,128)} %get-tuple-element.91, ...), kind=kLoop, calls=%fused_computation.64 | loop fusion | flops 4718592 | bytes 25165824 | tf_op jit(solution)/shard_map/transpose(jvp())/add_any | solution.py:29
  216.4 6.1 %fusion.15 = (f32[512,1536]{1,0:T(8,128)S(1)}, f32[512,1536]{1,0:T(8,128)}) fusion(f32[4,128,1536]{2,1,0:T(8,128)S(1)} %pad_add_fusion.1, f32[512,3072]{1,0:T(8,128)} %copy-done.2, f32[512]{0:T(512)S(1)} %get-tuple-element.119), kind=kLoop, calls=%fused_computation.60 | loop fusion | flops 7077888 | bytes 15730688 | tf_op jit(solution)/shard_map/transpose(jvp())/mul | solution.py:35
  222.5 9.0 %convolution_convert_fusion = bf16[1536,3072]{1,0:T(8,128)(2,1)S(1)} fusion(f32[512,1536]{1,0:T(8,128)} %get-tuple-element.84, f32[512,1536]{1,0:T(8,128)S(1)} %get-tuple-element.83, bf16[512,1536]{1,0:T(8,128)(2,1)S(1)} %copy-done.11, f32[1536]{0:T(1024)S(1)} %copy-done.14, f32[512]{0:T(512)S(1)} %fusion.39, f32[512]{0:T(512)S(1)} %broadcast_multiply_fusion.32), kind=kOutput, calls=%fused_computation.4 | convolution fusion | flops 4843634688 | bytes 17311744 | tf_op jit(solution)/shard_map/dot_general | solution.py:113
  231.5 7.4 %pad_maximum_fusion = bf16[1536,4608]{1,0:T(8,128)(2,1)} fusion(bf16[1536,1536]{1,0:T(8,128)(2,1)S(1)} %bitcast.117, bf16[1536,3072]{1,0:T(8,128)(2,1)S(1)} %convolution_convert_fusion), kind=kLoop, calls=%fused_computation.3 | loop fusion | flops 28311552 | bytes 28311552 | tf_op jit(solution)/shard_map/concatenate | solution.py:120
  239.0 18.6 %copy.26 = bf16[4,4,32,512]{3,1,0,2:T(4,128)(2,1)} copy(bf16[4,4,32,512]{1,2,0,3:T(8,128)(2,1)} %bitcast.111) | data formatting | bytes 1048576 | tf_op jit(solution)/shard_map/tigj,tgc->ijc/dot_general | solution.py:61
  257.6 2.0 dot_general.35
  259.6 11.1 %fusion.10 = (f32[512]{0:T(512)S(1)}, f32[512,1536]{1,0:T(8,128)S(1)}) fusion(bf16[512,1536]{1,0:T(8,128)(2,1)} %fusion.29, f32[1536]{0:T(1024)S(1)} %copy-done.14, f32[512]{0:T(512)S(1)} %broadcast_multiply_fusion.32, bf16[1536,3072]{1,0:T(8,128)(2,1)} %all-gather.3.cloned.1.call-done, f32[512,1536]{1,0:T(8,128)} %get-tuple-element.84, ...), kind=kOutput, calls=%fused_computation.55 | convolution fusion | flops 4838915584 | bytes 20457472 | tf_op jit(solution)/shard_map/dot_general | solution.py:104
  270.7 2.4 fusion.9
  273.2 4.0 fusion.18
  277.2 7.6 %multiply_reduce_fusion.31 = (f32[1536]{0:T(1024)S(1)}, f32[1536]{0:T(1024)S(1)}, f32[1536]{0:T(1024)S(1)}, f32[1536]{0:T(1024)S(1)}, f32[1536]{0:T(1024)S(1)}, ...) fusion(f32[4,128,1536]{2,1,0:T(8,128)S(1)} %bitcast.114, ...), kind=kLoop, calls=%fused_computation.113 | loop fusion | flops 28283904 | bytes 6402048 | tf_op jit(solution)/shard_map/transpose(jvp())/reduce_sum | solution.py:29
  284.8 59.1 %reduce-scatter.2.cloned.1.call-done = bf16[48,4608]{1,0:T(8,128)(2,1)} async-done(((bf16[1536,4608]{1,0:T(8,128)(2,1)}), bf16[48,4608]{1,0:T(8,128)(2,1)}) %reduce-scatter.2.cloned.1.call-update) | async-done | bytes 442384 | tf_op jit(solution)/shard_map/reduce_scatter | solution.py:119
  343.9 19.3 %multiply_reduce_fusion.30 = (f32[1536]{0:T(1024)S(1)}, f32[1536]{0:T(1024)S(1)}, f32[1536]{0:T(1024)S(1)}, f32[1536]{0:T(1024)S(1)}, f32[1536]{0:T(1024)S(1)}, ...) fusion(f32[4,128,1536]{2,1,0:T(8,128)} %bitcast.113, ...), kind=kLoop, calls=%fused_computation.112 | loop fusion | flops 18855936 | bytes 6365184 | tf_op jit(solution)/shard_map/transpose(jvp())/reduce_sum | solution.py:29
  363.7 1.7 copy.28
  365.4 1.0 pad_add_fusion.7
  366.5 7.1 %fusion.26 = bf16[512,1536]{1,0:T(8,128)(2,1)} fusion(bf16[512,1536]{1,0:T(8,128)(2,1)} %get-tuple-element.85, bf16[1536,1536]{1,0:T(8,128)(2,1)} %all-gather.5.cloned.1.call-done, bf16[512,1536]{1,0:T(8,128)(2,1)} %fusion.29, f32[512]{0:T(512)S(1)} %get-tuple-element.119), kind=kOutput, calls=%fused_computation.122 | convolution fusion | flops 2419064832 | bytes 9439232 | tf_op jit(solution)/shard_map/dot_general | solution.py:95
  373.6 0.5 convolution_bitcast_fusion
  374.1 65.7 %all-reduce.65 = (f32[16,48]{1,0:T(8,128)}, f32[1536]{0:T(1024)}, f32[1536]{0:T(1024)}) all-reduce(f32[16,48]{1,0:T(8,128)S(1)} %convolution_bitcast_fusion, f32[1536]{0:T(1024)S(1)} %get-tuple-element.39, f32[1536]{0:T(1024)S(1)} %get-tuple-element.7), channel_id=1, replica_groups=mesh['dp'=4,'fsdp'=32] {'dp','fsdp'}, use_global_device_ids=true, to_apply=%region_10.11 | all-reduce | flops 3840 | bytes 30720 | tf_op jit(solution)/shard_map/psum | solution.py:127
  439.8 1.6 slice.331
  441.4 1.8 slice.330
  443.2 94.0 %all-reduce.71.cloned.1.call-done = f32[31,1536]{1,0:T(8,128)} async-done(((f32[31,1536]{1,0:T(8,128)}), f32[31,1536]{1,0:T(8,128)}) %all-reduce.71.cloned.1.call-update) | async-done | bytes 190480 | tf_op jit(solution)/shard_map/psum | solution.py:127
  537.2 1.6 copy.37
  (93 shorter events, 0.9 us)
Async XLA Ops:
  7.2 2.2 copy-start
  7.2 16.1 %copy-start.13 = (f32[31,1536]{1,0:T(8,128)S(1)}, f32[31,1536]{1,0:T(8,128)}, u32[]{:S(2)}) copy-start(f32[31,1536]{1,0:T(8,128)} %param.16) | copy-start | bytes 571396
  7.2 16.6 %copy-start.17 = (s32[4]{0:T(128)S(1)}, s32[4]{0:T(128)}, u32[]{:S(2)}) copy-start(s32[4]{0:T(128)} %param.12) | copy-start | bytes 52
  7.2 92.9 %all-gather.3.cloned.1.call-start = ((), (), s32[]{:S(2)}) async-start(), calls=%async_computation.2 | async-start | bytes 9732096 | tf_op jit(solution)/shard_map/all_gather | solution.py:89
  7.9 122.2 %all-gather.5.cloned.1.call-start = ((), (), s32[]{:S(2)}) async-start(), calls=%async_computation.3 | async-start | bytes 4866048 | tf_op jit(solution)/shard_map/all_gather | solution.py:90
  11.7 25.2 %all-to-all-start = ((bf16[128,16,128]{2,1,0:T(8,128)(2,1)}), bf16[128,16,128]{2,1,0:T(8,128)(2,1)S(1)}, u32[]{:S(2)}, u32[]{:S(2)}) async-start(bf16[128,16,128]{2,1,0:T(8,128)(2,1)} %broadcast_select_fusion), calls=%async_computation | async-start | bytes 1048576 | tf_op jit(solution)/shard_map/all_to_all | solution.py:79
  23.2 320.6 %reduce-scatter.2.cloned.1.call-start = ((), (), s32[]{:S(2)}) async-start(), calls=%async_computation.4 | async-start | bytes 14598144 | tf_op jit(solution)/shard_map/reduce_scatter | solution.py:119
  23.9 50.0 %copy-start.16 = (bf16[16,48]{1,0:T(8,128)(2,1)S(1)}, bf16[16,48]{1,0:T(8,128)(2,1)}, u32[]{:S(2)}) copy-start(bf16[16,48]{1,0:T(8,128)(2,1)} %param.13) | copy-start | bytes 4612
  95.1 5.1 copy-start.5
  95.1 5.0 copy-start.14
  108.8 2.7 copy-start.2
  111.4 16.5 %copy-start.3 = (f32[512,1536]{1,0:T(8,128)}, f32[512,1536]{1,0:T(8,128)S(1)}, u32[]{:S(2)}) copy-start(f32[512,1536]{1,0:T(8,128)S(1)} %multiply_multiply_fusion) | copy-start | bytes 9437188
  127.9 1.7 copy-start.7
  127.9 2.2 copy-start.15
  130.1 7.6 %copy-start.8 = (f32[4,128,1536]{2,1,0:T(8,128)S(1)}, f32[4,128,1536]{2,1,0:T(8,128)}, u32[]{:S(2)}) copy-start(f32[4,128,1536]{2,1,0:T(8,128)} %copy-done.7) | copy-start | bytes 9437188
  216.4 6.1 %copy-start.11 = (bf16[512,1536]{1,0:T(8,128)(2,1)S(1)}, bf16[512,1536]{1,0:T(8,128)(2,1)}, u32[]{:S(2)}) copy-start(bf16[512,1536]{1,0:T(8,128)(2,1)} %fusion.29) | copy-start | bytes 4718596
  216.4 15.1 %slice-start = ((s8[4718592]{0:T(1024)(128)(4,1)}), s8[4194304]{0:T(1024)(128)(4,1)S(1)}, s32[]{:S(2)}) async-start(s8[4718592]{0:T(1024)(128)(4,1)} %bitcast.116), calls=%async_computation.7 | async-start | bytes 8388608
  222.5 9.0 %copy-start.9 = (f32[512,1536]{1,0:T(8,128)}, f32[512,1536]{1,0:T(8,128)S(1)}, u32[]{:S(2)}) copy-start(f32[512,1536]{1,0:T(8,128)S(1)} %get-tuple-element.83) | copy-start | bytes 9437188
  222.5 9.0 %slice-start.1 = ((s8[4718592]{0:T(1024)(128)(4,1)}), s8[524288]{0:T(1024)(128)(4,1)S(1)}, s32[]{:S(2)}) async-start(s8[4718592]{0:T(1024)(128)(4,1)} %bitcast.116), calls=%async_computation.8 | async-start | bytes 1048576
  238.9 200.8 %all-reduce.69.cloned.1.call-start = ((), (), s32[]{:S(2)}) async-start(), calls=%async_computation.5 | async-start | bytes 884736 | tf_op jit(solution)/shard_map/psum | solution.py:125
  259.6 11.2 %copy-start.6 = (f32[512,1536]{1,0:T(8,128)S(1)}, f32[512,1536]{1,0:T(8,128)}, u32[]{:S(2)}) copy-start(f32[512,1536]{1,0:T(8,128)} %copy-done.5) | copy-start | bytes 9437188
  270.7 2.4 copy-start.12
  273.2 4.0 copy-start.4
  343.9 193.3 %all-reduce.71.cloned.1.call-start = ((), (), s32[]{:S(2)}) async-start(), calls=%async_computation.6 | async-start | bytes 393216 | tf_op jit(solution)/shard_map/psum | solution.py:127
  366.4 7.1 %copy-start.10 = (bf16[16,32,512]{2,0,1:T(8,128)(2,1)S(1)}, bf16[16,32,512]{2,0,1:T(8,128)(2,1)}, u32[]{:S(2)}) copy-start(bf16[16,32,512]{2,0,1:T(8,128)(2,1)} %dot_general.35) | copy-start | bytes 1572868
  366.4 172.4 %copy-start.1 = (bf16[128,16,128]{2,1,0:T(8,128)(2,1)S(1)}, bf16[128,16,128]{2,1,0:T(8,128)(2,1)}, u32[]{:S(2)}) copy-start(bf16[128,16,128]{2,1,0:T(8,128)(2,1)} %param.10) | copy-start | bytes 1572868
Sparse Core Ops, SparseCore 0:
  10.3 63.9 all-gather.2
  76.6 46.4 all-gather.4
  239.0 104.7 reduce-scatter.1
  346.2 40.5 all-reduce.68
  391.9 145.2 all-reduce.70
where the time goes:
time: 556 us; the launch traced here: 546 us
  waiting for transfers between devices  168 us (30%)
  other arithmetic  145 us (26%)
  local copies, waits for them, and re-layouts  71.7 us (13%)
  matrix products  69.5 us (12%)
  blocking collectives  65.7 us (12%)
  between operations  14.8 us (3%)
  starting transfers between devices  11.7 us (2%)
    psum x1, waiting for transfers between devices, body(): lax.psum((stem_grad, first_grad, conv_grad, second_grad), ('dp', 'fsdp'))  94 us
    psum x1, blocking collectives, body(): lax.psum((stem_grad, first_grad, conv_grad, second_grad), ('dp', 'fsdp'))  65.7 us
    reduce_scatter x1, waiting for transfers between devices, body(): lax.psum_scatter(jnp.concatenate([gate_term, out_term], axis=1).astype(jn...  59.1 us
    another operation x1, local copies, waits for them, and re-layouts, stem_sum(): split_in = frames.reshape(rows, PATCH, groups, PATCH)  36.9 us
    add_any x3, other arithmetic, depthwise(): summed = summed + padded[:, offset:offset + length, :] * conv_kernel[offset]  34.9 us
    mul x2, other arithmetic, depthwise(): summed = summed + padded[:, offset:offset + length, :] * conv_kernel[offset]  31.5 us
    reduce_sum x3, other arithmetic, depthwise(): summed = summed + padded[:, offset:offset + length, :] * conv_kernel[offset]  30.3 us
    dot_general x2, local copies, waits for them, and re-layouts, stem_weight_grad(): jnp.einsum('tigj,tgc->ijc', split_in, split_grad, preferred_element_type=...  20.6 us
  transfers between devices with their start and end apart: 6, of which 3 were waited for; matrix products, arithmetic and copies ran while one was open for 32% of the time, Pallas kernels for 0%

commit v1 on v0

v1 whole, which is shorter than its diff:
```python
import functools

import jax
import jax.numpy as jnp
import numpy as np
from jax import lax
from jax.experimental import pallas as pl
from jax.experimental.pallas import tpu as pltpu
from jax.sharding import Mesh
from jax.sharding import PartitionSpec as P

PATCH = 4
UTT = 128
TOK = 512
NU = TOK // UTT
D = 1536
MEL = 128
CH = 48
TAPS = 31
HALF = TAPS // 2
EPS = 1e-05
ROWS = 48
CB = 256
NB = D // CB
ALL = ("x", "y", "z", "c")
F32 = jnp.float32
BF16 = jnp.bfloat16
MIB = 1024 * 1024
COST = 1

CYC = 144
BINS = CYC // 2 + 1
IM = 80
SPEC = 160


def hi_lo(values):
    high = values.astype(np.float32).astype(jnp.bfloat16)
    low = (values - high.astype(np.float64)).astype(np.float32).astype(jnp.bfloat16)
    return high, low


def side_by_side(values, three=False):
    high, low = hi_lo(values)
    parts = [high, low] + ([high] if three else [])
    return np.concatenate(parts, axis=1)


def transforms():
    angle = 2 * np.pi / CYC
    bins = np.arange(BINS)[:, None]
    places = np.arange(UTT)[None, :]
    offsets = np.arange(TAPS)[None, :] - HALF
    forward = np.zeros((SPEC, UTT))
    forward[:BINS] = np.cos(angle * bins * places)
    forward[IM : IM + BINS] = -np.sin(angle * bins * places)
    kernel = np.zeros((SPEC, 32))
    kernel[:BINS, :TAPS] = np.cos(angle * bins * offsets)
    kernel[IM : IM + BINS, :TAPS] = np.sin(angle * bins * offsets)
    weight = np.full((BINS, 1), 2.0 / CYC)
    weight[0] = weight[-1] = 1.0 / CYC
    back = np.zeros((UTT, SPEC))
    back[:, :BINS] = (weight * np.cos(angle * bins * places)).T
    back[:, IM : IM + BINS] = -(weight * np.sin(angle * bins * places)).T
    return {
        "fwd": side_by_side(forward),
        "inv": side_by_side(back),
        "fwd_t": side_by_side(forward.T),
        "inv_t": side_by_side(back.T),
        "ker": side_by_side(kernel, True),
        "ker_t": side_by_side(kernel.T, True),
    }


def twice(values):
    narrow = values.astype(BF16)
    return jnp.concatenate([narrow, narrow], axis=0)


def thrice(values):
    high = values.astype(BF16)
    low = (values - high.astype(F32)).astype(BF16)
    return jnp.concatenate([high, high, low], axis=0)


def mm(left, right):
    return jnp.dot(left, right, preferred_element_type=F32)


def mm_nt(left, right):
    return lax.dot_general(left, right, (((1,), (1,)), ((), ())), preferred_element_type=F32)


def keep(limit, shape):
    return lax.broadcasted_iota(jnp.int32, shape, 0) < limit


def row_mean(values):
    return jnp.sum(values, axis=-1, keepdims=True) * (1.0 / D)


def normalise(values):
    centred = values - row_mean(values)
    scale = lax.rsqrt(row_mean(centred * centred) + EPS)
    return centred * scale, scale


def normalise_back(grad, unit, scale):
    return scale * (grad - row_mean(grad) - unit * row_mean(grad * unit))


def stem_masks(rows, cols):
    row = lax.broadcasted_iota(jnp.int32, (rows, cols), 0)
    col = lax.broadcasted_iota(jnp.int32, (rows, cols), 1)
    group = (row % MEL) // PATCH
    first = group * CH
    return (col >= first) & (col < first + CH)


def tap_select(rows):
    row = lax.broadcasted_iota(jnp.int32, (rows, 16), 0)
    tap = lax.broadcasted_iota(jnp.int32, (rows, 16), 1)
    return (tap == PATCH * (row // MEL) + row % PATCH).astype(F32).astype(BF16)


def channel_select():
    row = lax.broadcasted_iota(jnp.int32, (CH, D), 0)
    col = lax.broadcasted_iota(jnp.int32, (CH, D), 1)
    return (col % CH == row).astype(F32).astype(BF16)


def stem_kernel(
    unused, frames_of, arrived, stem_weight, first_gain, conv_kernel, cotangent, ker,
    stem_total, embedded, normed, normed_t, frames_t, spectrum, mix_grad, wide, big,
):
    wide[...] = arrived[...].astype(F32)
    taps = mm(tap_select(TOK), stem_weight[...]).astype(BF16)
    spread = mm(taps, channel_select())
    big[...] = jnp.where(stem_masks(TOK, D), spread, 0.0).astype(BF16)
    padded = jnp.concatenate([conv_kernel[...], jnp.zeros((1, D), F32)], axis=0)
    spectrum[...] = mm(ker[...], thrice(padded))

    def one(u, carry):
        base = pl.multiple_of(u * UTT, UTT)
        rows = pl.ds(base, UTT)
        parts = [wide[pl.ds(base * PATCH + i, UTT, stride=PATCH), :].astype(BF16) for i in range(PATCH)]
        frames = jnp.concatenate(parts, axis=1)
        total = mm(frames, big[...])
        stem_total[rows, :] = total
        valid = keep(frames_of[u] // PATCH, (UTT, D))
        kept = jnp.where(valid, total * jax.nn.sigmoid(total), 0.0).astype(BF16)
        embedded[rows, :] = kept
        unit, scale = normalise(kept.astype(F32))
        narrow = (unit * first_gain[...]).astype(BF16)
        normed[rows, :] = narrow
        normed_t[:, rows] = narrow.T
        frames_t[:, rows] = frames.T
        mix_grad[rows, :] = jnp.where(valid, cotangent[rows, :].astype(F32), 0.0).astype(BF16)
        return carry

    lax.fori_loop(0, NU, one, 0)


def assemble(offsets, pieces, held, sems):
    copies = []
    for p, piece in enumerate(pieces):
        for j, (second, first) in enumerate(PIECES[p % len(PIECES)]):
            block = p // len(PIECES) * 16 + second * 4 + first
            start = pl.multiple_of(offsets[block], 16)
            copies.append(pltpu.make_async_copy(piece.at[j], held.at[pl.ds(start, ROWS), :], sems.at[block]))
    for copy in copies:
        copy.start()
    for copy in copies:
        copy.wait()


def gate_kernel(offsets, frames_of, *refs):
    pieces, refs = refs[:NP], refs[NP + 2 :]
    normed, spectrum, fwd, inv, value, gate, filtered, held, sems = refs
    n = pl.program_id(0)

    @pl.when(n == 0)
    def _():
        assemble(offsets, pieces, held, sems)

    start = pl.multiple_of(n * CB, CB)
    value[...] = mm(normed[...], held[:, pl.ds(start, CB)])
    gate[...] = mm(normed[...], held[:, pl.ds(pl.multiple_of(D + start, CB), CB)])
    re, im = spectrum[:IM, :], spectrum[IM:, :]
    for u in range(NU):
        rows = slice(u * UTT, (u + 1) * UTT)
        gated = value[rows, :] * jax.nn.sigmoid(gate[rows, :])
        gated = jnp.where(keep(frames_of[u] // PATCH, (UTT, CB)), gated, 0.0)
        seen = mm(fwd[...], twice(gated))
        a, b = seen[:IM], seen[IM:]
        moved = jnp.concatenate([a * re - b * im, a * im + b * re], axis=0)
        filtered[rows, :] = mm(inv[...], twice(moved))


def block_start(slots, i, flip):
    core = slots[32] if flip == 0 else 1 - slots[32]
    return pl.multiple_of((2 * i + core) * ROWS, 16)


def out_kernel(slots, unused, unused_too, filtered, mix_grad, second_gain, mine, other, swished, turned, term):
    def ahead(u, carry):
        rows = pl.ds(pl.multiple_of(u * UTT, UTT), UTT)
        unit, unused = normalise(filtered[rows, :])
        z = unit * second_gain[...]
        narrow = (z * jax.nn.sigmoid(z)).astype(BF16)
        swished[rows, :] = narrow
        turned[:, rows] = narrow.T
        return carry

    lax.fori_loop(0, NU, ahead, 0)

    def product(n, carry):
        cols = pl.ds(pl.multiple_of(n * CB, CB), CB)
        term[...] = mm(turned[...], mix_grad[:, cols]).astype(BF16)
        for i in range(16):
            mine[slots[i], :, cols] = term[pl.ds(block_start(slots, i, 0), ROWS), :]
            other[slots[16 + i], :, cols] = term[pl.ds(block_start(slots, i, 1), ROWS), :]
        return carry

    lax.fori_loop(0, NB, product, 0)


def mid_kernel(offsets, *refs):
    pieces, refs = refs[:NP], refs[NP:]
    filtered, mix_grad, second_gain, filter_grad, second_grad, held, sems, back = refs[3:]
    assemble(offsets, pieces, held, sems)
    second_grad[...] = jnp.zeros((1, D), F32)

    def product(n, carry):
        cols = pl.ds(pl.multiple_of(n * CB, CB), CB)
        back[:, cols] = mm_nt(mix_grad[...], held[cols, :])
        return carry

    lax.fori_loop(0, NB, product, 0)

    def behind(u, carry):
        rows = pl.ds(pl.multiple_of(u * UTT, UTT), UTT)
        unit, scale = normalise(filtered[rows, :])
        z = unit * second_gain[...]
        sig = jax.nn.sigmoid(z)
        dz = back[rows, :] * (sig * (1.0 + z * (1.0 - sig)))
        second_grad[...] += jnp.sum(dz * unit, axis=0, keepdims=True)
        filter_grad[rows, :] = normalise_back(dz * second_gain[...], unit, scale)
        return carry

    lax.fori_loop(0, NU, behind, 0)


def conv_back_kernel(
    slots, frames_of, unused_1, unused_2, unused_3, value, gate, filter_grad, normed_t, spectrum, fwd, inv_t, fwd_t, ker_t,
    value_grad, gate_grad, mine, other, conv_grad, term,
):
    re, im = spectrum[:IM, :], spectrum[IM:, :]
    sum_re = jnp.zeros((IM, CB), F32)
    sum_im = jnp.zeros((IM, CB), F32)
    for u in range(NU):
        rows = slice(u * UTT, (u + 1) * UTT)
        valid = keep(frames_of[u] // PATCH, (UTT, CB))
        v = value[rows, :]
        sig = jax.nn.sigmoid(gate[rows, :])
        gated = jnp.where(valid, v * sig, 0.0)
        seen = mm(fwd[...], twice(gated))
        a, b = seen[:IM], seen[IM:]
        grad = mm(inv_t[...], twice(filter_grad[rows, :]))
        da, db = grad[:IM], grad[IM:]
        sum_re = sum_re + a * da + b * db
        sum_im = sum_im + a * db - b * da
        spread = jnp.concatenate([re * da + im * db, re * db - im * da], axis=0)
        gated_grad = jnp.where(valid, mm(fwd_t[...], twice(spread)), 0.0)
        part = gated_grad * sig
        value_grad[rows, :] = part.astype(BF16)
        gate_grad[rows, :] = (part * v * (1.0 - sig)).astype(BF16)
    conv_grad[...] = mm(ker_t[...], thrice(jnp.concatenate([sum_re, sum_im], axis=0)))
    for h, grad_ref in enumerate((value_grad, gate_grad)):
        term[...] = mm(normed_t[...], grad_ref[...]).astype(BF16)
        for i in range(16):
            cols = slice(h * CB, (h + 1) * CB)
            mine[slots[i], :, cols] = term[pl.ds(block_start(slots, i, 0), ROWS), :]
            other[slots[16 + i], :, cols] = term[pl.ds(block_start(slots, i, 1), ROWS), :]


def stem_back_kernel(offsets, frames_of, *refs):
    pieces, refs = refs[:NP], refs[NP:]
    grads, refs = refs[:4], refs[4:]
    (unused_1, unused_2, unused_3, embedded, stem_total, mix_grad, first_gain, frames_t,
     first_grad, stem_grad, held, sems, back, pre_grad) = refs
    assemble(offsets, pieces, held, sems)
    first_grad[...] = jnp.zeros((1, D), F32)

    def product(n, carry):
        cols = pl.ds(pl.multiple_of(n * CB, CB), CB)
        total = jnp.zeros((TOK, CB), F32)
        begin = 0
        for grad in grads:
            total = total + mm_nt(grad[...], held[cols, begin : begin + grad.shape[1]])
            begin += grad.shape[1]
        back[:, cols] = total
        return carry

    lax.fori_loop(0, NB, product, 0)

    def behind(u, carry):
        rows = pl.ds(pl.multiple_of(u * UTT, UTT), UTT)
        unit, scale = normalise(embedded[rows, :].astype(F32))
        grad = back[rows, :]
        first_grad[...] += jnp.sum(grad * unit, axis=0, keepdims=True)
        grad = normalise_back(grad * first_gain[...], unit, scale) + mix_grad[rows, :].astype(F32)
        total = stem_total[rows, :]
        sig = jax.nn.sigmoid(total)
        grad = grad * (sig * (1.0 + total * (1.0 - sig)))
        valid = keep(frames_of[u] // PATCH, (UTT, D))
        pre_grad[rows, :] = jnp.where(valid, grad, 0.0).astype(BF16)
        return carry

    lax.fori_loop(0, NU, behind, 0)
    outer = mm(frames_t[...], pre_grad[...])
    outer = jnp.where(stem_masks(TOK, D), outer, 0.0)
    pick = tap_select(TOK).T
    folded = mm(jnp.concatenate([pick, pick], axis=1), split_rows(outer))
    channel = channel_select()
    high = folded.astype(BF16)
    low = (folded - high.astype(F32)).astype(BF16)
    stem_grad[...] = mm_nt(high, channel) + mm_nt(low, channel)


def split_rows(values):
    high = values.astype(BF16)
    low = (values - high.astype(F32)).astype(BF16)
    return jnp.concatenate([high, low], axis=0)


def mixed_kernel(offsets, frames_of, *refs):
    pieces, refs = refs[:NP], refs[NP:]
    unused, swished, embedded, output, held, sems = refs
    assemble(offsets, pieces, held, sems)

    def product(n, carry):
        cols = pl.ds(pl.multiple_of(n * CB, CB), CB)
        mixed = mm(swished[...], held[:, cols])
        for u in range(NU):
            rows = slice(u * UTT, (u + 1) * UTT)
            total = embedded[rows, cols].astype(F32) + mixed[rows]
            valid = keep(frames_of[u] // PATCH, (UTT, CB))
            output[rows, cols] = jnp.where(valid, total, 0.0).astype(BF16)
        return carry

    lax.fori_loop(0, NB, product, 0)


def chip_sum_kernel(mine_1, other_1, mine_2, other_2, *groups):
    wide = mine_1.shape[-1]
    for r, group in enumerate(groups):
        group[0, :, :wide] = (mine_1[r, 0].astype(F32) + other_1[r, 0].astype(F32)).astype(BF16)
        group[0, :, wide:] = (mine_2[r, 0].astype(F32) + other_2[r, 0].astype(F32)).astype(BF16)


SMEM = pl.BlockSpec(memory_space=pltpu.SMEM)
ANY = pl.BlockSpec(memory_space=pl.ANY)
VMEM = pl.BlockSpec(memory_space=pltpu.VMEM)


def shaped(shape, dtype):
    return jax.ShapeDtypeStruct(shape, dtype)


def call(kernel, name, operands, in_specs, outs, out_specs, scratch, flops, nbytes, vmem, grid=None):
    more = {} if grid is None else {"grid": grid}
    return pl.pallas_call(
        kernel,
        name=name,
        out_shape=outs,
        in_specs=in_specs,
        out_specs=out_specs,
        scratch_shapes=scratch,
        compiler_params=pltpu.CompilerParams(vmem_limit_bytes=vmem * MIB),
        cost_estimate=pl.CostEstimate(flops=flops // COST, bytes_accessed=nbytes // COST, transcendentals=0),
        **more,
    )(*operands)


def stem(before, arrived, frames_of, stem_weight, first_gain, conv_kernel, cotangent, tables):
    outs = [
        shaped((TOK, D), F32), shaped((TOK, D), BF16), shaped((TOK, D), BF16), shaped((D, TOK), BF16),
        shaped((TOK, TOK), BF16), shaped((SPEC, D), F32), shaped((TOK, D), BF16),
    ]
    return call(
        stem_kernel, "stem",
        (before, frames_of, arrived, stem_weight, first_gain, conv_kernel, cotangent, tables["ker"]),
        [ANY, SMEM] + [VMEM] * 6, outs, [VMEM] * 7,
        [pltpu.VMEM((TOK * PATCH, MEL), F32), pltpu.VMEM((TOK, D), BF16)],
        2 * TOK * TOK * D, 14 * MIB, 56,
    )


def gate_forward(offsets, frames_of, pieces, before, normed, spectrum, tables):
    whole = lambda n: (0, 0)
    block = lambda n: (0, n)
    return call(
        gate_kernel, "gate",
        (offsets, frames_of, *pieces, *before, normed, spectrum, tables["fwd"], tables["inv"]),
        [SMEM, SMEM] + [ANY] * (NP + 2)
        + [pl.BlockSpec((TOK, D), whole), pl.BlockSpec((SPEC, CB), block),
           pl.BlockSpec(tables["fwd"].shape, whole), pl.BlockSpec(tables["inv"].shape, whole)],
        [shaped((TOK, D), F32)] * 3, [pl.BlockSpec((TOK, CB), block)] * 3,
        [pltpu.VMEM((D, 2 * D), BF16), pltpu.SemaphoreType.DMA((32,))],
        2 * TOK * D * 2 * D, 22 * MIB, 56, grid=(NB,),
    )


def out_grad(slots, before, filtered, mix_grad, second_gain):
    half = shaped((16, ROWS, D), BF16)
    return call(
        out_kernel, "out_grad", (slots, *before, filtered, mix_grad, second_gain),
        [SMEM, ANY, ANY] + [VMEM] * 3, [half, half, shaped((TOK, D), BF16)], [VMEM] * 3,
        [pltpu.VMEM((D, TOK), BF16), pltpu.VMEM((D, CB), BF16)],
        2 * TOK * D * D, 11 * MIB, 56,
    )


def middle(offsets, pieces, before, filtered, mix_grad, second_gain):
    return call(
        mid_kernel, "middle", (offsets, *pieces, *before, filtered, mix_grad, second_gain),
        [SMEM] + [ANY] * (NP + 3) + [VMEM] * 3, [shaped((TOK, D), F32), shaped((1, D), F32)], [VMEM] * 2,
        [pltpu.VMEM((D, D), BF16), pltpu.SemaphoreType.DMA((32,)), pltpu.VMEM((TOK, D), F32)],
        2 * TOK * D * D, 13 * MIB, 56,
    )


def conv_back(slots, frames_of, before, value, gate, filter_grad, normed_t, spectrum, tables, begin, count):
    whole = lambda n: (0, 0)
    block = lambda n: (0, n + begin)
    own = lambda n: (0, n)
    width = count * CB
    names = ("fwd", "inv_t", "fwd_t", "ker_t")
    half = shaped((16, ROWS, 2 * width), BF16)
    half_spec = pl.BlockSpec((16, ROWS, 2 * CB), lambda n: (0, 0, n))
    outs = [shaped((TOK, width), BF16), shaped((TOK, width), BF16), half, half, shaped((32, width), F32)]
    return call(
        conv_back_kernel, "conv_back",
        (slots, frames_of, *before, value, gate, filter_grad, normed_t, spectrum, *[tables[k] for k in names]),
        [SMEM, SMEM, ANY, ANY, ANY] + [pl.BlockSpec((TOK, CB), block)] * 3
        + [pl.BlockSpec((D, TOK), whole), pl.BlockSpec((SPEC, CB), block)]
        + [pl.BlockSpec(tables[k].shape, whole) for k in names],
        outs,
        [pl.BlockSpec((TOK, CB), own)] * 2 + [half_spec, half_spec, pl.BlockSpec((32, CB), own)],
        [pltpu.VMEM((D, CB), BF16)], 2 * TOK * D * width * 2, 22 * MIB * count // NB, 56, grid=(count,),
    )


def stem_back(offsets, frames_of, pieces, grads, before, embedded, stem_total, mix_grad, first_gain, frames_t):
    return call(
        stem_back_kernel, "stem_back",
        (offsets, frames_of, *pieces, *grads, *before, embedded, stem_total, mix_grad, first_gain, frames_t),
        [SMEM, SMEM] + [ANY] * NP + [VMEM] * 4 + [ANY] * 3 + [VMEM] * 5,
        [shaped((1, D), F32), shaped((16, CH), F32)], [VMEM] * 2,
        [pltpu.VMEM((D, 2 * D), BF16), pltpu.SemaphoreType.DMA((32,)), pltpu.VMEM((TOK, D), F32), pltpu.VMEM((TOK, D), BF16)],
        2 * TOK * D * 2 * D, 20 * MIB, 56,
    )


def mixed_out(offsets, frames_of, pieces, before, swished, embedded):
    return call(
        mixed_kernel, "mixed",
        (offsets, frames_of, *pieces, before, swished, embedded),
        [SMEM, SMEM] + [ANY] * (NP + 1) + [VMEM] * 2,
        shaped((TOK, D), BF16), VMEM,
        [pltpu.VMEM((D, D), BF16), pltpu.SemaphoreType.DMA((32,))],
        2 * TOK * D * D, 10 * MIB, 56,
    )


def chip_sums(parts):
    operands = [value.reshape(4, 4, *value.shape[1:]) for part in parts for value in part]
    width = 2 * D
    spec = lambda value: pl.BlockSpec((4, 1, *value.shape[2:]), lambda m: (0, m, 0, 0))
    return call(
        chip_sum_kernel, "chip_sum", operands, [spec(value) for value in operands],
        [shaped((4, ROWS, width), BF16)] * 4, [pl.BlockSpec((1, ROWS, width), lambda m: (m, 0, 0))] * 4,
        [], 16 * ROWS * width, 14 * MIB, 48, grid=(4,),
    )


def place(x, y, z, c):
    return ((x % 4 * 4 + y % 4) * 4 + z % 4) * 2 + c


def pairs(step):
    found = []
    for x in range(4):
        for y in range(4):
            for z in range(4):
                for c in range(2):
                    found.append((place(x, y, z, c), step(x, y, z, c)))
    return found


def along_first(r):
    return pairs(lambda x, y, z, c: place(x, y ^ (r * c), z ^ (r * (1 - c)), c))


def along_second(r):
    return pairs(lambda x, y, z, c: place(x, y ^ (r * (1 - c)), z ^ (r * c), c))


def along_x(r):
    return pairs(lambda x, y, z, c: place(x ^ r, y, z, c))


def other_core():
    return pairs(lambda x, y, z, c: place(x, y, z, 1 - c))


def send(values, where):
    return lax.ppermute(values, ALL, where)


def gather_offsets(y, z, c):
    m, j = np.divmod(np.arange(16, dtype=np.int32), 4)

    def of(core):
        row_y = y ^ jnp.where(core == 0, m, j)
        row_z = z ^ jnp.where(core == 0, j, m)
        return ((row_y * 4 + row_z) * 2 + core) * ROWS

    return jnp.concatenate([of(c), of(1 - c)]).astype(jnp.int32)


def scatter_slots(y, z, c):
    block = np.arange(16, dtype=np.int32)
    far_y, far_z = (block // 4) ^ y, (block % 4) ^ z

    def of(core):
        return jnp.where(core == 0, far_z * 4 + far_y, far_y * 4 + far_z)

    return jnp.concatenate([of(c), of(1 - c), c[None]]).astype(jnp.int32)


def zero_of(values):
    return values[(0,) * values.ndim] * 0


def gather_near(shards):
    joined = jnp.concatenate(shards, axis=1)
    near = [joined] + [send(joined, along_first(r)) for r in (1, 2, 3)]
    wide = shards[0].shape[1]
    return jnp.stack([block[:, :wide] for block in near]), jnp.stack([block[:, wide:] for block in near])


def gather_far(near):
    halves = near[:2], near[2:]
    first = [send(half, along_second(r)) for half, r in zip(halves, (1, 3))]
    second = [
        send(jnp.stack([half, got]), along_second(r)) for half, got, r in zip(halves, first, (3, 1))
    ]
    return first, second


def gather_pieces(near, first, second, after):
    own = [near, first[0], first[1], second[0].reshape(4, *near.shape[1:]), second[1].reshape(4, *near.shape[1:])]
    return own + [send(piece + after, other_core()) for piece in own]


PIECES = (
    ((0, 0), (0, 1), (0, 2), (0, 3)),
    ((1, 0), (1, 1)),
    ((3, 2), (3, 3)),
    ((3, 0), (3, 1), (2, 0), (2, 1)),
    ((1, 2), (1, 3), (2, 2), (2, 3)),
)
NP = 2 * len(PIECES)


def total_of(parts):
    summed = parts[0].astype(F32)
    for part in parts[1:]:
        summed = summed + part.astype(F32)
    return summed


def chip_sum(mine, other):
    other = send(other, other_core())
    return [total_of([mine[4 * j : 4 * j + 4], other[4 * j : 4 * j + 4]]).astype(BF16) for j in range(4)]


def scatter_first(groups):
    return [groups[0]] + [send(groups[r], along_first(r)) for r in (1, 2, 3)]


def scatter_rest(near):
    close = total_of([near[0]] + [send(near[r], along_second(r)) for r in (1, 2, 3)]).astype(BF16)
    wide = close.shape[1] // 2
    halves = []
    for half, order in ((close[:, :wide], (1, 3)), (close[:, wide:], (3, 1))):
        half = total_of([half, send(half, along_x(order[0]))]).astype(BF16)
        halves.append(total_of([half, send(half, along_x(order[1]))]))
    return jnp.concatenate(halves, axis=1)


def half_of_chip(values, c):
    return jnp.where(c == 0, values[0], values[1]) + send(jnp.where(c == 0, values[1], values[0]), other_core())


def finish_small(values, rows, c):
    values = total_of([values] + [send(values, along_first(r)) for r in (1, 2, 3)])
    other = send(values, other_core())
    mine, late = values[:rows], values[rows:] + other[rows:]
    other = other[:rows]
    return jnp.concatenate([jnp.where(c == 0, mine, other), jnp.where(c == 0, other, mine)]), late


def body(
    tables, log_mel, bucket_list, utterance_frames, stem_weight, first_gain, gate_proj, conv_kernel, second_gain,
    out_proj, cotangent,
):
    y, z, c = lax.axis_index("y"), lax.axis_index("z"), lax.axis_index("c")
    offsets = gather_offsets(y, z, c)
    slots = scatter_slots(y, z, c)
    tables = {name: jnp.asarray(value) for name, value in tables.items()}
    first_gain, second_gain = first_gain[None], second_gain[None]

    gate_near, out_near = gather_near((gate_proj, out_proj))
    outgoing = jnp.take(log_mel, bucket_list[0], axis=0) + zero_of(gate_near)
    arrived = lax.all_to_all(outgoing, ALL, split_axis=0, concat_axis=0, tiled=True)
    gate_far = gather_far(gate_near)
    stem_total, embedded, normed, normed_t, frames_t, spectrum, mix_grad = stem(
        gate_far[0][0], arrived.reshape(TOK * PATCH, MEL), utterance_frames, stem_weight, first_gain, conv_kernel, cotangent, tables
    )
    gate_pieces = gather_pieces(gate_near, *gate_far, zero_of(normed))
    out_near = out_near + sum(zero_of(piece) for piece in gate_far[1])
    out_far = gather_far(out_near)
    out_pieces = gather_pieces(out_near, *out_far, jnp.zeros((), BF16))
    value, gate, filtered = gate_forward(
        offsets, utterance_frames, gate_pieces, out_far[0], normed, spectrum, tables
    )
    out_mine, out_other, swished = out_grad(slots, out_far[1], filtered, mix_grad, second_gain)
    out_groups = chip_sum(out_mine, out_other)
    filter_grad, second_grad = middle(offsets, out_pieces, out_groups[1:], filtered, mix_grad, second_gain)
    out_groups = scatter_first(out_groups)
    grads, nears, convs = [], [], []
    for begin, count in ((0, 4), (4, 2)):
        value_grad, gate_grad, mine, other, conv_grad = conv_back(
            slots, utterance_frames, out_groups[1:], value, gate, filter_grad, normed_t, spectrum, tables, begin, count
        )
        grads.append((value_grad, gate_grad))
        nears.append((mine, send(other, other_core())))
        convs.append(conv_grad[:TAPS])
    gate_groups = chip_sums(nears)
    first_grad, stem_grad = stem_back(
        offsets, utterance_frames, gate_pieces, [pair[k] for k in range(2) for pair in grads], gate_groups[1:], embedded,
        stem_total, mix_grad, first_gain, frames_t,
    )
    output = mixed_out(offsets, utterance_frames, out_pieces, first_grad, swished, embedded)
    early = jnp.concatenate([jnp.concatenate(convs, axis=1), second_grad], axis=0)
    early = half_of_chip(early.reshape(2, 16, D), c)
    follow = zero_of(output).astype(F32) + zero_of(first_grad)
    terms = [scatter_first(gate_groups), out_groups]
    near = jnp.concatenate([(total_of(term) + follow).astype(BF16) for term in terms], axis=-1)
    late = jnp.concatenate([first_grad, jnp.pad(stem_grad.reshape(1, -1), ((0, 0), (0, D - 16 * CH)))], axis=0)
    small = jnp.concatenate([early, late, jnp.zeros((6, D), F32)], axis=0)
    small = jnp.concatenate([small[:8], small[8:16], small[16:]], axis=1).astype(BF16)
    near = jnp.concatenate([near, jnp.broadcast_to(small[None], (4, *small.shape))], axis=1)
    sums = scatter_rest(near)
    small = sums[ROWS:]
    early, late = finish_small(
        jnp.concatenate([small[:, :D], small[:, D : 2 * D], small[:2, 2 * D :]]), 16, c
    )
    sums = sums[:ROWS]
    blocks = [sums[:, i * CB : (i + 1) * CB] for i in range(2 * NB)]
    gate_sums = jnp.concatenate(blocks[::2] + blocks[1::2], axis=1)
    return (
        output, gate_sums, sums[:, 2 * D :], late[1, : 16 * CH].reshape(16, CH), late[0],
        early[:TAPS], early[TAPS],
    )


def solution(mesh):
    grid = Mesh(mesh.devices.reshape(4, 4, 4, 2), ALL)
    rows = ("y", "z", "c")
    return jax.shard_map(
        functools.partial(body, transforms()),
        mesh=grid,
        in_specs=(
            P(ALL, None, None), P(ALL, None), P(ALL), P(), P(), P(rows, None), P(), P(), P(rows, None), P(ALL, None),
        ),
        out_specs=(P(ALL, None), P(rows, None), P(rows, None), P(), P(), P(), P()),
        check_vma=False,
    )
```

time: 556 us -> 262 us (0.47); the launches traced: 546 us -> 261 us
  other arithmetic: 145 us -> 19.6 us
  waiting for transfers between devices: 168 us -> 47.8 us
  Pallas kernels: 0 us -> 103 us
  matrix products: 69.5 us -> 0 us
  blocking collectives: 65.7 us -> 0 us
  starting transfers between devices: 11.7 us -> 60.4 us
  local copies, waits for them, and re-layouts: 71.7 us -> 24.1 us
  between operations: 14.8 us -> 5.65 us
    pallas_call x0 -> x9, Pallas kernels: none -> 103 us  [call(): pl.pallas_call(kernel, name=name, out_shape=outs, in_specs=in_specs, out_...]
    psum x2 -> x0, waiting for transfers between devices: 94 us -> none  [the longest x1 94 us: body(): lax.psum((stem_grad, first_grad, conv_grad, second_grad), ('dp', 'fsdp'))]
    dot_general x8 -> x0, matrix products: 69.5 us -> none  [the longest x1 18.8 us: stem_sum(): jnp.einsum('tigj,ijc->tgc', split_in, kernel, preferred_element_type=jnp....]
    psum x1 -> x0, blocking collectives: 65.7 us -> none  [body(): lax.psum((stem_grad, first_grad, conv_grad, second_grad), ('dp', 'fsdp'))]
    reduce_scatter x1 -> x0, waiting for transfers between devices: 59.1 us -> none  [body(): lax.psum_scatter(jnp.concatenate([gate_term, out_term], axis=1).astype(jn...]
    reduce_sum x8 -> x0, other arithmetic: 55.6 us -> none  [the longest x3 30.3 us: depthwise(): summed = summed + padded[:, offset:offset + length, :] * conv_kernel[offset]]
    ppermute x0 -> x42, starting transfers between devices: none -> 48.6 us  [send(): return lax.ppermute(values, ALL, where)]
    ppermute x0 -> x42, waiting for transfers between devices: none -> 47.8 us  [send(): return lax.ppermute(values, ALL, where)]
  transfers between devices with their start and end apart: 6 -> 43, of which waited for: 3 -> 18; matrix products, arithmetic and copies ran while one was open for 32% -> 10% of each run, Pallas kernels for 0% -> 29%
where the time goes in v1:
time: 262 us; the launch traced here: 261 us
  Pallas kernels  103 us (39%)
  starting transfers between devices  60.4 us (23%)
  waiting for transfers between devices  47.8 us (18%)
  local copies, waits for them, and re-layouts  24.1 us (9%)
  other arithmetic  19.6 us (7%)
  between operations  5.65 us (2%)
    pallas_call x9, Pallas kernels, call(): pl.pallas_call(kernel, name=name, out_shape=outs, in_specs=in_specs, out_...  103 us
    ppermute x42, starting transfers between devices, send(): return lax.ppermute(values, ALL, where)  48.6 us
    ppermute x42, waiting for transfers between devices, send(): return lax.ppermute(values, ALL, where)  47.8 us
    all_to_all x1, starting transfers between devices, body(): lax.all_to_all(outgoing, ALL, split_axis=0, concat_axis=0, tiled=True)  11.8 us
    unnamed x128, local copies, waits for them, and re-layouts  10.1 us
  transfers between devices with their start and end apart: 43, of which 18 were waited for; matrix products, arithmetic and copies ran while one was open for 10% of the time, Pallas kernels for 29%

profile of v1, /device:TPU:1, one launch (start us, length us, event | category | flops | bytes accessed | tf_op | source)
XLA Modules:
  0.0 260.7 jit_solution(7899623733401460540)
XLA Ops:
  2.6 3.6 %collective-permute-start.2 = (bf16[48,4608]{1,0:T(8,128)(2,1)S(1)}, bf16[48,4608]{1,0:T(8,128)(2,1)S(1)}, u32[]{:S(2)}, u32[]{:S(2)}) collective-permute-start(bf16[48,4608]{1,0:T(8,128)(2,1)S(1)} %constant_dynamic-update-slice_fusion), channel_id=1, source_target_pairs={{0,6},{1,25},{2,4},{3,27},{4,2},{5,29},{6,0},{7,31},{8,14},{9,17},... | collective-permute-start | bytes 1327112 | tf_op jit(solution)/shard_map/ppermute | solution.py:519
  11.2 11.8 %all-to-all-start = ((bf16[128,16,128]{2,1,0:T(8,128)(2,1)}), bf16[128,16,128]{2,1,0:T(8,128)(2,1)}, u32[]{:S(2)}, u32[]{:S(2)}) async-start(bf16[128,16,128]{2,1,0:T(8,128)(2,1)} %select_add_fusion), calls=%async_computation | async-start | bytes 1048576 | tf_op jit(solution)/shard_map/all_to_all | solution.py:628
  24.4 3.3 %collective-permute-start.5 = (bf16[2,48,3072]{2,1,0:T(8,128)(2,1)S(1)}, bf16[2,48,3072]{2,1,0:T(8,128)(2,1)S(1)}, u32[]{:S(2)}, u32[]{:S(2)}) collective-permute-start(bf16[2,48,3072]{2,1,0:T(8,128)(2,1)S(1)} %get-tuple-element.82), channel_id=1, source_target_pairs={{0,24},{1,7},{2,26},{3,5},{4,28},{5,3},{6,30},{7,1},{8,16},{9,15},... | collective-permute-start | bytes 1769480 | tf_op jit(solution)/shard_map/ppermute | solution.py:519
  29.8 10.1 %collective-permute-done.5.refs_2_ = bf16[2,48,3072]{2,1,0:T(8,128)(2,1)S(1)} collective-permute-done((bf16[2,48,3072]{2,1,0:T(8,128)(2,1)S(1)}, bf16[2,48,3072]{2,1,0:T(8,128)(2,1)S(1)}, u32[]{:S(2)}, u32[]{:S(2)}) %collective-permute-start.5) | collective-permute-done | bytes 589856 | tf_op jit(solution)/shard_map/ppermute | solution.py:519
  39.9 1.2 pad_maximum_fusion.2
  41.1 1.3 pad_maximum_fusion.1
  43.4 1.6 slice_bitcast_fusion.9
  45.0 10.0 %stem.1 = (f32[512,1536]{1,0:T(8,128)}, bf16[512,1536]{1,0:T(8,128)(2,1)}, bf16[512,1536]{1,0:T(8,128)(2,1)}, bf16[1536,512]{1,0:T(8,128)(2,1)}, bf16[512,512]{1...) custom-call(bf16[2,48,3072]{2,1,0:T(8,128)(2,1)} %copy-done.9, s32[4]{0:T(128)} %frames_of.11, ...), custom_call_target="tpu_custom_call" | custom-call | flops 805306368 | bytes 14680064 | tf_op jit(solution)/shard_map/stem/pallas_call | solution.py:373
  62.2 1.9 collective-permute-start.8
  65.4 1.7 collective-permute-done.7.refs_10_.refs_1_
  67.1 1.2 collective-permute-start.18
  71.2 1.2 collective-permute-start.10
  72.5 2.7 %collective-permute-start.9 = (bf16[2,2,48,1536]{3,2,1,0:T(8,128)(2,1)S(1)}, bf16[2,2,48,1536]{3,2,1,0:T(8,128)(2,1)S(1)}, u32[]{:S(2)}, u32[]{:S(2)}) collective-permute-start(bf16[2,2,48,1536]{3,2,1,0:T(8,128)(2,1)S(1)} %pad_maximum_fusion.6), channel_id=1, source_target_pairs={{0,24},{1,7},{2,26},{3,5},{4,28},{5,3},{6,30},{7,1},{8,16},{9,15},... | collective-permute-start | bytes 1769480 | tf_op jit(solution)/shard_map/ppermute | solution.py:519
  78.7 16.2 %gate.1 = (f32[512,1536]{1,0:T(8,128)}, f32[512,1536]{1,0:T(8,128)}, f32[512,1536]{1,0:T(8,128)}) custom-call(s32[32]{0:T(128)} %pad_add_fusion.offsets, s32[4]{0:T(128)} %frames_of.11, bf16[4,48,3072]{2,1,0:T(8,128)(2,1)} %get-tuple-element.76.refs_0_, bf16[2,48,3072]{2,1,0:T(8,128)(2,1)} %copy-done.9, bf16[2,48,3072]{2,1,0:T(8,128)(2,1)} %copy-done.8, ...), custom_call_target="tpu_custom_call" | custom-call | flops 4831838208 | bytes 23068672 | tf_op jit(solution)/shard_map/gate/pallas_call | solution.py:373
  95.9 10.7 %out_grad.1 = (bf16[16,48,1536]{2,1,0:T(8,128)(2,1)}, bf16[16,48,1536]{2,1,0:T(8,128)(2,1)}, bf16[512,1536]{1,0:T(8,128)(2,1)}) custom-call(s32[33]{0:T(128)} %pad_add_fusion.1.slots, bf16[2,2,48,1536]{3,2,1,0:T(8,128)(2,1)} %copy-done.27, bf16[2,2,48,1536]{3,2,1,0:T(8,128)(2,1)} %copy-done.26, f32[512,1536]{1,0:T(8,128)} %get-tuple-element.40.filtered.refs_13_, ...), custom_call_target="tpu_custom_call" | custom-call | flops 2415919104 | bytes 11534336 | tf_op jit(solution)/shard_map/out_grad/pallas_call | solution.py:373
  107.7 5.3 %collective-permute-done.21 = bf16[16,48,1536]{2,1,0:T(8,128)(2,1)S(1)} collective-permute-done((bf16[16,48,1536]{2,1,0:T(8,128)(2,1)}, bf16[16,48,1536]{2,1,0:T(8,128)(2,1)S(1)}, u32[]{:S(2)}, u32[]{:S(2)}) %collective-permute-start.21) | collective-permute-done | bytes 2359328 | tf_op jit(solution)/shard_map/ppermute | solution.py:519
  113.2 2.6 add_convert_fusion.3
  116.0 2.6 collective-permute-start.23
  118.5 1.3 collective-permute-start.24
  121.5 13.4 %middle.1 = (f32[512,1536]{1,0:T(8,128)}, f32[1,1536]{1,0:T(1,128)}) custom-call(s32[32]{0:T(128)} %pad_add_fusion.offsets, bf16[4,48,1536]{2,1,0:T(8,128)(2,1)} %copy-done.7, bf16[2,48,1536]{2,1,0:T(8,128)(2,1)} %copy-done.14, bf16[2,48,1536]{2,1,0:T(8,128)(2,1)} %copy-done.16, bf16[4,48,1536]{2,1,0:T(8,128)(2,1)} %bitcast.78, ...), custom_call_target="tpu_custom_call" | custom-call | flops 2415919104 | bytes 13631488 | tf_op jit(solution)/shard_map/middle/pallas_call | solution.py:373
  135.2 11.6 %conv_back.2 = (bf16[512,1024]{1,0:T(8,128)(2,1)}, bf16[512,1024]{1,0:T(8,128)(2,1)}, bf16[16,48,2048]{2,1,0:T(8,128)(2,1)}, bf16[16,48,2048]{2,1,0:T(8,128)(2,1)}, f32[32,1024]{1,0:T(8,128)}) custom-call(s32[33]{0:T(128)} %pad_add_fusion.1.slots, s32[4]{0:T(128)} %frames_of.11, bf16[4,48,1536]{2,1,0:T(8,128)(2,1)} %collective-permute-done.22.unused_1, ...), custom_call_target="tpu_custom_call" | custom-call | flops 3221225472 | bytes 15379114 | tf_op jit(solution)/shard_map/conv_back/pallas_call | solution.py:373
  146.8 2.2 collective-permute-start.25
  149.0 7.3 %conv_back.3 = (bf16[512,512]{1,0:T(8,128)(2,1)}, bf16[512,512]{1,0:T(8,128)(2,1)}, bf16[16,48,1024]{2,1,0:T(8,128)(2,1)}, bf16[16,48,1024]{2,1,0:T(8,128)(2,1)}, f32[32,512]{1,0:T(8,128)}) custom-call(s32[33]{0:T(128)} %pad_add_fusion.1.slots, s32[4]{0:T(128)} %frames_of.11, bf16[4,48,1536]{2,1,0:T(8,128)(2,1)} %collective-permute-done.22.unused_1, ...), custom_call_target="tpu_custom_call" | custom-call | flops 1610612736 | bytes 7689557 | tf_op jit(solution)/shard_map/conv_back/pallas_call | solution.py:373
  157.8 2.2 collective-permute-done.30
  161.4 1.2 copy-done.35
  163.5 4.6 %chip_sum.1 = (bf16[4,48,3072]{2,1,0:T(8,128)(2,1)S(1)}, bf16[4,48,3072]{2,1,0:T(8,128)(2,1)S(1)}, bf16[4,48,3072]{2,1,0:T(8,128)(2,1)S(1)}, bf16[4,48,3072]{2,1,0:T(8,128)(2,1)S(1)}) custom-call(bf16[4,4,48,2048]{3,2,1,0:T(8,128)(2,1)} %bitcast.67, bf16[4,4,48,2048]{3,2,1,0:T(8,128)(2,1)} %bitcast.68, bf16[4,4,48,1024]{3,2,1,0:T(8,128)(2,1)} %bitcast.80, ...), custom_call_target="tpu_custom_call" | custom-call | flops 2359296 | bytes 14680064 | tf_op jit(solution)/shard_map/chip_sum/pallas_call | solution.py:373
  169.4 2.2 collective-permute-start.28
  171.6 1.4 collective-permute-start.29
  173.0 20.1 %stem_back.1 = (f32[1,1536]{1,0:T(1,128)}, f32[16,48]{1,0:T(8,128)}) custom-call(s32[32]{0:T(128)} %pad_add_fusion.offsets, s32[4]{0:T(128)} %frames_of.11, bf16[4,48,3072]{2,1,0:T(8,128)(2,1)} %get-tuple-element.76.refs_0_, bf16[2,48,3072]{2,1,0:T(8,128)(2,1)} %copy-done.9, bf16[2,48,3072]{2,1,0:T(8,128)(2,1)} %copy-done.8, bf16[4,48,3072]{2,1,0:T(8,128)(2,1)} %bitcast.66, ...), custom_call_target="tpu_custom_call" | custom-call | flops 4831838208 | bytes 20971520 | tf_op jit(solution)/shard_map/stem_back/pallas_call | solution.py:373
  193.2 9.2 %mixed.1 = bf16[512,1536]{1,0:T(8,128)(2,1)} custom-call(s32[32]{0:T(128)} %pad_add_fusion.offsets, s32[4]{0:T(128)} %frames_of.11, bf16[4,48,1536]{2,1,0:T(8,128)(2,1)} %copy-done.7, bf16[2,48,1536]{2,1,0:T(8,128)(2,1)} %copy-done.14, bf16[2,48,1536]{2,1,0:T(8,128)(2,1)} %copy-done.16, bf16[4,48,1536]{2,1,0:T(8,128)(2,1)} %bitcast.79, ...), custom_call_target="tpu_custom_call" | custom-call | flops 2415919104 | bytes 10485760 | tf_op jit(solution)/shard_map/mixed/pallas_call | solution.py:373
  206.4 2.3 add_convert_fusion.1
  208.7 2.8 %add_convert_fusion = bf16[4,48,3072]{2,1,0:T(8,128)(2,1)S(1)} fusion(bf16[4,48,3072]{2,1,0:T(8,128)(2,1)} %collective-permute-done.29, bf16[4,48,3072]{2,1,0:T(8,128)(2,1)} %collective-permute-done.28, bf16[4,48,3072]{2,1,0:T(8,128)(2,1)} %collective-permute-done.27, bf16[4,48,3072]{2,1,0:T(8,128)(2,1)S(1)} %copy-done.6, f32[]{:T(128)} %bitcast.32), kind=kLoop, calls=%fused_computation.1 | loop fusion | flops 5308416 | bytes 5898244 | tf_op jit(solution)/shard_map/convert_element_type | solution.py:662
  211.9 1.9 collective-permute-start.32
  213.8 1.9 collective-permute-start.33
  215.7 4.4 %collective-permute-done.31 = bf16[56,4608]{1,0:T(8,128)(2,1)S(1)} collective-permute-done((bf16[56,4608]{1,0:T(8,128)(2,1)S(1)}, bf16[56,4608]{1,0:T(8,128)(2,1)S(1)}, u32[]{:S(2)}, u32[]{:S(2)}) %collective-permute-start.31) | collective-permute-done | bytes 516128 | tf_op jit(solution)/shard_map/ppermute | solution.py:519
  220.1 6.0 %collective-permute-done.32 = bf16[56,4608]{1,0:T(8,128)(2,1)S(1)} collective-permute-done((bf16[56,4608]{1,0:T(8,128)(2,1)S(1)}, bf16[56,4608]{1,0:T(8,128)(2,1)S(1)}, u32[]{:S(2)}, u32[]{:S(2)}) %collective-permute-start.32) | collective-permute-done | bytes 516128 | tf_op jit(solution)/shard_map/ppermute | solution.py:519
  226.1 2.6 %collective-permute-done.33 = bf16[56,4608]{1,0:T(8,128)(2,1)S(1)} collective-permute-done((bf16[56,4608]{1,0:T(8,128)(2,1)S(1)}, bf16[56,4608]{1,0:T(8,128)(2,1)S(1)}, u32[]{:S(2)}, u32[]{:S(2)}) %collective-permute-start.33) | collective-permute-done | bytes 516128 | tf_op jit(solution)/shard_map/ppermute | solution.py:519
  229.7 1.6 collective-permute-start.36
  231.3 3.1 %collective-permute-done.34 = bf16[56,2304]{1,0:T(8,128)(2,1)S(1)} collective-permute-done((bf16[56,2304]{1,0:T(8,128)(2,1)S(1)}, bf16[56,2304]{1,0:T(8,128)(2,1)S(1)}, u32[]{:S(2)}, u32[]{:S(2)}) %collective-permute-start.34) | collective-permute-done | bytes 258080 | tf_op jit(solution)/shard_map/ppermute | solution.py:519
  234.3 1.7 collective-permute-done.36
  236.3 1.7 collective-permute-start.35
  238.0 3.5 %collective-permute-done.37 = bf16[56,2304]{1,0:T(8,128)(2,1)S(1)} collective-permute-done((bf16[56,2304]{1,0:T(8,128)(2,1)S(1)}, bf16[56,2304]{1,0:T(8,128)(2,1)S(1)}, u32[]{:S(2)}, u32[]{:S(2)}) %collective-permute-start.37) | collective-permute-done | bytes 258080 | tf_op jit(solution)/shard_map/ppermute | solution.py:519
  241.5 1.2 collective-permute-done.35
  242.9 2.5 collective-permute-start.39
  245.5 1.3 collective-permute-start.40
  247.2 2.4 collective-permute-done.39
  249.6 1.5 collective-permute-done.40
  251.2 6.5 %collective-permute-start.41 = (f32[18,1536]{1,0:T(8,128)S(1)}, f32[18,1536]{1,0:T(8,128)S(1)}, u32[]{:S(2)}, u32[]{:S(2)}) collective-permute-start(f32[18,1536]{1,0:T(8,128)S(1)} %add_add_fusion), channel_id=1, source_target_pairs={{0,1},{1,0},{2,3},{3,2},{4,5},{5,4},{6,7},{7,6},{8,9},{9,8},{10,11... | collective-permute-start | bytes 331784 | tf_op jit(solution)/shard_map/ppermute | solution.py:519
  (242 shorter events, 40.3 us)
Async XLA Ops:
  2.6 21.0 %collective-permute-start.2 = (bf16[48,4608]{1,0:T(8,128)(2,1)S(1)}, bf16[48,4608]{1,0:T(8,128)(2,1)S(1)}, u32[]{:S(2)}, u32[]{:S(2)}) collective-permute-start(bf16[48,4608]{1,0:T(8,128)(2,1)S(1)} %constant_dynamic-update-slice_fusion), channel_id=1, source_target_pairs={{0,6},{1,25},{2,4},{3,27},{4,2},{5,29},{6,0},{7,31},{8,14},{9,17},... | collective-permute-start | bytes 1327112 | tf_op jit(solution)/shard_map/ppermute | solution.py:519
  6.3 17.4 %collective-permute-start.1 = (bf16[48,4608]{1,0:T(8,128)(2,1)S(1)}, bf16[48,4608]{1,0:T(8,128)(2,1)S(1)}, u32[]{:S(2)}, u32[]{:S(2)}) collective-permute-start(bf16[48,4608]{1,0:T(8,128)(2,1)S(1)} %constant_dynamic-update-slice_fusion), channel_id=1, source_target_pairs={{0,4},{1,17},{2,6},{3,19},{4,0},{5,21},{6,2},{7,23},{8,12},{9,25},... | collective-permute-start | bytes 1327112 | tf_op jit(solution)/shard_map/ppermute | solution.py:519
  6.6 21.0 %collective-permute-start = (bf16[48,4608]{1,0:T(8,128)(2,1)S(1)}, bf16[48,4608]{1,0:T(8,128)(2,1)S(1)}, u32[]{:S(2)}, u32[]{:S(2)}) collective-permute-start(bf16[48,4608]{1,0:T(8,128)(2,1)S(1)} %constant_dynamic-update-slice_fusion), channel_id=1, source_target_pairs={{0,2},{1,9},{2,0},{3,11},{4,6},{5,13},{6,4},{7,15},{8,10},{9,1},{1... | collective-permute-start | bytes 1327112 | tf_op jit(solution)/shard_map/ppermute | solution.py:519
  10.2 12.9 %copy-start.51 = (f32[1536]{0:T(1024)S(1)}, f32[1536]{0:T(1024)}, u32[]{:S(2)}) copy-start(f32[1536]{0:T(1024)} %param.24) | copy-start | bytes 18436
  11.2 33.8 %all-to-all-start = ((bf16[128,16,128]{2,1,0:T(8,128)(2,1)}), bf16[128,16,128]{2,1,0:T(8,128)(2,1)}, u32[]{:S(2)}, u32[]{:S(2)}) async-start(bf16[128,16,128]{2,1,0:T(8,128)(2,1)} %select_add_fusion), calls=%async_computation | async-start | bytes 1048576 | tf_op jit(solution)/shard_map/all_to_all | solution.py:628
  24.4 15.5 %collective-permute-start.5 = (bf16[2,48,3072]{2,1,0:T(8,128)(2,1)S(1)}, bf16[2,48,3072]{2,1,0:T(8,128)(2,1)S(1)}, u32[]{:S(2)}, u32[]{:S(2)}) collective-permute-start(bf16[2,48,3072]{2,1,0:T(8,128)(2,1)S(1)} %get-tuple-element.82), channel_id=1, source_target_pairs={{0,24},{1,7},{2,26},{3,5},{4,28},{5,3},{6,30},{7,1},{8,16},{9,15},... | collective-permute-start | bytes 1769480 | tf_op jit(solution)/shard_map/ppermute | solution.py:519
  28.4 12.7 %collective-permute-start.3 = (bf16[2,48,3072]{2,1,0:T(8,128)(2,1)S(1)}, bf16[2,48,3072]{2,1,0:T(8,128)(2,1)S(1)}, u32[]{:S(2)}, u32[]{:S(2)}) collective-permute-start(bf16[2,48,3072]{2,1,0:T(8,128)(2,1)S(1)} %get-tuple-element.84), channel_id=1, source_target_pairs={{0,8},{1,3},{2,10},{3,1},{4,12},{5,7},{6,14},{7,5},{8,0},{9,11},{1... | collective-permute-start | bytes 1769480 | tf_op jit(solution)/shard_map/ppermute | solution.py:519
  39.9 18.4 %copy-start.8 = (bf16[2,48,3072]{2,1,0:T(8,128)(2,1)}, bf16[2,48,3072]{2,1,0:T(8,128)(2,1)S(1)}, u32[]{:S(2)}) copy-start(bf16[2,48,3072]{2,1,0:T(8,128)(2,1)S(1)} %collective-permute-done.5.refs_2_) | copy-start | bytes 1769476
  41.1 17.2 %collective-permute-start.6 = (bf16[2,2,48,3072]{3,2,1,0:T(8,128)(2,1)}, bf16[2,2,48,3072]{3,2,1,0:T(8,128)(2,1)S(1)}, u32[]{:S(2)}, u32[]{:S(2)}) collective-permute-start(bf16[2,2,48,3072]{3,2,1,0:T(8,128)(2,1)} %pad_maximum_fusion.2), channel_id=1, source_target_pairs={{0,8},{1,3},{2,10},{3,1},{4,12},{5,7},{6,14},{7,5},{8,0},{9,11},{1... | collective-permute-start | bytes 3538952 | tf_op jit(solution)/shard_map/ppermute | solution.py:519
  42.4 16.7 %collective-permute-start.4 = (bf16[2,2,48,3072]{3,2,1,0:T(8,128)(2,1)}, bf16[2,2,48,3072]{3,2,1,0:T(8,128)(2,1)S(1)}, u32[]{:S(2)}, u32[]{:S(2)}) collective-permute-start(bf16[2,2,48,3072]{3,2,1,0:T(8,128)(2,1)} %pad_maximum_fusion.1), channel_id=1, source_target_pairs={{0,24},{1,7},{2,26},{3,5},{4,28},{5,3},{6,30},{7,1},{8,16},{9,15},... | collective-permute-start | bytes 3538952 | tf_op jit(solution)/shard_map/ppermute | solution.py:519
  45.0 11.9 %copy-start.25 = (bf16[1,48,3072]{2,1,0:T(8,128)(2,1)S(1)}, bf16[1,48,3072]{2,1,0:T(8,128)(2,1)}, u32[]{:S(2)}) copy-start(bf16[1,48,3072]{2,1,0:T(8,128)(2,1)} %copy-done.24) | copy-start | bytes 884740
  58.2 18.7 %collective-permute-start.16 = (bf16[4,48,3072]{2,1,0:T(8,128)(2,1)S(1)}, bf16[4,48,3072]{2,1,0:T(8,128)(2,1)S(1)}, u32[]{:S(2)}, u32[]{:S(2)}) collective-permute-start(bf16[4,48,3072]{2,1,0:T(8,128)(2,1)S(1)} %get-tuple-element.75), channel_id=1, source_target_pairs={{0,1},{1,0},{2,3},{3,2},{4,5},{5,4},{6,7},{7,6},{8,9},{9,8},{10,11... | collective-permute-start | bytes 3538952 | tf_op jit(solution)/shard_map/ppermute | solution.py:519
  61.1 45.5 %copy-start.7 = (bf16[4,48,1536]{2,1,0:T(8,128)(2,1)}, bf16[4,48,1536]{2,1,0:T(8,128)(2,1)S(1)}, u32[]{:S(2)}) copy-start(bf16[4,48,1536]{2,1,0:T(8,128)(2,1)S(1)} %maximum_add_fusion.refs_0_) | copy-start | bytes 1769476
  61.2 5.9 %collective-permute-start.7 = (bf16[2,48,1536]{2,1,0:T(8,128)(2,1)S(1)}, bf16[2,48,1536]{2,1,0:T(8,128)(2,1)S(1)}, u32[]{:S(2)}, u32[]{:S(2)}) collective-permute-start(bf16[2,48,1536]{2,1,0:T(8,128)(2,1)S(1)} %get-tuple-element.80), channel_id=1, source_target_pairs={{0,8},{1,3},{2,10},{3,1},{4,12},{5,7},{6,14},{7,5},{8,0},{9,11},{1... | collective-permute-start | bytes 884744 | tf_op jit(solution)/shard_map/ppermute | solution.py:519
  62.2 7.1 %collective-permute-start.8 = (bf16[2,48,1536]{2,1,0:T(8,128)(2,1)S(1)}, bf16[2,48,1536]{2,1,0:T(8,128)(2,1)S(1)}, u32[]{:S(2)}, u32[]{:S(2)}) collective-permute-start(bf16[2,48,1536]{2,1,0:T(8,128)(2,1)S(1)} %get-tuple-element.79), channel_id=1, source_target_pairs={{0,24},{1,7},{2,26},{3,5},{4,28},{5,3},{6,30},{7,1},{8,16},{9,15},... | collective-permute-start | bytes 884744 | tf_op jit(solution)/shard_map/ppermute | solution.py:519
  64.3 12.7 %collective-permute-start.20 = (bf16[4,48,3072]{2,1,0:T(8,128)(2,1)S(1)}, bf16[4,48,3072]{2,1,0:T(8,128)(2,1)S(1)}, u32[]{:S(2)}, u32[]{:S(2)}) collective-permute-start(bf16[4,48,3072]{2,1,0:T(8,128)(2,1)S(1)} %broadcast_add_fusion), channel_id=1, source_target_pairs={{0,1},{1,0},{2,3},{3,2},{4,5},{5,4},{6,7},{7,6},{8,9},{9,8},{10,11... | collective-permute-start | bytes 3538952 | tf_op jit(solution)/shard_map/ppermute | solution.py:519
  64.6 12.4 %collective-permute-start.19 = (bf16[4,48,3072]{2,1,0:T(8,128)(2,1)S(1)}, bf16[4,48,3072]{2,1,0:T(8,128)(2,1)S(1)}, u32[]{:S(2)}, u32[]{:S(2)}) collective-permute-start(bf16[4,48,3072]{2,1,0:T(8,128)(2,1)S(1)} %broadcast_add_fusion.1), channel_id=1, source_target_pairs={{0,1},{1,0},{2,3},{3,2},{4,5},{5,4},{6,7},{7,6},{8,9},{9,8},{10,11... | collective-permute-start | bytes 3538952 | tf_op jit(solution)/shard_map/ppermute | solution.py:519
  67.1 4.1 %collective-permute-start.18 = (bf16[2,48,3072]{2,1,0:T(8,128)(2,1)S(1)}, bf16[2,48,3072]{2,1,0:T(8,128)(2,1)S(1)}, u32[]{:S(2)}, u32[]{:S(2)}) collective-permute-start(bf16[2,48,3072]{2,1,0:T(8,128)(2,1)S(1)} %broadcast_add_fusion.3), channel_id=1, source_target_pairs={{0,1},{1,0},{2,3},{3,2},{4,5},{5,4},{6,7},{7,6},{8,9},{9,8},{10,11... | collective-permute-start | bytes 1769480 | tf_op jit(solution)/shard_map/ppermute | solution.py:519
  69.3 3.2 %collective-permute-start.17 = (bf16[2,48,3072]{2,1,0:T(8,128)(2,1)S(1)}, bf16[2,48,3072]{2,1,0:T(8,128)(2,1)S(1)}, u32[]{:S(2)}, u32[]{:S(2)}) collective-permute-start(bf16[2,48,3072]{2,1,0:T(8,128)(2,1)S(1)} %broadcast_add_fusion.4), channel_id=1, source_target_pairs={{0,1},{1,0},{2,3},{3,2},{4,5},{5,4},{6,7},{7,6},{8,9},{9,8},{10,11... | collective-permute-start | bytes 1769480 | tf_op jit(solution)/shard_map/ppermute | solution.py:519
  71.2 23.6 %collective-permute-start.10 = (bf16[2,2,48,1536]{3,2,1,0:T(8,128)(2,1)}, bf16[2,2,48,1536]{3,2,1,0:T(8,128)(2,1)S(1)}, u32[]{:S(2)}, u32[]{:S(2)}) collective-permute-start(bf16[2,2,48,1536]{3,2,1,0:T(8,128)(2,1)} %pad_maximum_fusion.7), channel_id=1, source_target_pairs={{0,8},{1,3},{2,10},{3,1},{4,12},{5,7},{6,14},{7,5},{8,0},{9,11},{1... | collective-permute-start | bytes 1769480 | tf_op jit(solution)/shard_map/ppermute | solution.py:519
  72.5 22.4 %collective-permute-start.9 = (bf16[2,2,48,1536]{3,2,1,0:T(8,128)(2,1)S(1)}, bf16[2,2,48,1536]{3,2,1,0:T(8,128)(2,1)S(1)}, u32[]{:S(2)}, u32[]{:S(2)}) collective-permute-start(bf16[2,2,48,1536]{3,2,1,0:T(8,128)(2,1)S(1)} %pad_maximum_fusion.6), channel_id=1, source_target_pairs={{0,24},{1,7},{2,26},{3,5},{4,28},{5,3},{6,30},{7,1},{8,16},{9,15},... | collective-permute-start | bytes 1769480 | tf_op jit(solution)/shard_map/ppermute | solution.py:519
  106.6 6.4 %collective-permute-start.21 = (bf16[16,48,1536]{2,1,0:T(8,128)(2,1)}, bf16[16,48,1536]{2,1,0:T(8,128)(2,1)S(1)}, u32[]{:S(2)}, u32[]{:S(2)}) collective-permute-start(bf16[16,48,1536]{2,1,0:T(8,128)(2,1)} %get-tuple-element.43), channel_id=1, source_target_pairs={{0,1},{1,0},{2,3},{3,2},{4,5},{5,4},{6,7},{7,6},{8,9},{9,8},{10,11... | collective-permute-start | bytes 7077896 | tf_op jit(solution)/shard_map/ppermute | solution.py:519
  106.6 11.9 %collective-permute-start.11 = (bf16[4,48,1536]{2,1,0:T(8,128)(2,1)S(1)}, bf16[4,48,1536]{2,1,0:T(8,128)(2,1)S(1)}, u32[]{:S(2)}, u32[]{:S(2)}) collective-permute-start(bf16[4,48,1536]{2,1,0:T(8,128)(2,1)S(1)} %maximum_add_fusion.refs_0_), channel_id=1, source_target_pairs={{0,1},{1,0},{2,3},{3,2},{4,5},{5,4},{6,7},{7,6},{8,9},{9,8},{10,11... | collective-permute-start | bytes 1769480 | tf_op jit(solution)/shard_map/ppermute | solution.py:519
  107.1 8.7 %collective-permute-start.12 = (bf16[2,48,1536]{2,1,0:T(8,128)(2,1)S(1)}, bf16[2,48,1536]{2,1,0:T(8,128)(2,1)S(1)}, u32[]{:S(2)}, u32[]{:S(2)}) collective-permute-start(bf16[2,48,1536]{2,1,0:T(8,128)(2,1)S(1)} %copy-done.15), channel_id=1, source_target_pairs={{0,1},{1,0},{2,3},{3,2},{4,5},{5,4},{6,7},{7,6},{8,9},{9,8},{10,11... | collective-permute-start | bytes 884744 | tf_op jit(solution)/shard_map/ppermute | solution.py:519
  107.2 8.7 %collective-permute-start.13 = (bf16[2,48,1536]{2,1,0:T(8,128)(2,1)S(1)}, bf16[2,48,1536]{2,1,0:T(8,128)(2,1)S(1)}, u32[]{:S(2)}, u32[]{:S(2)}) collective-permute-start(bf16[2,48,1536]{2,1,0:T(8,128)(2,1)S(1)} %copy-done.17), channel_id=1, source_target_pairs={{0,1},{1,0},{2,3},{3,2},{4,5},{5,4},{6,7},{7,6},{8,9},{9,8},{10,11... | collective-permute-start | bytes 884744 | tf_op jit(solution)/shard_map/ppermute | solution.py:519
  107.6 12.2 %collective-permute-start.15 = (bf16[4,48,1536]{2,1,0:T(8,128)(2,1)}, bf16[4,48,1536]{2,1,0:T(8,128)(2,1)S(1)}, u32[]{:S(2)}, u32[]{:S(2)}) collective-permute-start(bf16[4,48,1536]{2,1,0:T(8,128)(2,1)} %bitcast.74), channel_id=1, source_target_pairs={{0,1},{1,0},{2,3},{3,2},{4,5},{5,4},{6,7},{7,6},{8,9},{9,8},{10,11... | collective-permute-start | bytes 1769480 | tf_op jit(solution)/shard_map/ppermute | solution.py:519
  113.0 6.8 %collective-permute-start.14 = (bf16[4,48,1536]{2,1,0:T(8,128)(2,1)}, bf16[4,48,1536]{2,1,0:T(8,128)(2,1)S(1)}, u32[]{:S(2)}, u32[]{:S(2)}) collective-permute-start(bf16[4,48,1536]{2,1,0:T(8,128)(2,1)} %bitcast.77), channel_id=1, source_target_pairs={{0,1},{1,0},{2,3},{3,2},{4,5},{5,4},{6,7},{7,6},{8,9},{9,8},{10,11... | collective-permute-start | bytes 1769480 | tf_op jit(solution)/shard_map/ppermute | solution.py:519
  115.8 19.0 %collective-permute-start.22 = (bf16[4,48,1536]{2,1,0:T(8,128)(2,1)S(1)}, bf16[4,48,1536]{2,1,0:T(8,128)(2,1)}, u32[]{:S(2)}, u32[]{:S(2)}) collective-permute-start(bf16[4,48,1536]{2,1,0:T(8,128)(2,1)S(1)} %get-tuple-element.71.refs_10_), channel_id=1, source_target_pairs={{0,2},{1,9},{2,0},{3,11},{4,6},{5,13},{6,4},{7,15},{8,10},{9,1},{1... | collective-permute-start | bytes 1769480 | tf_op jit(solution)/shard_map/ppermute | solution.py:519
  116.0 18.9 %collective-permute-start.23 = (bf16[4,48,1536]{2,1,0:T(8,128)(2,1)S(1)}, bf16[4,48,1536]{2,1,0:T(8,128)(2,1)}, u32[]{:S(2)}, u32[]{:S(2)}) collective-permute-start(bf16[4,48,1536]{2,1,0:T(8,128)(2,1)S(1)} %get-tuple-element.70.refs_11_), channel_id=1, source_target_pairs={{0,4},{1,17},{2,6},{3,19},{4,0},{5,21},{6,2},{7,23},{8,12},{9,25},... | collective-permute-start | bytes 1769480 | tf_op jit(solution)/shard_map/ppermute | solution.py:519
  118.5 16.7 %collective-permute-start.24 = (bf16[4,48,1536]{2,1,0:T(8,128)(2,1)S(1)}, bf16[4,48,1536]{2,1,0:T(8,128)(2,1)}, u32[]{:S(2)}, u32[]{:S(2)}) collective-permute-start(bf16[4,48,1536]{2,1,0:T(8,128)(2,1)S(1)} %get-tuple-element.69.refs_12_), channel_id=1, source_target_pairs={{0,6},{1,25},{2,4},{3,27},{4,2},{5,29},{6,0},{7,31},{8,14},{9,17},... | collective-permute-start | bytes 1769480 | tf_op jit(solution)/shard_map/ppermute | solution.py:519
  146.8 14.6 %collective-permute-start.25 = (bf16[16,48,2048]{2,1,0:T(8,128)(2,1)}, bf16[16,48,2048]{2,1,0:T(8,128)(2,1)S(1)}, u32[]{:S(2)}, u32[]{:S(2)}) collective-permute-start(bf16[16,48,2048]{2,1,0:T(8,128)(2,1)} %get-tuple-element.53), channel_id=1, source_target_pairs={{0,1},{1,0},{2,3},{3,2},{4,5},{5,4},{6,7},{7,6},{8,9},{9,8},{10,11... | collective-permute-start | bytes 9437192 | tf_op jit(solution)/shard_map/ppermute | solution.py:519
  156.3 5.1 %collective-permute-start.26 = (bf16[16,48,1024]{2,1,0:T(8,128)(2,1)}, bf16[16,48,1024]{2,1,0:T(8,128)(2,1)S(1)}, u32[]{:S(2)}, u32[]{:S(2)}) collective-permute-start(bf16[16,48,1024]{2,1,0:T(8,128)(2,1)} %get-tuple-element.55), channel_id=1, source_target_pairs={{0,1},{1,0},{2,3},{3,2},{4,5},{5,4},{6,7},{7,6},{8,9},{9,8},{10,11... | collective-permute-start | bytes 4718600 | tf_op jit(solution)/shard_map/ppermute | solution.py:519
  157.3 2.7 %collective-permute-start.30 = (f32[16,1536]{1,0:T(8,128)S(1)}, f32[16,1536]{1,0:T(8,128)S(1)}, u32[]{:S(2)}, u32[]{:S(2)}) collective-permute-start(f32[16,1536]{1,0:T(8,128)S(1)} %broadcast_select_fusion), channel_id=1, source_target_pairs={{0,1},{1,0},{2,3},{3,2},{4,5},{5,4},{6,7},{7,6},{8,9},{9,8},{10,11... | collective-permute-start | bytes 294920 | tf_op jit(solution)/shard_map/ppermute | solution.py:519
  169.2 39.5 %collective-permute-start.27 = (bf16[4,48,3072]{2,1,0:T(8,128)(2,1)S(1)}, bf16[4,48,3072]{2,1,0:T(8,128)(2,1)}, u32[]{:S(2)}, u32[]{:S(2)}) collective-permute-start(bf16[4,48,3072]{2,1,0:T(8,128)(2,1)S(1)} %get-tuple-element.56.refs_14_), channel_id=1, source_target_pairs={{0,2},{1,9},{2,0},{3,11},{4,6},{5,13},{6,4},{7,15},{8,10},{9,1},{1... | collective-permute-start | bytes 3538952 | tf_op jit(solution)/shard_map/ppermute | solution.py:519
  169.4 39.3 %collective-permute-start.28 = (bf16[4,48,3072]{2,1,0:T(8,128)(2,1)S(1)}, bf16[4,48,3072]{2,1,0:T(8,128)(2,1)}, u32[]{:S(2)}, u32[]{:S(2)}) collective-permute-start(bf16[4,48,3072]{2,1,0:T(8,128)(2,1)S(1)} %get-tuple-element.57.refs_15_), channel_id=1, source_target_pairs={{0,4},{1,17},{2,6},{3,19},{4,0},{5,21},{6,2},{7,23},{8,12},{9,25},... | collective-permute-start | bytes 3538952 | tf_op jit(solution)/shard_map/ppermute | solution.py:519
  171.6 37.1 %collective-permute-start.29 = (bf16[4,48,3072]{2,1,0:T(8,128)(2,1)S(1)}, bf16[4,48,3072]{2,1,0:T(8,128)(2,1)}, u32[]{:S(2)}, u32[]{:S(2)}) collective-permute-start(bf16[4,48,3072]{2,1,0:T(8,128)(2,1)S(1)} %get-tuple-element.58.refs_16_), channel_id=1, source_target_pairs={{0,6},{1,25},{2,4},{3,27},{4,2},{5,29},{6,0},{7,31},{8,14},{9,17},... | collective-permute-start | bytes 3538952 | tf_op jit(solution)/shard_map/ppermute | solution.py:519
  211.8 8.3 %collective-permute-start.31 = (bf16[56,4608]{1,0:T(8,128)(2,1)S(1)}, bf16[56,4608]{1,0:T(8,128)(2,1)S(1)}, u32[]{:S(2)}, u32[]{:S(2)}) collective-permute-start(bf16[56,4608]{1,0:T(8,128)(2,1)S(1)} %get-tuple-element.72), channel_id=1, source_target_pairs={{0,8},{1,3},{2,10},{3,1},{4,12},{5,7},{6,14},{7,5},{8,0},{9,11},{1... | collective-permute-start | bytes 1548296 | tf_op jit(solution)/shard_map/ppermute | solution.py:519
  211.9 14.2 %collective-permute-start.32 = (bf16[56,4608]{1,0:T(8,128)(2,1)S(1)}, bf16[56,4608]{1,0:T(8,128)(2,1)S(1)}, u32[]{:S(2)}, u32[]{:S(2)}) collective-permute-start(bf16[56,4608]{1,0:T(8,128)(2,1)S(1)} %get-tuple-element.74), channel_id=1, source_target_pairs={{0,16},{1,5},{2,18},{3,7},{4,20},{5,1},{6,22},{7,3},{8,24},{9,13},... | collective-permute-start | bytes 1548296 | tf_op jit(solution)/shard_map/ppermute | solution.py:519
  213.8 15.0 %collective-permute-start.33 = (bf16[56,4608]{1,0:T(8,128)(2,1)S(1)}, bf16[56,4608]{1,0:T(8,128)(2,1)S(1)}, u32[]{:S(2)}, u32[]{:S(2)}) collective-permute-start(bf16[56,4608]{1,0:T(8,128)(2,1)S(1)} %get-tuple-element.73), channel_id=1, source_target_pairs={{0,24},{1,7},{2,26},{3,5},{4,28},{5,3},{6,30},{7,1},{8,16},{9,15},... | collective-permute-start | bytes 1548296 | tf_op jit(solution)/shard_map/ppermute | solution.py:519
  229.1 5.3 %collective-permute-start.34 = (bf16[56,2304]{1,0:T(8,128)(2,1)S(1)}, bf16[56,2304]{1,0:T(8,128)(2,1)S(1)}, u32[]{:S(2)}, u32[]{:S(2)}) collective-permute-start(bf16[56,2304]{1,0:T(8,128)(2,1)S(1)} %get-tuple-element.88), channel_id=1, source_target_pairs={{0,32},{1,33},{2,34},{3,35},{4,36},{5,37},{6,38},{7,39},{8,40},{9,... | collective-permute-start | bytes 774152 | tf_op jit(solution)/shard_map/ppermute | solution.py:519
  229.7 6.4 %collective-permute-start.36 = (bf16[56,2304]{1,0:T(8,128)(2,1)S(1)}, bf16[56,2304]{1,0:T(8,128)(2,1)S(1)}, u32[]{:S(2)}, u32[]{:S(2)}) collective-permute-start(bf16[56,2304]{1,0:T(8,128)(2,1)S(1)} %get-tuple-element.87), channel_id=1, source_target_pairs={{0,96},{1,97},{2,98},{3,99},{4,100},{5,101},{6,102},{7,103},{8,104... | collective-permute-start | bytes 774152 | tf_op jit(solution)/shard_map/ppermute | solution.py:519
  236.2 5.3 %collective-permute-start.37 = (bf16[56,2304]{1,0:T(8,128)(2,1)S(1)}, bf16[56,2304]{1,0:T(8,128)(2,1)S(1)}, u32[]{:S(2)}, u32[]{:S(2)}) collective-permute-start(bf16[56,2304]{1,0:T(8,128)(2,1)S(1)} %get-tuple-element.85), channel_id=1, source_target_pairs={{0,32},{1,33},{2,34},{3,35},{4,36},{5,37},{6,38},{7,39},{8,40},{9,... | collective-permute-start | bytes 774152 | tf_op jit(solution)/shard_map/ppermute | solution.py:519
  236.3 6.4 %collective-permute-start.35 = (bf16[56,2304]{1,0:T(8,128)(2,1)S(1)}, bf16[56,2304]{1,0:T(8,128)(2,1)S(1)}, u32[]{:S(2)}, u32[]{:S(2)}) collective-permute-start(bf16[56,2304]{1,0:T(8,128)(2,1)S(1)} %get-tuple-element.86), channel_id=1, source_target_pairs={{0,96},{1,97},{2,98},{3,99},{4,100},{5,101},{6,102},{7,103},{8,104... | collective-permute-start | bytes 774152 | tf_op jit(solution)/shard_map/ppermute | solution.py:519
  242.8 4.4 %collective-permute-start.38 = (f32[18,1536]{1,0:T(8,128)S(1)}, f32[18,1536]{1,0:T(8,128)S(1)}, u32[]{:S(2)}, u32[]{:S(2)}) collective-permute-start(f32[18,1536]{1,0:T(8,128)S(1)} %fusion.4), channel_id=1, source_target_pairs={{0,2},{1,9},{2,0},{3,11},{4,6},{5,13},{6,4},{7,15},{8,10},{9,1},{1... | collective-permute-start | bytes 331784 | tf_op jit(solution)/shard_map/ppermute | solution.py:519
  242.9 6.7 %collective-permute-start.39 = (f32[18,1536]{1,0:T(8,128)S(1)}, f32[18,1536]{1,0:T(8,128)S(1)}, u32[]{:S(2)}, u32[]{:S(2)}) collective-permute-start(f32[18,1536]{1,0:T(8,128)S(1)} %fusion.4), channel_id=1, source_target_pairs={{0,4},{1,17},{2,6},{3,19},{4,0},{5,21},{6,2},{7,23},{8,12},{9,25},... | collective-permute-start | bytes 331784 | tf_op jit(solution)/shard_map/ppermute | solution.py:519
  245.5 5.7 %collective-permute-start.40 = (f32[18,1536]{1,0:T(8,128)S(1)}, f32[18,1536]{1,0:T(8,128)S(1)}, u32[]{:S(2)}, u32[]{:S(2)}) collective-permute-start(f32[18,1536]{1,0:T(8,128)S(1)} %fusion.4), channel_id=1, source_target_pairs={{0,6},{1,25},{2,4},{3,27},{4,2},{5,29},{6,0},{7,31},{8,14},{9,17},... | collective-permute-start | bytes 331784 | tf_op jit(solution)/shard_map/ppermute | solution.py:519
  246.9 13.8 %copy-start.1 = (bf16[128,16,128]{2,1,0:T(8,128)(2,1)S(1)}, bf16[128,16,128]{2,1,0:T(8,128)(2,1)}, u32[]{:S(2)}) copy-start(bf16[128,16,128]{2,1,0:T(8,128)(2,1)} %param.20) | copy-start | bytes 1572868
  251.2 7.5 %collective-permute-start.41 = (f32[18,1536]{1,0:T(8,128)S(1)}, f32[18,1536]{1,0:T(8,128)S(1)}, u32[]{:S(2)}, u32[]{:S(2)}) collective-permute-start(f32[18,1536]{1,0:T(8,128)S(1)} %add_add_fusion), channel_id=1, source_target_pairs={{0,1},{1,0},{2,3},{3,2},{4,5},{5,4},{6,7},{7,6},{8,9},{9,8},{10,11... | collective-permute-start | bytes 331784 | tf_op jit(solution)/shard_map/ppermute | solution.py:519
  (53 other events, 239.0 us)

commit v2 on v1

--- a/solution.py
+++ b/solution.py
@@ -161,13 +161,19 @@
     lax.fori_loop(0, NU, one, 0)
 
 
-def assemble(offsets, pieces, held, sems):
+def assembly(offsets, pieces, held, sems):
     copies = []
+    layout = PIECES if len(pieces) == NP else DIRECT
     for p, piece in enumerate(pieces):
-        for j, (second, first) in enumerate(PIECES[p % len(PIECES)]):
-            block = p // len(PIECES) * 16 + second * 4 + first
+        for j, (second, first) in enumerate(layout[p % len(layout)]):
+            block = p // len(layout) * 16 + second * 4 + first
             start = pl.multiple_of(offsets[block], 16)
             copies.append(pltpu.make_async_copy(piece.at[j], held.at[pl.ds(start, ROWS), :], sems.at[block]))
+    return copies
+
+
+def assemble(offsets, pieces, held, sems):
+    copies = assembly(offsets, pieces, held, sems)
     for copy in copies:
         copy.start()
     for copy in copies:
@@ -175,7 +181,7 @@
 
 
 def gate_kernel(offsets, frames_of, *refs):
-    pieces, refs = refs[:NP], refs[NP + 2 :]
+    pieces, refs = refs[:NP], refs[NP:]
     normed, spectrum, fwd, inv, value, gate, filtered, held, sems = refs
     n = pl.program_id(0)
 
@@ -202,7 +208,7 @@
     return pl.multiple_of((2 * i + core) * ROWS, 16)
 
 
-def out_kernel(slots, unused, unused_too, filtered, mix_grad, second_gain, mine, other, swished, turned, term):
+def out_kernel(slots, unused_1, unused_2, unused_3, filtered, mix_grad, second_gain, mine, other, swished, turned, term):
     def ahead(u, carry):
         rows = pl.ds(pl.multiple_of(u * UTT, UTT), UTT)
         unit, unused = normalise(filtered[rows, :])
@@ -226,26 +232,40 @@
 
 
 def mid_kernel(offsets, *refs):
-    pieces, refs = refs[:NP], refs[NP:]
-    filtered, mix_grad, second_gain, filter_grad, second_grad, held, sems, back = refs[3:]
-    assemble(offsets, pieces, held, sems)
+    pieces, refs = refs[:ND], refs[ND:]
+    filtered, mix_grad, second_gain, filter_grad, second_grad, held, sems, back, slope, scales = refs
+    copies = assembly(offsets, pieces, held, sems)
+    for copy in copies:
+        copy.start()
     second_grad[...] = jnp.zeros((1, D), F32)
 
-    def product(n, carry):
-        cols = pl.ds(pl.multiple_of(n * CB, CB), CB)
-        back[:, cols] = mm_nt(mix_grad[...], held[cols, :])
-        return carry
-
-    lax.fori_loop(0, NB, product, 0)
-
-    def behind(u, carry):
+    def ahead(u, carry):
         rows = pl.ds(pl.multiple_of(u * UTT, UTT), UTT)
         unit, scale = normalise(filtered[rows, :])
         z = unit * second_gain[...]
         sig = jax.nn.sigmoid(z)
-        dz = back[rows, :] * (sig * (1.0 + z * (1.0 - sig)))
+        slope[rows, :] = sig * (1.0 + z * (1.0 - sig))
+        filter_grad[rows, :] = unit
+        scales[rows, :] = jnp.broadcast_to(scale, (UTT, 128))
+        return carry
+
+    lax.fori_loop(0, NU, ahead, 0)
+    for copy in copies:
+        copy.wait()
+
+    def product(n, carry):
+        cols = pl.ds(pl.multiple_of(n * 2 * CB, 2 * CB), 2 * CB)
+        back[:, cols] = mm_nt(mix_grad[...], held[cols, :])
+        return carry
+
+    lax.fori_loop(0, NB // 2, product, 0)
+
+    def behind(u, carry):
+        rows = pl.ds(pl.multiple_of(u * UTT, UTT), UTT)
+        unit = filter_grad[rows, :]
+        dz = back[rows, :] * slope[rows, :]
         second_grad[...] += jnp.sum(dz * unit, axis=0, keepdims=True)
-        filter_grad[rows, :] = normalise_back(dz * second_gain[...], unit, scale)
+        filter_grad[rows, :] = normalise_back(dz * second_gain[...], unit, scales[rows, :1])
         return carry
 
     lax.fori_loop(0, NU, behind, 0)
@@ -335,7 +355,7 @@
 
 
 def mixed_kernel(offsets, frames_of, *refs):
-    pieces, refs = refs[:NP], refs[NP:]
+    pieces, refs = refs[:ND], refs[ND:]
     unused, swished, embedded, output, held, sems = refs
     assemble(offsets, pieces, held, sems)
 
@@ -393,22 +413,22 @@
         (before, frames_of, arrived, stem_weight, first_gain, conv_kernel, cotangent, tables["ker"]),
         [ANY, SMEM] + [VMEM] * 6, outs, [VMEM] * 7,
         [pltpu.VMEM((TOK * PATCH, MEL), F32), pltpu.VMEM((TOK, D), BF16)],
-        2 * TOK * TOK * D, 14 * MIB, 56,
-    )
-
-
-def gate_forward(offsets, frames_of, pieces, before, normed, spectrum, tables):
+        2 * TOK * TOK * D, 14 * MIB, 26,
+    )
+
+
+def gate_forward(offsets, frames_of, pieces, normed, spectrum, tables):
     whole = lambda n: (0, 0)
     block = lambda n: (0, n)
     return call(
         gate_kernel, "gate",
-        (offsets, frames_of, *pieces, *before, normed, spectrum, tables["fwd"], tables["inv"]),
-        [SMEM, SMEM] + [ANY] * (NP + 2)
+        (offsets, frames_of, *pieces, normed, spectrum, tables["fwd"], tables["inv"]),
+        [SMEM, SMEM] + [ANY] * NP
         + [pl.BlockSpec((TOK, D), whole), pl.BlockSpec((SPEC, CB), block),
            pl.BlockSpec(tables["fwd"].shape, whole), pl.BlockSpec(tables["inv"].shape, whole)],
         [shaped((TOK, D), F32)] * 3, [pl.BlockSpec((TOK, CB), block)] * 3,
         [pltpu.VMEM((D, 2 * D), BF16), pltpu.SemaphoreType.DMA((32,))],
-        2 * TOK * D * 2 * D, 22 * MIB, 56, grid=(NB,),
+        2 * TOK * D * 2 * D, 22 * MIB, 26, grid=(NB,),
     )
 
 
@@ -416,18 +436,19 @@
     half = shaped((16, ROWS, D), BF16)
     return call(
         out_kernel, "out_grad", (slots, *before, filtered, mix_grad, second_gain),
-        [SMEM, ANY, ANY] + [VMEM] * 3, [half, half, shaped((TOK, D), BF16)], [VMEM] * 3,
+        [SMEM] + [ANY] * 3 + [VMEM] * 3, [half, half, shaped((TOK, D), BF16)], [VMEM] * 3,
         [pltpu.VMEM((D, TOK), BF16), pltpu.VMEM((D, CB), BF16)],
-        2 * TOK * D * D, 11 * MIB, 56,
-    )
-
-
-def middle(offsets, pieces, before, filtered, mix_grad, second_gain):
+        16 * 2 * TOK * D * D, 16 * 11 * MIB, 24,
+    )
+
+
+def middle(offsets, pieces, filtered, mix_grad, second_gain):
     return call(
-        mid_kernel, "middle", (offsets, *pieces, *before, filtered, mix_grad, second_gain),
-        [SMEM] + [ANY] * (NP + 3) + [VMEM] * 3, [shaped((TOK, D), F32), shaped((1, D), F32)], [VMEM] * 2,
-        [pltpu.VMEM((D, D), BF16), pltpu.SemaphoreType.DMA((32,)), pltpu.VMEM((TOK, D), F32)],
-        2 * TOK * D * D, 13 * MIB, 56,
+        mid_kernel, "middle", (offsets, *pieces, filtered, mix_grad, second_gain),
+        [SMEM] + [ANY] * ND + [VMEM] * 3, [shaped((TOK, D), F32), shaped((1, D), F32)], [VMEM] * 2,
+        [pltpu.VMEM((D, D), BF16), pltpu.SemaphoreType.DMA((32,)), pltpu.VMEM((TOK, D), F32),
+         pltpu.VMEM((TOK, D), F32), pltpu.VMEM((TOK, 128), F32)],
+        16 * 2 * TOK * D * D, 16 * 13 * MIB, 28,
     )
 
 
@@ -448,7 +469,7 @@
         + [pl.BlockSpec(tables[k].shape, whole) for k in names],
         outs,
         [pl.BlockSpec((TOK, CB), own)] * 2 + [half_spec, half_spec, pl.BlockSpec((32, CB), own)],
-        [pltpu.VMEM((D, CB), BF16)], 2 * TOK * D * width * 2, 22 * MIB * count // NB, 56, grid=(count,),
+        [pltpu.VMEM((D, CB), BF16)], 2 * TOK * D * width * 2 * 16, 22 * MIB * count // NB * 16, 22, grid=(count,),
     )
 
 
@@ -459,7 +480,7 @@
         [SMEM, SMEM] + [ANY] * NP + [VMEM] * 4 + [ANY] * 3 + [VMEM] * 5,
         [shaped((1, D), F32), shaped((16, CH), F32)], [VMEM] * 2,
         [pltpu.VMEM((D, 2 * D), BF16), pltpu.SemaphoreType.DMA((32,)), pltpu.VMEM((TOK, D), F32), pltpu.VMEM((TOK, D), BF16)],
-        2 * TOK * D * 2 * D, 20 * MIB, 56,
+        16 * 2 * TOK * D * 2 * D, 16 * 20 * MIB, 36,
     )
 
 
@@ -467,10 +488,10 @@
     return call(
         mixed_kernel, "mixed",
         (offsets, frames_of, *pieces, before, swished, embedded),
-        [SMEM, SMEM] + [ANY] * (NP + 1) + [VMEM] * 2,
+        [SMEM, SMEM] + [ANY] * (ND + 1) + [VMEM] * 2,
         shaped((TOK, D), BF16), VMEM,
         [pltpu.VMEM((D, D), BF16), pltpu.SemaphoreType.DMA((32,))],
-        2 * TOK * D * D, 10 * MIB, 56,
+        2 * TOK * D * D, 10 * MIB, 18,
     )
 
 
@@ -481,7 +502,7 @@
     return call(
         chip_sum_kernel, "chip_sum", operands, [spec(value) for value in operands],
         [shaped((4, ROWS, width), BF16)] * 4, [pl.BlockSpec((1, ROWS, width), lambda m: (m, 0, 0))] * 4,
-        [], 16 * ROWS * width, 14 * MIB, 48, grid=(4,),
+        [], 16 * ROWS * width, 14 * MIB, 18, grid=(4,),
     )
 
 
@@ -565,6 +586,15 @@
     return own + [send(piece + after, other_core()) for piece in own]
 
 
+def gather_direct(near):
+    return [near] + [send(near, along_second(r)) for r in (1, 2, 3)]
+
+
+def with_other(own, after):
+    return own + [send(piece + after if i else piece, other_core()) for i, piece in enumerate(own)]
+
+
+DIRECT = tuple(tuple((r, j) for j in range(4)) for r in range(4))
 PIECES = (
     ((0, 0), (0, 1), (0, 2), (0, 3)),
     ((1, 0), (1, 1)),
@@ -573,6 +603,7 @@
     ((1, 2), (1, 3), (2, 2), (2, 3)),
 )
 NP = 2 * len(PIECES)
+ND = 2 * len(DIRECT)
 
 
 def total_of(parts):
@@ -591,8 +622,9 @@
     return [groups[0]] + [send(groups[r], along_first(r)) for r in (1, 2, 3)]
 
 
-def scatter_rest(near):
-    close = total_of([near[0]] + [send(near[r], along_second(r)) for r in (1, 2, 3)]).astype(BF16)
+def scatter_rest(near, follow):
+    close = total_of([near[0]] + [send(near[r], along_second(r)) for r in (1, 2, 3)]) + follow
+    close = close.astype(BF16)
     wide = close.shape[1] // 2
     halves = []
     for half, order in ((close[:, :wide], (1, 3)), (close[:, wide:], (3, 1))):
@@ -632,21 +664,21 @@
     )
     gate_pieces = gather_pieces(gate_near, *gate_far, zero_of(normed))
     out_near = out_near + sum(zero_of(piece) for piece in gate_far[1])
-    out_far = gather_far(out_near)
-    out_pieces = gather_pieces(out_near, *out_far, jnp.zeros((), BF16))
-    value, gate, filtered = gate_forward(
-        offsets, utterance_frames, gate_pieces, out_far[0], normed, spectrum, tables
-    )
-    out_mine, out_other, swished = out_grad(slots, out_far[1], filtered, mix_grad, second_gain)
-    out_groups = chip_sum(out_mine, out_other)
-    filter_grad, second_grad = middle(offsets, out_pieces, out_groups[1:], filtered, mix_grad, second_gain)
-    out_groups = scatter_first(out_groups)
+    out_own = gather_direct(out_near)
+    value, gate, filtered = gate_forward(offsets, utterance_frames, gate_pieces, normed, spectrum, tables)
+    out_pieces = with_other(out_own, zero_of(filtered).astype(BF16))
+    out_mine, out_other, swished = out_grad(slots, out_own[1:], filtered, mix_grad, second_gain)
+    filter_grad, second_grad = middle(offsets, out_pieces, filtered, mix_grad, second_gain)
+    out_sums = chip_sum(out_mine, out_other)
+    out_groups = scatter_first(out_sums)
     grads, nears, convs = [], [], []
     for begin, count in ((0, 4), (4, 2)):
         value_grad, gate_grad, mine, other, conv_grad = conv_back(
-            slots, utterance_frames, out_groups[1:], value, gate, filter_grad, normed_t, spectrum, tables, begin, count
+            slots, utterance_frames, out_sums[1:], value, gate, filter_grad, normed_t, spectrum, tables, begin, count
         )
         grads.append((value_grad, gate_grad))
+        if begin:
+            other = other + sum(zero_of(group) for group in out_groups[1:])
         nears.append((mine, send(other, other_core())))
         convs.append(conv_grad[:TAPS])
     gate_groups = chip_sums(nears)
@@ -654,17 +686,17 @@
         offsets, utterance_frames, gate_pieces, [pair[k] for k in range(2) for pair in grads], gate_groups[1:], embedded,
         stem_total, mix_grad, first_gain, frames_t,
     )
-    output = mixed_out(offsets, utterance_frames, out_pieces, first_grad, swished, embedded)
     early = jnp.concatenate([jnp.concatenate(convs, axis=1), second_grad], axis=0)
     early = half_of_chip(early.reshape(2, 16, D), c)
-    follow = zero_of(output).astype(F32) + zero_of(first_grad)
+    follow = zero_of(first_grad)
     terms = [scatter_first(gate_groups), out_groups]
     near = jnp.concatenate([(total_of(term) + follow).astype(BF16) for term in terms], axis=-1)
     late = jnp.concatenate([first_grad, jnp.pad(stem_grad.reshape(1, -1), ((0, 0), (0, D - 16 * CH)))], axis=0)
     small = jnp.concatenate([early, late, jnp.zeros((6, D), F32)], axis=0)
     small = jnp.concatenate([small[:8], small[8:16], small[16:]], axis=1).astype(BF16)
     near = jnp.concatenate([near, jnp.broadcast_to(small[None], (4, *small.shape))], axis=1)
-    sums = scatter_rest(near)
+    output = mixed_out(offsets, utterance_frames, out_pieces, near, swished, embedded)
+    sums = scatter_rest(near, zero_of(output).astype(F32))
     small = sums[ROWS:]
     early, late = finish_small(
         jnp.concatenate([small[:, :D], small[:, D : 2 * D], small[:2, 2 * D :]]), 16, c

time: 262 us -> 231 us (0.88)
  waiting for transfers between devices: 47.8 us -> 31.6 us
  Pallas kernels: 103 us -> 87.1 us
  local copies, waits for them, and re-layouts: 24.1 us -> 31.5 us
  starting transfers between devices: 60.4 us -> 56.2 us
  other arithmetic: 19.6 us -> 15.5 us
  between operations: 5.65 us -> 8.68 us
    ppermute x42 -> x40, waiting for transfers between devices: 47.8 us -> 31.6 us  [send(): return lax.ppermute(values, ALL, where)]
    pallas_call x9, Pallas kernels: 103 us -> 87.1 us  [call(): pl.pallas_call(kernel, name=name, out_shape=outs, in_specs=in_specs, out_...]
    unnamed x128 -> x180, local copies, waits for them, and re-layouts: 10.1 us -> 16.8 us
    ppermute x42 -> x40, starting transfers between devices: 48.6 us -> 44.4 us  [send(): return lax.ppermute(values, ALL, where)]
    slice x6 -> x10, local copies, waits for them, and re-layouts: 5.14 us -> 6.66 us  [zero_of(): return values[(0,) * values.ndim] * 0]
  transfers between devices with their start and end apart: 43 -> 41, of which waited for: 18 -> 10; matrix products, arithmetic and copies ran while one was open for 10% -> 9% of each run, Pallas kernels for 29% -> 36%
where the time goes in v2:
time: 231 us
  Pallas kernels  87.1 us (38%)
  starting transfers between devices  56.2 us (24%)
  waiting for transfers between devices  31.6 us (14%)
  local copies, waits for them, and re-layouts  31.5 us (14%)
  other arithmetic  15.5 us (7%)
  between operations  8.68 us (4%)
    pallas_call x9, Pallas kernels, call(): pl.pallas_call(kernel, name=name, out_shape=outs, in_specs=in_specs, out_...  87.1 us
    ppermute x40, starting transfers between devices, send(): return lax.ppermute(values, ALL, where)  44.4 us
    ppermute x40, waiting for transfers between devices, send(): return lax.ppermute(values, ALL, where)  31.6 us
    unnamed x180, local copies, waits for them, and re-layouts  16.8 us
    all_to_all x1, starting transfers between devices, body(): lax.all_to_all(outgoing, ALL, split_axis=0, concat_axis=0, tiled=True)  11.8 us
    slice x10, local copies, waits for them, and re-layouts, zero_of(): return values[(0,) * values.ndim] * 0  6.66 us
    convert_element_type x2, other arithmetic, body(): (total_of(term) + follow).astype(BF16)  5.02 us
  transfers between devices with their start and end apart: 41, of which 10 were waited for; matrix products, arithmetic and copies ran while one was open for 9% of the time, Pallas kernels for 36%

profile of v2, /device:TPU:1, one launch (start us, length us, event | category | flops | bytes accessed | tf_op | source)
XLA Modules:
  0.0 230.6 jit_solution(896413280110001266)
XLA Ops:
  0.6 1.0 constant_dynamic-update-slice_fusion.1
  2.6 3.6 %collective-permute-start.2 = (bf16[48,4608]{1,0:T(8,128)(2,1)S(1)}, bf16[48,4608]{1,0:T(8,128)(2,1)S(1)}, u32[]{:S(2)}, u32[]{:S(2)}) collective-permute-start(bf16[48,4608]{1,0:T(8,128)(2,1)S(1)} %constant_dynamic-update-slice_fusion), channel_id=1, source_target_pairs={{0,6},{1,25},{2,4},{3,27},{4,2},{5,29},{6,0},{7,31},{8,14},{9,17},... | collective-permute-start | bytes 1327112 | tf_op jit(solution)/shard_map/ppermute | solution.py:540
  8.3 1.2 slice.294
  11.9 11.8 %all-to-all-start = ((bf16[128,16,128]{2,1,0:T(8,128)(2,1)}), bf16[128,16,128]{2,1,0:T(8,128)(2,1)}, u32[]{:S(2)}, u32[]{:S(2)}) async-start(bf16[128,16,128]{2,1,0:T(8,128)(2,1)} %select_add_fusion), calls=%async_computation | async-start | bytes 1048576 | tf_op jit(solution)/shard_map/all_to_all | solution.py:660
  25.2 1.5 collective-permute-start.3
  27.6 2.1 collective-permute-start.5
  31.0 7.9 %collective-permute-done.3.unused.refs_1_ = bf16[2,48,3072]{2,1,0:T(8,128)(2,1)S(1)} collective-permute-done((bf16[2,48,3072]{2,1,0:T(8,128)(2,1)S(1)}, bf16[2,48,3072]{2,1,0:T(8,128)(2,1)S(1)}, u32[]{:S(2)}, u32[]{:S(2)}) %collective-permute-start.3) | collective-permute-done | bytes 589856 | tf_op jit(solution)/shard_map/ppermute | solution.py:540
  38.9 1.1 pad_maximum_fusion.1
  40.0 2.5 %collective-permute-start.4 = (bf16[2,2,48,3072]{3,2,1,0:T(8,128)(2,1)}, bf16[2,2,48,3072]{3,2,1,0:T(8,128)(2,1)S(1)}, u32[]{:S(2)}, u32[]{:S(2)}) collective-permute-start(bf16[2,2,48,3072]{3,2,1,0:T(8,128)(2,1)} %pad_maximum_fusion.1), channel_id=1, source_target_pairs={{0,24},{1,7},{2,26},{3,5},{4,28},{5,3},{6,30},{7,1},{8,16},{9,15},... | collective-permute-start | bytes 3538952 | tf_op jit(solution)/shard_map/ppermute | solution.py:540
  42.4 1.1 pad_maximum_fusion.2
  44.0 1.4 copy-done.28
  47.1 5.8 %stem.1 = (f32[512,1536]{1,0:T(8,128)S(1)}, bf16[512,1536]{1,0:T(8,128)(2,1)S(1)}, bf16[512,1536]{1,0:T(8,128)(2,1)S(1)}, bf16[1536,512]{1,0:T(8,128)(2,1)S(1)},...) custom-call(bf16[2,48,3072]{2,1,0:T(8,128)(2,1)S(1)} %collective-permute-done.3.unused.refs_1_,, ...), custom_call_target="tpu_custom_call" | custom-call | flops 805306368 | bytes 14680064 | tf_op jit(solution)/shard_map/stem/pallas_call | solution.py:393
  53.0 1.7 copy-done.47
  63.3 1.7 collective-permute-start.7
  65.2 3.1 %collective-permute-start.8 = (bf16[4,48,1536]{2,1,0:T(8,128)(2,1)S(1)}, bf16[4,48,1536]{2,1,0:T(8,128)(2,1)S(1)}, u32[]{:S(2)}, u32[]{:S(2)}) collective-permute-start(bf16[4,48,1536]{2,1,0:T(8,128)(2,1)S(1)} %maximum_add_fusion.refs_0_), channel_id=1, source_target_pairs={{0,16},{1,5},{2,18},{3,7},{4,20},{5,1},{6,22},{7,3},{8,24},{9,13},... | collective-permute-start | bytes 1769480 | tf_op jit(solution)/shard_map/ppermute | solution.py:540
  68.7 13.8 %gate.1 = (f32[512,1536]{1,0:T(8,128)S(1)}, f32[512,1536]{1,0:T(8,128)S(1)}, f32[512,1536]{1,0:T(8,128)S(1)}) custom-call(s32[32]{0:T(128)S(1)} %pad_add_fusion.offsets, s32[4]{0:T(128)S(1)} %copy-done.27, bf16[4,48,3072]{2,1,0:T(8,128)(2,1)S(1)} %get-tuple-element.76.refs_0_, bf16[2,48,3072]{2,1,0:T(8,128)(2,1)S(1)} %collective-permute-done.3.unused.refs_1_, ...), custom_call_target="tpu_custom_call" | custom-call | flops 4831838208 | bytes 23068672 | tf_op jit(solution)/shard_map/gate/pallas_call | solution.py:393
  82.6 1.7 copy-done.51
  84.2 1.7 copy-done.53
  88.4 6.1 %out_grad.1 = (bf16[16,48,1536]{2,1,0:T(8,128)(2,1)S(1)}, bf16[16,48,1536]{2,1,0:T(8,128)(2,1)S(1)}, bf16[512,1536]{1,0:T(8,128)(2,1)S(1)}) custom-call(s32[33]{0:T(128)S(1)} %pad_add_fusion.1.slots, bf16[4,48,1536]{2,1,0:T(8,128)(2,1)S(1)} %collective-permute-done.7.unused_1.refs_1_, bf16[4,48,1536]{2,1,0:T(8,128)(2,1)S(1)} %collective-permute-done.8.unused_2.refs_2_, ...), custom_call_target="tpu_custom_call" | custom-call | flops 38654705664 | bytes 184549376 | tf_op jit(solution)/shard_map/out_grad/pallas_call | solution.py:393
  94.6 1.1 copy-done.13
  96.1 14.3 %middle.1 = (f32[512,1536]{1,0:T(8,128)S(1)}, f32[1,1536]{1,0:T(1,128)S(1)}) custom-call(s32[32]{0:T(128)S(1)} %pad_add_fusion.offsets, bf16[4,48,1536]{2,1,0:T(8,128)(2,1)S(1)} %maximum_add_fusion.refs_0_, bf16[4,48,1536]{2,1,0:T(8,128)(2,1)S(1)} %collective-permute-done.7.unused_1.refs_1_, ...), custom_call_target="tpu_custom_call" | custom-call | flops 38654705664 | bytes 218103808 | tf_op jit(solution)/shard_map/middle/pallas_call | solution.py:393
  112.5 1.9 collective-permute-start.22
  114.4 1.3 collective-permute-start.23
  115.8 1.9 copy-done.54
  117.7 9.8 %conv_back.2 = (bf16[512,1024]{1,0:T(8,128)(2,1)S(1)}, bf16[512,1024]{1,0:T(8,128)(2,1)S(1)}, bf16[16,48,2048]{2,1,0:T(8,128)(2,1)S(1)}, bf16[16,48,2048]{2,1,0:T(8,128)(2,1)S(1)}, f32[32,1024]{1,0:T(8,128)S(1)}) custom-call(s32[33]{0:T(128)S(1)} %pad_add_fusion.1.slots, s32[4]{0:T(128)S(1)} %copy-done.27, ...), custom_call_target="tpu_custom_call" | custom-call | flops 51539607552 | bytes 246065824 | tf_op jit(solution)/shard_map/conv_back/pallas_call | solution.py:393
  127.5 1.6 collective-permute-start.20
  129.1 5.1 %conv_back.3 = (bf16[512,512]{1,0:T(8,128)(2,1)S(1)}, bf16[512,512]{1,0:T(8,128)(2,1)S(1)}, bf16[16,48,1024]{2,1,0:T(8,128)(2,1)S(1)}, bf16[16,48,1024]{2,1,0:T(8,128)(2,1)S(1)}, f32[32,512]{1,0:T(8,128)S(1)}) custom-call(s32[33]{0:T(128)S(1)} %pad_add_fusion.1.slots, s32[4]{0:T(128)S(1)} %copy-done.27, bf16[4,48,1536]{2,1,0:T(8,128)(2,1)S(1)} %get-tuple-element.71.unused_1, ...), custom_call_target="tpu_custom_call" | custom-call | flops 25769803776 | bytes 123032912 | tf_op jit(solution)/shard_map/conv_back/pallas_call | solution.py:393
  138.8 2.9 %collective-permute-done.28 = f32[16,1536]{1,0:T(8,128)S(1)} collective-permute-done((f32[16,1536]{1,0:T(8,128)S(1)}, f32[16,1536]{1,0:T(8,128)S(1)}, u32[]{:S(2)}, u32[]{:S(2)}) %collective-permute-start.28) | collective-permute-done | bytes 98336 | tf_op jit(solution)/shard_map/ppermute | solution.py:540
  142.4 3.0 %chip_sum.1 = (bf16[4,48,3072]{2,1,0:T(8,128)(2,1)S(1)}, bf16[4,48,3072]{2,1,0:T(8,128)(2,1)}, bf16[4,48,3072]{2,1,0:T(8,128)(2,1)}, bf16[4,48,3072]{2,1,0:T(8,128)(2,1)}) custom-call(bf16[4,4,48,2048]{3,2,1,0:T(8,128)(2,1)S(1)} %bitcast.57, bf16[4,4,48,2048]{3,2,1,0:T(8,128)(2,1)S(1)} %bitcast.58, bf16[4,4,48,1024]{3,2,1,0:T(8,128)(2,1)S(1)} %bitcast.61, ...), custom_call_target="tpu_custom_call" | custom-call | flops 2359296 | bytes 14680064 | tf_op jit(solution)/shard_map/chip_sum/pallas_call | solution.py:393
  145.5 1.1 collective-permute-start.27
  147.6 1.1 collective-permute-start.25
  148.8 1.1 copy-done.38
  149.9 16.9 %stem_back.1 = (f32[1,1536]{1,0:T(1,128)S(1)}, f32[16,48]{1,0:T(8,128)S(1)}) custom-call(s32[32]{0:T(128)S(1)} %pad_add_fusion.offsets, s32[4]{0:T(128)S(1)} %copy-done.27, bf16[4,48,3072]{2,1,0:T(8,128)(2,1)S(1)} %copy-done.16, bf16[2,48,3072]{2,1,0:T(8,128)(2,1)S(1)} %collective-permute-done.3.unused.refs_1_, ...), custom_call_target="tpu_custom_call" | custom-call | flops 77309411328 | bytes 335544320 | tf_op jit(solution)/shard_map/stem_back/pallas_call | solution.py:393
  168.9 2.3 add_convert_fusion.1
  171.2 3.8 %collective-permute-done.27 = bf16[4,48,3072]{2,1,0:T(8,128)(2,1)} collective-permute-done((bf16[4,48,3072]{2,1,0:T(8,128)(2,1)}, bf16[4,48,3072]{2,1,0:T(8,128)(2,1)}, u32[]{:S(2)}, u32[]{:S(2)}) %collective-permute-start.27) | collective-permute-done | bytes 1179680 | tf_op jit(solution)/shard_map/ppermute | solution.py:540
  175.6 2.7 %add_convert_fusion = bf16[4,48,3072]{2,1,0:T(8,128)(2,1)S(1)} fusion(bf16[4,48,3072]{2,1,0:T(8,128)(2,1)} %collective-permute-done.27, bf16[4,48,3072]{2,1,0:T(8,128)(2,1)} %collective-permute-done.26, bf16[4,48,3072]{2,1,0:T(8,128)(2,1)} %collective-permute-done.25, bf16[4,48,3072]{2,1,0:T(8,128)(2,1)S(1)} %copy-done.18, f32[]{:T(128)} %bitcast.28), kind=kLoop, calls=%fused_computation.1 | loop fusion | flops 5308416 | bytes 5898244 | tf_op jit(solution)/shard_map/convert_element_type | solution.py:693
  178.6 1.2 slice_bitcast_fusion.2
  179.8 2.9 %collective-permute-start.31 = (bf16[56,4608]{1,0:T(8,128)(2,1)}, bf16[56,4608]{1,0:T(8,128)(2,1)}, u32[]{:S(2)}, u32[]{:S(2)}) collective-permute-start(bf16[56,4608]{1,0:T(8,128)(2,1)} %get-tuple-element.73), channel_id=1, source_target_pairs={{0,24},{1,7},{2,26},{3,5},{4,28},{5,3},{6,30},{7,1},{8,16},{9,15},... | collective-permute-start | bytes 1548296 | tf_op jit(solution)/shard_map/ppermute | solution.py:540
  183.4 12.3 %mixed.1 = bf16[512,1536]{1,0:T(8,128)(2,1)} custom-call(s32[32]{0:T(128)S(1)} %pad_add_fusion.offsets, s32[4]{0:T(128)S(1)} %copy-done.27, bf16[4,48,1536]{2,1,0:T(8,128)(2,1)S(1)} %copy-done.3, bf16[4,48,1536]{2,1,0:T(8,128)(2,1)S(1)} %copy-done.5, bf16[4,48,1536]{2,1,0:T(8,128)(2,1)S(1)} %copy-done.7, bf16[4,48,1536]{2,1,0:T(8,128)(2,1)S(1)} %copy-done.9, ...), custom_call_target="tpu_custom_call" | custom-call | flops 2415919104 | bytes 10485760 | tf_op jit(solution)/shard_map/mixed/pallas_call | solution.py:393
  195.7 1.2 slice.308
  197.6 1.7 fusion.3
  199.3 1.2 collective-permute-start.34
  200.6 5.9 %collective-permute-done.34 = bf16[56,2304]{1,0:T(8,128)(2,1)S(1)} collective-permute-done((bf16[56,2304]{1,0:T(8,128)(2,1)S(1)}, bf16[56,2304]{1,0:T(8,128)(2,1)S(1)}, u32[]{:S(2)}, u32[]{:S(2)}) %collective-permute-start.34) | collective-permute-done | bytes 258080 | tf_op jit(solution)/shard_map/ppermute | solution.py:540
  206.6 1.3 collective-permute-start.33
  207.9 5.2 %collective-permute-done.33 = bf16[56,2304]{1,0:T(8,128)(2,1)S(1)} collective-permute-done((bf16[56,2304]{1,0:T(8,128)(2,1)S(1)}, bf16[56,2304]{1,0:T(8,128)(2,1)S(1)}, u32[]{:S(2)}, u32[]{:S(2)}) %collective-permute-start.33) | collective-permute-done | bytes 258080 | tf_op jit(solution)/shard_map/ppermute | solution.py:540
  215.2 1.4 collective-permute-start.36
  216.7 3.4 %collective-permute-done.38 = f32[18,1536]{1,0:T(8,128)S(1)} collective-permute-done((f32[18,1536]{1,0:T(8,128)S(1)}, f32[18,1536]{1,0:T(8,128)S(1)}, u32[]{:S(2)}, u32[]{:S(2)}) %collective-permute-start.38) | collective-permute-done | bytes 110624 | tf_op jit(solution)/shard_map/ppermute | solution.py:540
  220.7 6.8 %collective-permute-start.39 = (f32[18,1536]{1,0:T(8,128)S(1)}, f32[18,1536]{1,0:T(8,128)S(1)}, u32[]{:S(2)}, u32[]{:S(2)}) collective-permute-start(f32[18,1536]{1,0:T(8,128)S(1)} %add_add_fusion), channel_id=1, source_target_pairs={{0,1},{1,0},{2,3},{3,2},{4,5},{5,4},{6,7},{7,6},{8,9},{9,8},{10,11... | collective-permute-start | bytes 331784 | tf_op jit(solution)/shard_map/ppermute | solution.py:540
  (295 shorter events, 34.5 us)
Async XLA Ops:
  2.6 24.1 %collective-permute-start.2 = (bf16[48,4608]{1,0:T(8,128)(2,1)S(1)}, bf16[48,4608]{1,0:T(8,128)(2,1)S(1)}, u32[]{:S(2)}, u32[]{:S(2)}) collective-permute-start(bf16[48,4608]{1,0:T(8,128)(2,1)S(1)} %constant_dynamic-update-slice_fusion), channel_id=1, source_target_pairs={{0,6},{1,25},{2,4},{3,27},{4,2},{5,29},{6,0},{7,31},{8,14},{9,17},... | collective-permute-start | bytes 1327112 | tf_op jit(solution)/shard_map/ppermute | solution.py:540
  6.3 20.5 %collective-permute-start.1 = (bf16[48,4608]{1,0:T(8,128)(2,1)S(1)}, bf16[48,4608]{1,0:T(8,128)(2,1)S(1)}, u32[]{:S(2)}, u32[]{:S(2)}) collective-permute-start(bf16[48,4608]{1,0:T(8,128)(2,1)S(1)} %constant_dynamic-update-slice_fusion), channel_id=1, source_target_pairs={{0,4},{1,17},{2,6},{3,19},{4,0},{5,21},{6,2},{7,23},{8,12},{9,25},... | collective-permute-start | bytes 1327112 | tf_op jit(solution)/shard_map/ppermute | solution.py:540
  6.6 17.7 %collective-permute-start = (bf16[48,4608]{1,0:T(8,128)(2,1)S(1)}, bf16[48,4608]{1,0:T(8,128)(2,1)S(1)}, u32[]{:S(2)}, u32[]{:S(2)}) collective-permute-start(bf16[48,4608]{1,0:T(8,128)(2,1)S(1)} %constant_dynamic-update-slice_fusion), channel_id=1, source_target_pairs={{0,2},{1,9},{2,0},{3,11},{4,6},{5,13},{6,4},{7,15},{8,10},{9,1},{1... | collective-permute-start | bytes 1327112 | tf_op jit(solution)/shard_map/ppermute | solution.py:540
  11.9 32.1 %all-to-all-start = ((bf16[128,16,128]{2,1,0:T(8,128)(2,1)}), bf16[128,16,128]{2,1,0:T(8,128)(2,1)}, u32[]{:S(2)}, u32[]{:S(2)}) async-start(bf16[128,16,128]{2,1,0:T(8,128)(2,1)} %select_add_fusion), calls=%async_computation | async-start | bytes 1048576 | tf_op jit(solution)/shard_map/all_to_all | solution.py:660
  25.2 13.6 %collective-permute-start.3 = (bf16[2,48,3072]{2,1,0:T(8,128)(2,1)S(1)}, bf16[2,48,3072]{2,1,0:T(8,128)(2,1)S(1)}, u32[]{:S(2)}, u32[]{:S(2)}) collective-permute-start(bf16[2,48,3072]{2,1,0:T(8,128)(2,1)S(1)} %get-tuple-element.80), channel_id=1, source_target_pairs={{0,8},{1,3},{2,10},{3,1},{4,12},{5,7},{6,14},{7,5},{8,0},{9,11},{1... | collective-permute-start | bytes 1769480 | tf_op jit(solution)/shard_map/ppermute | solution.py:540
  27.6 14.9 %collective-permute-start.5 = (bf16[2,48,3072]{2,1,0:T(8,128)(2,1)S(1)}, bf16[2,48,3072]{2,1,0:T(8,128)(2,1)S(1)}, u32[]{:S(2)}, u32[]{:S(2)}) collective-permute-start(bf16[2,48,3072]{2,1,0:T(8,128)(2,1)S(1)} %get-tuple-element.78), channel_id=1, source_target_pairs={{0,24},{1,7},{2,26},{3,5},{4,28},{5,3},{6,30},{7,1},{8,16},{9,15},... | collective-permute-start | bytes 1769480 | tf_op jit(solution)/shard_map/ppermute | solution.py:540
  40.0 17.7 %collective-permute-start.4 = (bf16[2,2,48,3072]{3,2,1,0:T(8,128)(2,1)}, bf16[2,2,48,3072]{3,2,1,0:T(8,128)(2,1)S(1)}, u32[]{:S(2)}, u32[]{:S(2)}) collective-permute-start(bf16[2,2,48,3072]{3,2,1,0:T(8,128)(2,1)} %pad_maximum_fusion.1), channel_id=1, source_target_pairs={{0,24},{1,7},{2,26},{3,5},{4,28},{5,3},{6,30},{7,1},{8,16},{9,15},... | collective-permute-start | bytes 3538952 | tf_op jit(solution)/shard_map/ppermute | solution.py:540
  43.6 15.3 %collective-permute-start.6 = (bf16[2,2,48,3072]{3,2,1,0:T(8,128)(2,1)}, bf16[2,2,48,3072]{3,2,1,0:T(8,128)(2,1)S(1)}, u32[]{:S(2)}, u32[]{:S(2)}) collective-permute-start(bf16[2,2,48,3072]{3,2,1,0:T(8,128)(2,1)} %pad_maximum_fusion.2), channel_id=1, source_target_pairs={{0,8},{1,3},{2,10},{3,1},{4,12},{5,7},{6,14},{7,5},{8,0},{9,11},{1... | collective-permute-start | bytes 3538952 | tf_op jit(solution)/shard_map/ppermute | solution.py:540
  55.4 40.6 %copy-start.48 = (bf16[512,1536]{1,0:T(8,128)(2,1)}, bf16[512,1536]{1,0:T(8,128)(2,1)S(1)}, u32[]{:S(2)}) copy-start(bf16[512,1536]{1,0:T(8,128)(2,1)S(1)} %get-tuple-element.41.mix_grad.refs_9_.refs_19_) | copy-start | bytes 4718596
  55.4 93.3 %copy-start.11 = (bf16[512,1536]{1,0:T(8,128)(2,1)}, bf16[512,1536]{1,0:T(8,128)(2,1)S(1)}, u32[]{:S(2)}) copy-start(bf16[512,1536]{1,0:T(8,128)(2,1)S(1)} %get-tuple-element.60.refs_17_.refs_10_) | copy-start | bytes 4718596
  56.9 11.4 %collective-permute-start.11 = (bf16[4,48,3072]{2,1,0:T(8,128)(2,1)S(1)}, bf16[4,48,3072]{2,1,0:T(8,128)(2,1)S(1)}, u32[]{:S(2)}, u32[]{:S(2)}) collective-permute-start(bf16[4,48,3072]{2,1,0:T(8,128)(2,1)S(1)} %get-tuple-element.75), channel_id=1, source_target_pairs={{0,1},{1,0},{2,3},{3,2},{4,5},{5,4},{6,7},{7,6},{8,9},{9,8},{10,11... | collective-permute-start | bytes 3538952 | tf_op jit(solution)/shard_map/ppermute | solution.py:540
  57.1 6.2 %collective-permute-start.12 = (bf16[2,48,3072]{2,1,0:T(8,128)(2,1)S(1)}, bf16[2,48,3072]{2,1,0:T(8,128)(2,1)S(1)}, u32[]{:S(2)}, u32[]{:S(2)}) collective-permute-start(bf16[2,48,3072]{2,1,0:T(8,128)(2,1)S(1)} %broadcast_add_fusion.8), channel_id=1, source_target_pairs={{0,1},{1,0},{2,3},{3,2},{4,5},{5,4},{6,7},{7,6},{8,9},{9,8},{10,11... | collective-permute-start | bytes 1769480 | tf_op jit(solution)/shard_map/ppermute | solution.py:540
  57.8 10.6 %collective-permute-start.14 = (bf16[4,48,3072]{2,1,0:T(8,128)(2,1)S(1)}, bf16[4,48,3072]{2,1,0:T(8,128)(2,1)S(1)}, u32[]{:S(2)}, u32[]{:S(2)}) collective-permute-start(bf16[4,48,3072]{2,1,0:T(8,128)(2,1)S(1)} %broadcast_add_fusion.2), channel_id=1, source_target_pairs={{0,1},{1,0},{2,3},{3,2},{4,5},{5,4},{6,7},{7,6},{8,9},{9,8},{10,11... | collective-permute-start | bytes 3538952 | tf_op jit(solution)/shard_map/ppermute | solution.py:540
  59.2 9.6 %collective-permute-start.15 = (bf16[4,48,3072]{2,1,0:T(8,128)(2,1)S(1)}, bf16[4,48,3072]{2,1,0:T(8,128)(2,1)S(1)}, u32[]{:S(2)}, u32[]{:S(2)}) collective-permute-start(bf16[4,48,3072]{2,1,0:T(8,128)(2,1)S(1)} %broadcast_add_fusion.1), channel_id=1, source_target_pairs={{0,1},{1,0},{2,3},{3,2},{4,5},{5,4},{6,7},{7,6},{8,9},{9,8},{10,11... | collective-permute-start | bytes 3538952 | tf_op jit(solution)/shard_map/ppermute | solution.py:540
  59.7 5.5 %collective-permute-start.13 = (bf16[2,48,3072]{2,1,0:T(8,128)(2,1)S(1)}, bf16[2,48,3072]{2,1,0:T(8,128)(2,1)S(1)}, u32[]{:S(2)}, u32[]{:S(2)}) collective-permute-start(bf16[2,48,3072]{2,1,0:T(8,128)(2,1)S(1)} %broadcast_add_fusion.7), channel_id=1, source_target_pairs={{0,1},{1,0},{2,3},{3,2},{4,5},{5,4},{6,7},{7,6},{8,9},{9,8},{10,11... | collective-permute-start | bytes 1769480 | tf_op jit(solution)/shard_map/ppermute | solution.py:540
  63.2 32.8 %copy-start.2 = (bf16[4,48,1536]{2,1,0:T(8,128)(2,1)}, bf16[4,48,1536]{2,1,0:T(8,128)(2,1)S(1)}, u32[]{:S(2)}) copy-start(bf16[4,48,1536]{2,1,0:T(8,128)(2,1)S(1)} %maximum_add_fusion.refs_0_) | copy-start | bytes 1769476
  63.3 19.2 %copy-start.35 = (bf16[2,48,3072]{2,1,0:T(8,128)(2,1)}, bf16[2,48,3072]{2,1,0:T(8,128)(2,1)S(1)}, u32[]{:S(2)}) copy-start(bf16[2,48,3072]{2,1,0:T(8,128)(2,1)S(1)} %collective-permute-done.12.refs_6_) | copy-start | bytes 1769476
  63.3 23.8 %collective-permute-start.7 = (bf16[4,48,1536]{2,1,0:T(8,128)(2,1)S(1)}, bf16[4,48,1536]{2,1,0:T(8,128)(2,1)S(1)}, u32[]{:S(2)}, u32[]{:S(2)}) collective-permute-start(bf16[4,48,1536]{2,1,0:T(8,128)(2,1)S(1)} %maximum_add_fusion.refs_0_), channel_id=1, source_target_pairs={{0,8},{1,3},{2,10},{3,1},{4,12},{5,7},{6,14},{7,5},{8,0},{9,11},{1... | collective-permute-start | bytes 1769480 | tf_op jit(solution)/shard_map/ppermute | solution.py:540
  65.2 17.3 %copy-start.37 = (bf16[2,48,3072]{2,1,0:T(8,128)(2,1)}, bf16[2,48,3072]{2,1,0:T(8,128)(2,1)S(1)}, u32[]{:S(2)}) copy-start(bf16[2,48,3072]{2,1,0:T(8,128)(2,1)S(1)} %collective-permute-done.13.refs_7_) | copy-start | bytes 1769476
  65.2 22.5 %collective-permute-start.8 = (bf16[4,48,1536]{2,1,0:T(8,128)(2,1)S(1)}, bf16[4,48,1536]{2,1,0:T(8,128)(2,1)S(1)}, u32[]{:S(2)}, u32[]{:S(2)}) collective-permute-start(bf16[4,48,1536]{2,1,0:T(8,128)(2,1)S(1)} %maximum_add_fusion.refs_0_), channel_id=1, source_target_pairs={{0,16},{1,5},{2,18},{3,7},{4,20},{5,1},{6,22},{7,3},{8,24},{9,13},... | collective-permute-start | bytes 1769480 | tf_op jit(solution)/shard_map/ppermute | solution.py:540
  68.3 19.8 %collective-permute-start.9 = (bf16[4,48,1536]{2,1,0:T(8,128)(2,1)S(1)}, bf16[4,48,1536]{2,1,0:T(8,128)(2,1)S(1)}, u32[]{:S(2)}, u32[]{:S(2)}) collective-permute-start(bf16[4,48,1536]{2,1,0:T(8,128)(2,1)S(1)} %maximum_add_fusion.refs_0_), channel_id=1, source_target_pairs={{0,24},{1,7},{2,26},{3,5},{4,28},{5,3},{6,30},{7,1},{8,16},{9,15},... | collective-permute-start | bytes 1769480 | tf_op jit(solution)/shard_map/ppermute | solution.py:540
  68.4 27.6 %collective-permute-start.10 = (bf16[4,48,1536]{2,1,0:T(8,128)(2,1)S(1)}, bf16[4,48,1536]{2,1,0:T(8,128)(2,1)S(1)}, u32[]{:S(2)}, u32[]{:S(2)}) collective-permute-start(bf16[4,48,1536]{2,1,0:T(8,128)(2,1)S(1)} %maximum_add_fusion.refs_0_), channel_id=1, source_target_pairs={{0,1},{1,0},{2,3},{3,2},{4,5},{5,4},{6,7},{7,6},{8,9},{9,8},{10,11... | collective-permute-start | bytes 1769480 | tf_op jit(solution)/shard_map/ppermute | solution.py:540
  87.2 8.8 %collective-permute-start.16 = (bf16[4,48,1536]{2,1,0:T(8,128)(2,1)S(1)}, bf16[4,48,1536]{2,1,0:T(8,128)(2,1)S(1)}, u32[]{:S(2)}, u32[]{:S(2)}) collective-permute-start(bf16[4,48,1536]{2,1,0:T(8,128)(2,1)S(1)} %broadcast_add_fusion.6), channel_id=1, source_target_pairs={{0,1},{1,0},{2,3},{3,2},{4,5},{5,4},{6,7},{7,6},{8,9},{9,8},{10,11... | collective-permute-start | bytes 1769480 | tf_op jit(solution)/shard_map/ppermute | solution.py:540
  87.7 8.3 %collective-permute-start.17 = (bf16[4,48,1536]{2,1,0:T(8,128)(2,1)S(1)}, bf16[4,48,1536]{2,1,0:T(8,128)(2,1)S(1)}, u32[]{:S(2)}, u32[]{:S(2)}) collective-permute-start(bf16[4,48,1536]{2,1,0:T(8,128)(2,1)S(1)} %broadcast_add_fusion.5), channel_id=1, source_target_pairs={{0,1},{1,0},{2,3},{3,2},{4,5},{5,4},{6,7},{7,6},{8,9},{9,8},{10,11... | collective-permute-start | bytes 1769480 | tf_op jit(solution)/shard_map/ppermute | solution.py:540
  88.1 7.9 %collective-permute-start.18 = (bf16[4,48,1536]{2,1,0:T(8,128)(2,1)S(1)}, bf16[4,48,1536]{2,1,0:T(8,128)(2,1)S(1)}, u32[]{:S(2)}, u32[]{:S(2)}) collective-permute-start(bf16[4,48,1536]{2,1,0:T(8,128)(2,1)S(1)} %broadcast_add_fusion.4), channel_id=1, source_target_pairs={{0,1},{1,0},{2,3},{3,2},{4,5},{5,4},{6,7},{7,6},{8,9},{9,8},{10,11... | collective-permute-start | bytes 1769480 | tf_op jit(solution)/shard_map/ppermute | solution.py:540
  95.7 14.7 %copy-start.10 = (bf16[16,48,1536]{2,1,0:T(8,128)(2,1)}, bf16[16,48,1536]{2,1,0:T(8,128)(2,1)S(1)}, u32[]{:S(2)}) copy-start(bf16[16,48,1536]{2,1,0:T(8,128)(2,1)S(1)} %get-tuple-element.42) | copy-start | bytes 7077892
  95.7 14.7 %collective-permute-start.19 = (bf16[16,48,1536]{2,1,0:T(8,128)(2,1)S(1)}, bf16[16,48,1536]{2,1,0:T(8,128)(2,1)S(1)}, u32[]{:S(2)}, u32[]{:S(2)}) collective-permute-start(bf16[16,48,1536]{2,1,0:T(8,128)(2,1)S(1)} %get-tuple-element.43), channel_id=1, source_target_pairs={{0,1},{1,0},{2,3},{3,2},{4,5},{5,4},{6,7},{7,6},{8,9},{9,8},{10,11... | collective-permute-start | bytes 7077896 | tf_op jit(solution)/shard_map/ppermute | solution.py:540
  111.9 22.3 %collective-permute-start.21 = (bf16[4,48,1536]{2,1,0:T(8,128)(2,1)S(1)}, bf16[4,48,1536]{2,1,0:T(8,128)(2,1)S(1)}, u32[]{:S(2)}, u32[]{:S(2)}) collective-permute-start(bf16[4,48,1536]{2,1,0:T(8,128)(2,1)S(1)} %get-tuple-element.71.unused_1), channel_id=1, source_target_pairs={{0,2},{1,9},{2,0},{3,11},{4,6},{5,13},{6,4},{7,15},{8,10},{9,1},{1... | collective-permute-start | bytes 1769480 | tf_op jit(solution)/shard_map/ppermute | solution.py:540
  112.5 22.3 %collective-permute-start.22 = (bf16[4,48,1536]{2,1,0:T(8,128)(2,1)S(1)}, bf16[4,48,1536]{2,1,0:T(8,128)(2,1)S(1)}, u32[]{:S(2)}, u32[]{:S(2)}) collective-permute-start(bf16[4,48,1536]{2,1,0:T(8,128)(2,1)S(1)} %get-tuple-element.70.unused_2), channel_id=1, source_target_pairs={{0,4},{1,17},{2,6},{3,19},{4,0},{5,21},{6,2},{7,23},{8,12},{9,25},... | collective-permute-start | bytes 1769480 | tf_op jit(solution)/shard_map/ppermute | solution.py:540
  114.4 22.2 %collective-permute-start.23 = (bf16[4,48,1536]{2,1,0:T(8,128)(2,1)S(1)}, bf16[4,48,1536]{2,1,0:T(8,128)(2,1)S(1)}, u32[]{:S(2)}, u32[]{:S(2)}) collective-permute-start(bf16[4,48,1536]{2,1,0:T(8,128)(2,1)S(1)} %get-tuple-element.69.unused_3), channel_id=1, source_target_pairs={{0,6},{1,25},{2,4},{3,27},{4,2},{5,29},{6,0},{7,31},{8,14},{9,17},... | collective-permute-start | bytes 1769480 | tf_op jit(solution)/shard_map/ppermute | solution.py:540
  127.5 14.9 %collective-permute-start.20 = (bf16[16,48,2048]{2,1,0:T(8,128)(2,1)S(1)}, bf16[16,48,2048]{2,1,0:T(8,128)(2,1)S(1)}, u32[]{:S(2)}, u32[]{:S(2)}) collective-permute-start(bf16[16,48,2048]{2,1,0:T(8,128)(2,1)S(1)} %get-tuple-element.49), channel_id=1, source_target_pairs={{0,1},{1,0},{2,3},{3,2},{4,5},{5,4},{6,7},{7,6},{8,9},{9,8},{10,11... | collective-permute-start | bytes 9437192 | tf_op jit(solution)/shard_map/ppermute | solution.py:540
  138.1 4.3 %collective-permute-start.24 = (bf16[16,48,1024]{2,1,0:T(8,128)(2,1)S(1)}, bf16[16,48,1024]{2,1,0:T(8,128)(2,1)S(1)}, u32[]{:S(2)}, u32[]{:S(2)}) collective-permute-start(bf16[16,48,1024]{2,1,0:T(8,128)(2,1)S(1)} %broadcast_add_fusion), channel_id=1, source_target_pairs={{0,1},{1,0},{2,3},{3,2},{4,5},{5,4},{6,7},{7,6},{8,9},{9,8},{10,11... | collective-permute-start | bytes 4718600 | tf_op jit(solution)/shard_map/ppermute | solution.py:540
  138.2 3.5 %collective-permute-start.28 = (f32[16,1536]{1,0:T(8,128)S(1)}, f32[16,1536]{1,0:T(8,128)S(1)}, u32[]{:S(2)}, u32[]{:S(2)}) collective-permute-start(f32[16,1536]{1,0:T(8,128)S(1)} %broadcast_select_fusion), channel_id=1, source_target_pairs={{0,1},{1,0},{2,3},{3,2},{4,5},{5,4},{6,7},{7,6},{8,9},{9,8},{10,11... | collective-permute-start | bytes 294920 | tf_op jit(solution)/shard_map/ppermute | solution.py:540
  145.5 21.3 %copy-start.17 = (bf16[4,48,3072]{2,1,0:T(8,128)(2,1)}, bf16[4,48,3072]{2,1,0:T(8,128)(2,1)S(1)}, u32[]{:S(2)}) copy-start(bf16[4,48,3072]{2,1,0:T(8,128)(2,1)S(1)} %get-tuple-element.52) | copy-start | bytes 3538948
  145.5 29.5 %collective-permute-start.27 = (bf16[4,48,3072]{2,1,0:T(8,128)(2,1)}, bf16[4,48,3072]{2,1,0:T(8,128)(2,1)}, u32[]{:S(2)}, u32[]{:S(2)}) collective-permute-start(bf16[4,48,3072]{2,1,0:T(8,128)(2,1)} %get-tuple-element.55.refs_16_), channel_id=1, source_target_pairs={{0,6},{1,25},{2,4},{3,27},{4,2},{5,29},{6,0},{7,31},{8,14},{9,17},... | collective-permute-start | bytes 3538952 | tf_op jit(solution)/shard_map/ppermute | solution.py:540
  146.6 28.4 %collective-permute-start.26 = (bf16[4,48,3072]{2,1,0:T(8,128)(2,1)}, bf16[4,48,3072]{2,1,0:T(8,128)(2,1)}, u32[]{:S(2)}, u32[]{:S(2)}) collective-permute-start(bf16[4,48,3072]{2,1,0:T(8,128)(2,1)} %get-tuple-element.54.refs_15_), channel_id=1, source_target_pairs={{0,4},{1,17},{2,6},{3,19},{4,0},{5,21},{6,2},{7,23},{8,12},{9,25},... | collective-permute-start | bytes 3538952 | tf_op jit(solution)/shard_map/ppermute | solution.py:540
  147.6 28.0 %collective-permute-start.25 = (bf16[4,48,3072]{2,1,0:T(8,128)(2,1)}, bf16[4,48,3072]{2,1,0:T(8,128)(2,1)}, u32[]{:S(2)}, u32[]{:S(2)}) collective-permute-start(bf16[4,48,3072]{2,1,0:T(8,128)(2,1)} %get-tuple-element.53.refs_14_), channel_id=1, source_target_pairs={{0,2},{1,9},{2,0},{3,11},{4,6},{5,13},{6,4},{7,15},{8,10},{9,1},{1... | collective-permute-start | bytes 3538952 | tf_op jit(solution)/shard_map/ppermute | solution.py:540
  179.8 17.8 %collective-permute-start.31 = (bf16[56,4608]{1,0:T(8,128)(2,1)}, bf16[56,4608]{1,0:T(8,128)(2,1)}, u32[]{:S(2)}, u32[]{:S(2)}) collective-permute-start(bf16[56,4608]{1,0:T(8,128)(2,1)} %get-tuple-element.73), channel_id=1, source_target_pairs={{0,24},{1,7},{2,26},{3,5},{4,28},{5,3},{6,30},{7,1},{8,16},{9,15},... | collective-permute-start | bytes 1548296 | tf_op jit(solution)/shard_map/ppermute | solution.py:540
  182.7 14.9 %collective-permute-start.30 = (bf16[56,4608]{1,0:T(8,128)(2,1)}, bf16[56,4608]{1,0:T(8,128)(2,1)}, u32[]{:S(2)}, u32[]{:S(2)}) collective-permute-start(bf16[56,4608]{1,0:T(8,128)(2,1)} %get-tuple-element.74), channel_id=1, source_target_pairs={{0,16},{1,5},{2,18},{3,7},{4,20},{5,1},{6,22},{7,3},{8,24},{9,13},... | collective-permute-start | bytes 1548296 | tf_op jit(solution)/shard_map/ppermute | solution.py:540
  182.8 14.9 %collective-permute-start.29 = (bf16[56,4608]{1,0:T(8,128)(2,1)}, bf16[56,4608]{1,0:T(8,128)(2,1)}, u32[]{:S(2)}, u32[]{:S(2)}) collective-permute-start(bf16[56,4608]{1,0:T(8,128)(2,1)} %get-tuple-element.72), channel_id=1, source_target_pairs={{0,8},{1,3},{2,10},{3,1},{4,12},{5,7},{6,14},{7,5},{8,0},{9,11},{1... | collective-permute-start | bytes 1548296 | tf_op jit(solution)/shard_map/ppermute | solution.py:540
  199.3 7.1 %collective-permute-start.34 = (bf16[56,2304]{1,0:T(8,128)(2,1)S(1)}, bf16[56,2304]{1,0:T(8,128)(2,1)S(1)}, u32[]{:S(2)}, u32[]{:S(2)}) collective-permute-start(bf16[56,2304]{1,0:T(8,128)(2,1)S(1)} %get-tuple-element.83), channel_id=1, source_target_pairs={{0,96},{1,97},{2,98},{3,99},{4,100},{5,101},{6,102},{7,103},{8,104... | collective-permute-start | bytes 774152 | tf_op jit(solution)/shard_map/ppermute | solution.py:540
  200.5 5.9 %collective-permute-start.32 = (bf16[56,2304]{1,0:T(8,128)(2,1)S(1)}, bf16[56,2304]{1,0:T(8,128)(2,1)S(1)}, u32[]{:S(2)}, u32[]{:S(2)}) collective-permute-start(bf16[56,2304]{1,0:T(8,128)(2,1)S(1)} %get-tuple-element.84), channel_id=1, source_target_pairs={{0,32},{1,33},{2,34},{3,35},{4,36},{5,37},{6,38},{7,39},{8,40},{9,... | collective-permute-start | bytes 774152 | tf_op jit(solution)/shard_map/ppermute | solution.py:540
  206.6 6.5 %collective-permute-start.33 = (bf16[56,2304]{1,0:T(8,128)(2,1)S(1)}, bf16[56,2304]{1,0:T(8,128)(2,1)S(1)}, u32[]{:S(2)}, u32[]{:S(2)}) collective-permute-start(bf16[56,2304]{1,0:T(8,128)(2,1)S(1)} %get-tuple-element.82), channel_id=1, source_target_pairs={{0,96},{1,97},{2,98},{3,99},{4,100},{5,101},{6,102},{7,103},{8,104... | collective-permute-start | bytes 774152 | tf_op jit(solution)/shard_map/ppermute | solution.py:540
  207.9 5.3 %collective-permute-start.35 = (bf16[56,2304]{1,0:T(8,128)(2,1)S(1)}, bf16[56,2304]{1,0:T(8,128)(2,1)S(1)}, u32[]{:S(2)}, u32[]{:S(2)}) collective-permute-start(bf16[56,2304]{1,0:T(8,128)(2,1)S(1)} %get-tuple-element.81), channel_id=1, source_target_pairs={{0,32},{1,33},{2,34},{3,35},{4,36},{5,37},{6,38},{7,39},{8,40},{9,... | collective-permute-start | bytes 774152 | tf_op jit(solution)/shard_map/ppermute | solution.py:540
  213.3 6.9 %collective-permute-start.38 = (f32[18,1536]{1,0:T(8,128)S(1)}, f32[18,1536]{1,0:T(8,128)S(1)}, u32[]{:S(2)}, u32[]{:S(2)}) collective-permute-start(f32[18,1536]{1,0:T(8,128)S(1)} %fusion.5), channel_id=1, source_target_pairs={{0,6},{1,25},{2,4},{3,27},{4,2},{5,29},{6,0},{7,31},{8,14},{9,17},... | collective-permute-start | bytes 331784 | tf_op jit(solution)/shard_map/ppermute | solution.py:540
  214.3 5.9 %collective-permute-start.37 = (f32[18,1536]{1,0:T(8,128)S(1)}, f32[18,1536]{1,0:T(8,128)S(1)}, u32[]{:S(2)}, u32[]{:S(2)}) collective-permute-start(f32[18,1536]{1,0:T(8,128)S(1)} %fusion.5), channel_id=1, source_target_pairs={{0,4},{1,17},{2,6},{3,19},{4,0},{5,21},{6,2},{7,23},{8,12},{9,25},... | collective-permute-start | bytes 331784 | tf_op jit(solution)/shard_map/ppermute | solution.py:540
  215.2 5.5 %collective-permute-start.36 = (f32[18,1536]{1,0:T(8,128)S(1)}, f32[18,1536]{1,0:T(8,128)S(1)}, u32[]{:S(2)}, u32[]{:S(2)}) collective-permute-start(f32[18,1536]{1,0:T(8,128)S(1)} %fusion.5), channel_id=1, source_target_pairs={{0,2},{1,9},{2,0},{3,11},{4,6},{5,13},{6,4},{7,15},{8,10},{9,1},{1... | collective-permute-start | bytes 331784 | tf_op jit(solution)/shard_map/ppermute | solution.py:540
  220.7 7.8 %collective-permute-start.39 = (f32[18,1536]{1,0:T(8,128)S(1)}, f32[18,1536]{1,0:T(8,128)S(1)}, u32[]{:S(2)}, u32[]{:S(2)}) collective-permute-start(f32[18,1536]{1,0:T(8,128)S(1)} %add_add_fusion), channel_id=1, source_target_pairs={{0,1},{1,0},{2,3},{3,2},{4,5},{5,4},{6,7},{7,6},{8,9},{9,8},{10,11... | collective-permute-start | bytes 331784 | tf_op jit(solution)/shard_map/ppermute | solution.py:540
  (77 other events, 486.2 us)

commit v3 on v2

--- a/solution.py
+++ b/solution.py
@@ -565,11 +565,8 @@
     return values[(0,) * values.ndim] * 0
 
 
-def gather_near(shards):
-    joined = jnp.concatenate(shards, axis=1)
-    near = [joined] + [send(joined, along_first(r)) for r in (1, 2, 3)]
-    wide = shards[0].shape[1]
-    return jnp.stack([block[:, :wide] for block in near]), jnp.stack([block[:, wide:] for block in near])
+def gather_near(shard):
+    return jnp.stack([shard] + [send(shard, along_first(r)) for r in (1, 2, 3)])
 
 
 def gather_far(near):
@@ -655,15 +652,15 @@
     tables = {name: jnp.asarray(value) for name, value in tables.items()}
     first_gain, second_gain = first_gain[None], second_gain[None]
 
-    gate_near, out_near = gather_near((gate_proj, out_proj))
-    outgoing = jnp.take(log_mel, bucket_list[0], axis=0) + zero_of(gate_near)
+    gate_near = gather_near(gate_proj)
+    outgoing = jnp.take(log_mel, bucket_list[0], axis=0) + zero_of(gate_near[1])
     arrived = lax.all_to_all(outgoing, ALL, split_axis=0, concat_axis=0, tiled=True)
     gate_far = gather_far(gate_near)
     stem_total, embedded, normed, normed_t, frames_t, spectrum, mix_grad = stem(
         gate_far[0][0], arrived.reshape(TOK * PATCH, MEL), utterance_frames, stem_weight, first_gain, conv_kernel, cotangent, tables
     )
     gate_pieces = gather_pieces(gate_near, *gate_far, zero_of(normed))
-    out_near = out_near + sum(zero_of(piece) for piece in gate_far[1])
+    out_near = gather_near(out_proj + zero_of(gate_far[0][0])) + sum(zero_of(piece) for piece in gate_far[1])
     out_own = gather_direct(out_near)
     value, gate, filtered = gate_forward(offsets, utterance_frames, gate_pieces, normed, spectrum, tables)
     out_pieces = with_other(out_own, zero_of(filtered).astype(BF16))

time: 231 us -> 229 us (level)
  local copies, waits for them, and re-layouts: 31.5 us -> 24.7 us
  other arithmetic: 15.5 us -> 20.6 us
  waiting for transfers between devices: 31.6 us -> 26.5 us
  starting transfers between devices: 56.2 us -> 60.4 us
    ppermute x40 -> x43, starting transfers between devices: 44.4 us -> 52.3 us  [send(): return lax.ppermute(values, ALL, where)]
    ppermute x40 -> x43, waiting for transfers between devices: 31.6 us -> 24.7 us  [send(): return lax.ppermute(values, ALL, where)]
    unnamed x180 -> x167, local copies, waits for them, and re-layouts: 16.8 us -> 12.8 us
    all_to_all x1, starting transfers between devices: 11.8 us -> 8.14 us  [body(): lax.all_to_all(outgoing, ALL, split_axis=0, concat_axis=0, tiled=True)]
    add x2 -> x3, other arithmetic: 1.08 us -> 3.74 us  [the longest x1 1.58 us: body(): out_proj + zero_of(gate_far[0][0])]
    another operation x6 -> x0, local copies, waits for them, and re-layouts: 2.33 us -> none  [the longest x3 2.27 us: gather_near(): jnp.stack([block[:, wide:] for block in near])]
    slice x10 -> x11, local copies, waits for them, and re-layouts: 6.66 us -> 6.49 us  [zero_of(): return values[(0,) * values.ndim] * 0]
  transfers between devices with their start and end apart: 41 -> 44, of which waited for: 10 -> 15; matrix products, arithmetic and copies ran while one was open for 9% -> 11% of each run, Pallas kernels for 36% -> 37%
where the time goes in v3:
time: 229 us
  Pallas kernels  86.6 us (38%)
  starting transfers between devices  60.4 us (26%)
  waiting for transfers between devices  26.5 us (12%)
  local copies, waits for them, and re-layouts  24.7 us (11%)
  other arithmetic  20.6 us (9%)
  between operations  9.75 us (4%)
    pallas_call x9, Pallas kernels, call(): pl.pallas_call(kernel, name=name, out_shape=outs, in_specs=in_specs, out_...  86.6 us
    ppermute x43, starting transfers between devices, send(): return lax.ppermute(values, ALL, where)  52.3 us
    ppermute x43, waiting for transfers between devices, send(): return lax.ppermute(values, ALL, where)  24.7 us
    unnamed x167, local copies, waits for them, and re-layouts  12.8 us
    all_to_all x1, starting transfers between devices, body(): lax.all_to_all(outgoing, ALL, split_axis=0, concat_axis=0, tiled=True)  8.14 us
    slice x11, local copies, waits for them, and re-layouts, zero_of(): return values[(0,) * values.ndim] * 0  6.49 us
    convert_element_type x2, other arithmetic, body(): (total_of(term) + follow).astype(BF16)  5.13 us
  transfers between devices with their start and end apart: 44, of which 15 were waited for; matrix products, arithmetic and copies ran while one was open for 11% of the time, Pallas kernels for 37%

profile of v3, /device:TPU:1, one launch (start us, length us, event | category | flops | bytes accessed | tf_op | source)
XLA Modules:
  0.0 228.6 jit_solution(16735670669614936739)
XLA Ops:
  0.7 2.2 collective-permute-start
  2.9 1.9 collective-permute-start.7
  8.2 1.3 broadcast_select_fusion.4
  10.4 1.6 collective-permute-start.1
  14.2 3.5 %collective-permute-start.8 = (bf16[2,48,3072]{2,1,0:T(8,128)(2,1)}, bf16[2,48,3072]{2,1,0:T(8,128)(2,1)S(1)}, u32[]{:S(2)}, u32[]{:S(2)}) collective-permute-start(bf16[2,48,3072]{2,1,0:T(8,128)(2,1)} %get-tuple-element.78), channel_id=1, source_target_pairs={{0,24},{1,7},{2,26},{3,5},{4,28},{5,3},{6,30},{7,1},{8,16},{9,15},... | collective-permute-start | bytes 1769480 | tf_op jit(solution)/shard_map/ppermute | solution.py:540
  19.9 8.1 %all-to-all-start = ((bf16[128,16,128]{2,1,0:T(8,128)(2,1)}), bf16[128,16,128]{2,1,0:T(8,128)(2,1)}, u32[]{:S(2)}, u32[]{:S(2)}) async-start(bf16[128,16,128]{2,1,0:T(8,128)(2,1)} %select_add_fusion), calls=%async_computation | async-start | bytes 1048576 | tf_op jit(solution)/shard_map/all_to_all | solution.py:657
  29.2 1.6 broadcast_add_fusion.9
  30.8 2.6 %collective-permute-start.4 = (bf16[48,1536]{1,0:T(8,128)(2,1)}, bf16[48,1536]{1,0:T(8,128)(2,1)}, u32[]{:S(2)}, u32[]{:S(2)}) collective-permute-start(bf16[48,1536]{1,0:T(8,128)(2,1)} %broadcast_add_fusion.9), channel_id=1, source_target_pairs={{0,6},{1,25},{2,4},{3,27},{4,2},{5,29},{6,0},{7,31},{8,14},{9,17},... | collective-permute-start | bytes 442376 | tf_op jit(solution)/shard_map/ppermute | solution.py:540
  34.1 1.2 pad_maximum_fusion.1
  35.3 3.3 %collective-permute-start.5 = (bf16[2,2,48,3072]{3,2,1,0:T(8,128)(2,1)}, bf16[2,2,48,3072]{3,2,1,0:T(8,128)(2,1)S(1)}, u32[]{:S(2)}, u32[]{:S(2)}) collective-permute-start(bf16[2,2,48,3072]{3,2,1,0:T(8,128)(2,1)} %pad_maximum_fusion.1), channel_id=1, source_target_pairs={{0,24},{1,7},{2,26},{3,5},{4,28},{5,3},{6,30},{7,1},{8,16},{9,15},... | collective-permute-start | bytes 3538952 | tf_op jit(solution)/shard_map/ppermute | solution.py:540
  39.7 1.8 all-to-all-done
  41.5 1.4 copy-done.28
  44.7 5.7 %stem.1 = (f32[512,1536]{1,0:T(8,128)S(1)}, bf16[512,1536]{1,0:T(8,128)(2,1)S(1)}, bf16[512,1536]{1,0:T(8,128)(2,1)S(1)}, bf16[1536,512]{1,0:T(8,128)(2,1)S(1)},...) custom-call(bf16[2,48,3072]{2,1,0:T(8,128)(2,1)S(1)} %collective-permute-done.1.unused.refs_1_,, ...), custom_call_target="tpu_custom_call" | custom-call | flops 805306368 | bytes 14680064 | tf_op jit(solution)/shard_map/stem/pallas_call | solution.py:393
  50.4 1.7 copy-done.47
  55.6 1.6 collective-permute-start.17
  62.3 1.2 collective-permute-start.10
  63.7 3.0 %collective-permute-start.11 = (bf16[4,48,1536]{2,1,0:T(8,128)(2,1)S(1)}, bf16[4,48,1536]{2,1,0:T(8,128)(2,1)S(1)}, u32[]{:S(2)}, u32[]{:S(2)}) collective-permute-start(bf16[4,48,1536]{2,1,0:T(8,128)(2,1)S(1)} %maximum_add_fusion.refs_0_), channel_id=1, source_target_pairs={{0,16},{1,5},{2,18},{3,7},{4,20},{5,1},{6,22},{7,3},{8,24},{9,13},... | collective-permute-start | bytes 1769480 | tf_op jit(solution)/shard_map/ppermute | solution.py:540
  67.6 13.7 %gate.1 = (f32[512,1536]{1,0:T(8,128)S(1)}, f32[512,1536]{1,0:T(8,128)S(1)}, f32[512,1536]{1,0:T(8,128)S(1)}) custom-call(s32[32]{0:T(128)S(1)} %pad_add_fusion.offsets, s32[4]{0:T(128)S(1)} %copy-done.27, bf16[4,48,3072]{2,1,0:T(8,128)(2,1)S(1)} %get-tuple-element.76.refs_0_, bf16[2,48,3072]{2,1,0:T(8,128)(2,1)S(1)} %collective-permute-done.1.unused.refs_1_, ...), custom_call_target="tpu_custom_call" | custom-call | flops 4831838208 | bytes 23068672 | tf_op jit(solution)/shard_map/gate/pallas_call | solution.py:393
  81.4 1.7 copy-done.51
  83.1 1.7 copy-done.53
  86.9 6.1 %out_grad.1 = (bf16[16,48,1536]{2,1,0:T(8,128)(2,1)S(1)}, bf16[16,48,1536]{2,1,0:T(8,128)(2,1)S(1)}, bf16[512,1536]{1,0:T(8,128)(2,1)S(1)}) custom-call(s32[33]{0:T(128)S(1)} %pad_add_fusion.1.slots, bf16[4,48,1536]{2,1,0:T(8,128)(2,1)S(1)} %collective-permute-done.10.unused_1.refs_1_, bf16[4,48,1536]{2,1,0:T(8,128)(2,1)S(1)} %collective-permute-done.11.unused_2.refs_2_, ...), custom_call_target="tpu_custom_call" | custom-call | flops 38654705664 | bytes 184549376 | tf_op jit(solution)/shard_map/out_grad/pallas_call | solution.py:393
  94.8 14.3 %middle.1 = (f32[512,1536]{1,0:T(8,128)S(1)}, f32[1,1536]{1,0:T(1,128)S(1)}) custom-call(s32[32]{0:T(128)S(1)} %pad_add_fusion.offsets, bf16[4,48,1536]{2,1,0:T(8,128)(2,1)S(1)} %maximum_add_fusion.refs_0_, bf16[4,48,1536]{2,1,0:T(8,128)(2,1)S(1)} %collective-permute-done.10.unused_1.refs_1_, ...), custom_call_target="tpu_custom_call" | custom-call | flops 38654705664 | bytes 218103808 | tf_op jit(solution)/shard_map/middle/pallas_call | solution.py:393
  109.8 2.6 %collective-permute-start.25 = (bf16[4,48,1536]{2,1,0:T(8,128)(2,1)S(1)}, bf16[4,48,1536]{2,1,0:T(8,128)(2,1)S(1)}, u32[]{:S(2)}, u32[]{:S(2)}) collective-permute-start(bf16[4,48,1536]{2,1,0:T(8,128)(2,1)S(1)} %get-tuple-element.70.unused_2), channel_id=1, source_target_pairs={{0,4},{1,17},{2,6},{3,19},{4,0},{5,21},{6,2},{7,23},{8,12},{9,25},... | collective-permute-start | bytes 1769480 | tf_op jit(solution)/shard_map/ppermute | solution.py:540
  112.4 1.2 collective-permute-start.26
  113.7 1.9 copy-done.54
  115.6 9.8 %conv_back.2 = (bf16[512,1024]{1,0:T(8,128)(2,1)S(1)}, bf16[512,1024]{1,0:T(8,128)(2,1)S(1)}, bf16[16,48,2048]{2,1,0:T(8,128)(2,1)S(1)}, bf16[16,48,2048]{2,1,0:T(8,128)(2,1)S(1)}, f32[32,1024]{1,0:T(8,128)S(1)}) custom-call(s32[33]{0:T(128)S(1)} %pad_add_fusion.1.slots, s32[4]{0:T(128)S(1)} %copy-done.27, ...), custom_call_target="tpu_custom_call" | custom-call | flops 51539607552 | bytes 246065824 | tf_op jit(solution)/shard_map/conv_back/pallas_call | solution.py:393
  126.5 5.0 %conv_back.3 = (bf16[512,512]{1,0:T(8,128)(2,1)S(1)}, bf16[512,512]{1,0:T(8,128)(2,1)S(1)}, bf16[16,48,1024]{2,1,0:T(8,128)(2,1)S(1)}, bf16[16,48,1024]{2,1,0:T(8,128)(2,1)S(1)}, f32[32,512]{1,0:T(8,128)S(1)}) custom-call(s32[33]{0:T(128)S(1)} %pad_add_fusion.1.slots, s32[4]{0:T(128)S(1)} %copy-done.27, bf16[4,48,1536]{2,1,0:T(8,128)(2,1)S(1)} %get-tuple-element.71.unused_1, ...), custom_call_target="tpu_custom_call" | custom-call | flops 25769803776 | bytes 123032912 | tf_op jit(solution)/shard_map/conv_back/pallas_call | solution.py:393
  136.1 2.9 %collective-permute-done.31 = f32[16,1536]{1,0:T(8,128)S(1)} collective-permute-done((f32[16,1536]{1,0:T(8,128)S(1)}, f32[16,1536]{1,0:T(8,128)S(1)}, u32[]{:S(2)}, u32[]{:S(2)}) %collective-permute-start.31) | collective-permute-done | bytes 98336 | tf_op jit(solution)/shard_map/ppermute | solution.py:540
  139.8 3.0 %chip_sum.1 = (bf16[4,48,3072]{2,1,0:T(8,128)(2,1)S(1)}, bf16[4,48,3072]{2,1,0:T(8,128)(2,1)}, bf16[4,48,3072]{2,1,0:T(8,128)(2,1)}, bf16[4,48,3072]{2,1,0:T(8,128)(2,1)}) custom-call(bf16[4,4,48,2048]{3,2,1,0:T(8,128)(2,1)S(1)} %bitcast.53, bf16[4,4,48,2048]{3,2,1,0:T(8,128)(2,1)S(1)} %bitcast.54, bf16[4,4,48,1024]{3,2,1,0:T(8,128)(2,1)S(1)} %bitcast.57, ...), custom_call_target="tpu_custom_call" | custom-call | flops 2359296 | bytes 14680064 | tf_op jit(solution)/shard_map/chip_sum/pallas_call | solution.py:393
  142.7 1.5 collective-permute-start.30
  144.3 1.7 collective-permute-start.28
  147.1 16.7 %stem_back.1 = (f32[1,1536]{1,0:T(1,128)S(1)}, f32[16,48]{1,0:T(8,128)S(1)}) custom-call(s32[32]{0:T(128)S(1)} %pad_add_fusion.offsets, s32[4]{0:T(128)S(1)} %copy-done.27, bf16[4,48,3072]{2,1,0:T(8,128)(2,1)S(1)} %copy-done.16, bf16[2,48,3072]{2,1,0:T(8,128)(2,1)S(1)} %collective-permute-done.1.unused.refs_1_, ...), custom_call_target="tpu_custom_call" | custom-call | flops 77309411328 | bytes 335544320 | tf_op jit(solution)/shard_map/stem_back/pallas_call | solution.py:393
  165.9 2.3 add_convert_fusion.1
  168.2 4.1 %collective-permute-done.30 = bf16[4,48,3072]{2,1,0:T(8,128)(2,1)} collective-permute-done((bf16[4,48,3072]{2,1,0:T(8,128)(2,1)}, bf16[4,48,3072]{2,1,0:T(8,128)(2,1)}, u32[]{:S(2)}, u32[]{:S(2)}) %collective-permute-start.30) | collective-permute-done | bytes 1179680 | tf_op jit(solution)/shard_map/ppermute | solution.py:540
  172.9 2.8 %add_convert_fusion = bf16[4,48,3072]{2,1,0:T(8,128)(2,1)S(1)} fusion(bf16[4,48,3072]{2,1,0:T(8,128)(2,1)} %collective-permute-done.30, bf16[4,48,3072]{2,1,0:T(8,128)(2,1)} %collective-permute-done.29, bf16[4,48,3072]{2,1,0:T(8,128)(2,1)} %collective-permute-done.28, bf16[4,48,3072]{2,1,0:T(8,128)(2,1)S(1)} %copy-done.18, f32[]{:T(128)} %bitcast.29), kind=kLoop, calls=%fused_computation.1 | loop fusion | flops 5308416 | bytes 5898244 | tf_op jit(solution)/shard_map/convert_element_type | solution.py:690
  177.1 2.9 %collective-permute-start.34 = (bf16[56,4608]{1,0:T(8,128)(2,1)}, bf16[56,4608]{1,0:T(8,128)(2,1)S(1)}, u32[]{:S(2)}, u32[]{:S(2)}) collective-permute-start(bf16[56,4608]{1,0:T(8,128)(2,1)} %get-tuple-element.73), channel_id=1, source_target_pairs={{0,24},{1,7},{2,26},{3,5},{4,28},{5,3},{6,30},{7,1},{8,16},{9,15},... | collective-permute-start | bytes 1548296 | tf_op jit(solution)/shard_map/ppermute | solution.py:540
  180.7 12.3 %mixed.1 = bf16[512,1536]{1,0:T(8,128)(2,1)} custom-call(s32[32]{0:T(128)S(1)} %pad_add_fusion.offsets, s32[4]{0:T(128)S(1)} %copy-done.27, bf16[4,48,1536]{2,1,0:T(8,128)(2,1)S(1)} %copy-done.3, bf16[4,48,1536]{2,1,0:T(8,128)(2,1)S(1)} %copy-done.5, bf16[4,48,1536]{2,1,0:T(8,128)(2,1)S(1)} %copy-done.7, bf16[4,48,1536]{2,1,0:T(8,128)(2,1)S(1)} %copy-done.9, ...), custom_call_target="tpu_custom_call" | custom-call | flops 2415919104 | bytes 10485760 | tf_op jit(solution)/shard_map/mixed/pallas_call | solution.py:393
  193.0 1.2 slice.283
  194.9 1.5 fusion.3
  196.5 2.5 %collective-permute-start.37 = (bf16[56,2304]{1,0:T(8,128)(2,1)S(1)}, bf16[56,2304]{1,0:T(8,128)(2,1)S(1)}, u32[]{:S(2)}, u32[]{:S(2)}) collective-permute-start(bf16[56,2304]{1,0:T(8,128)(2,1)S(1)} %get-tuple-element.83), channel_id=1, source_target_pairs={{0,96},{1,97},{2,98},{3,99},{4,100},{5,101},{6,102},{7,103},{8,104... | collective-permute-start | bytes 774152 | tf_op jit(solution)/shard_map/ppermute | solution.py:540
  199.0 4.6 %collective-permute-done.37 = bf16[56,2304]{1,0:T(8,128)(2,1)S(1)} collective-permute-done((bf16[56,2304]{1,0:T(8,128)(2,1)S(1)}, bf16[56,2304]{1,0:T(8,128)(2,1)S(1)}, u32[]{:S(2)}, u32[]{:S(2)}) %collective-permute-start.37) | collective-permute-done | bytes 258080 | tf_op jit(solution)/shard_map/ppermute | solution.py:540
  204.7 1.6 collective-permute-start.36
  206.3 4.9 %collective-permute-done.36 = bf16[56,2304]{1,0:T(8,128)(2,1)S(1)} collective-permute-done((bf16[56,2304]{1,0:T(8,128)(2,1)S(1)}, bf16[56,2304]{1,0:T(8,128)(2,1)S(1)}, u32[]{:S(2)}, u32[]{:S(2)}) %collective-permute-start.36) | collective-permute-done | bytes 258080 | tf_op jit(solution)/shard_map/ppermute | solution.py:540
  211.5 1.5 collective-permute-start.41
  213.0 1.8 collective-permute-start.39
  215.0 1.8 collective-permute-done.41
  216.8 1.7 collective-permute-done.40
  219.0 6.5 %collective-permute-start.42 = (f32[18,1536]{1,0:T(8,128)S(1)}, f32[18,1536]{1,0:T(8,128)S(1)}, u32[]{:S(2)}, u32[]{:S(2)}) collective-permute-start(f32[18,1536]{1,0:T(8,128)S(1)} %add_add_fusion), channel_id=1, source_target_pairs={{0,1},{1,0},{2,3},{3,2},{4,5},{5,4},{6,7},{7,6},{8,9},{9,8},{10,11... | collective-permute-start | bytes 331784 | tf_op jit(solution)/shard_map/ppermute | solution.py:540
  (284 shorter events, 37.1 us)
Async XLA Ops:
  0.7 8.9 %collective-permute-start = (bf16[48,3072]{1,0:T(8,128)(2,1)}, bf16[48,3072]{1,0:T(8,128)(2,1)S(1)}, u32[]{:S(2)}, u32[]{:S(2)}) collective-permute-start(bf16[48,3072]{1,0:T(8,128)(2,1)} %param.25), channel_id=1, source_target_pairs={{0,2},{1,9},{2,0},{3,11},{4,6},{5,13},{6,4},{7,15},{8,10},{9,1},{1... | collective-permute-start | bytes 884744 | tf_op jit(solution)/shard_map/ppermute | solution.py:540
  2.9 9.2 %collective-permute-start.7 = (bf16[48,3072]{1,0:T(8,128)(2,1)}, bf16[48,3072]{1,0:T(8,128)(2,1)S(1)}, u32[]{:S(2)}, u32[]{:S(2)}) collective-permute-start(bf16[48,3072]{1,0:T(8,128)(2,1)} %param.25), channel_id=1, source_target_pairs={{0,6},{1,25},{2,4},{3,27},{4,2},{5,29},{6,0},{7,31},{8,14},{9,17},... | collective-permute-start | bytes 884744 | tf_op jit(solution)/shard_map/ppermute | solution.py:540
  4.8 8.5 %collective-permute-start.6 = (bf16[48,3072]{1,0:T(8,128)(2,1)}, bf16[48,3072]{1,0:T(8,128)(2,1)S(1)}, u32[]{:S(2)}, u32[]{:S(2)}) collective-permute-start(bf16[48,3072]{1,0:T(8,128)(2,1)} %param.25), channel_id=1, source_target_pairs={{0,4},{1,17},{2,6},{3,19},{4,0},{5,21},{6,2},{7,23},{8,12},{9,25},... | collective-permute-start | bytes 884744 | tf_op jit(solution)/shard_map/ppermute | solution.py:540
  10.4 17.6 %collective-permute-start.1 = (bf16[2,48,3072]{2,1,0:T(8,128)(2,1)}, bf16[2,48,3072]{2,1,0:T(8,128)(2,1)S(1)}, u32[]{:S(2)}, u32[]{:S(2)}) collective-permute-start(bf16[2,48,3072]{2,1,0:T(8,128)(2,1)} %get-tuple-element.80), channel_id=1, source_target_pairs={{0,8},{1,3},{2,10},{3,1},{4,12},{5,7},{6,14},{7,5},{8,0},{9,11},{1... | collective-permute-start | bytes 1769480 | tf_op jit(solution)/shard_map/ppermute | solution.py:540
  14.2 24.4 %collective-permute-start.8 = (bf16[2,48,3072]{2,1,0:T(8,128)(2,1)}, bf16[2,48,3072]{2,1,0:T(8,128)(2,1)S(1)}, u32[]{:S(2)}, u32[]{:S(2)}) collective-permute-start(bf16[2,48,3072]{2,1,0:T(8,128)(2,1)} %get-tuple-element.78), channel_id=1, source_target_pairs={{0,24},{1,7},{2,26},{3,5},{4,28},{5,3},{6,30},{7,1},{8,16},{9,15},... | collective-permute-start | bytes 1769480 | tf_op jit(solution)/shard_map/ppermute | solution.py:540
  19.9 21.6 %all-to-all-start = ((bf16[128,16,128]{2,1,0:T(8,128)(2,1)}), bf16[128,16,128]{2,1,0:T(8,128)(2,1)}, u32[]{:S(2)}, u32[]{:S(2)}) async-start(bf16[128,16,128]{2,1,0:T(8,128)(2,1)} %select_add_fusion), calls=%async_computation | async-start | bytes 1048576 | tf_op jit(solution)/shard_map/all_to_all | solution.py:657
  30.8 26.7 %collective-permute-start.4 = (bf16[48,1536]{1,0:T(8,128)(2,1)}, bf16[48,1536]{1,0:T(8,128)(2,1)}, u32[]{:S(2)}, u32[]{:S(2)}) collective-permute-start(bf16[48,1536]{1,0:T(8,128)(2,1)} %broadcast_add_fusion.9), channel_id=1, source_target_pairs={{0,6},{1,25},{2,4},{3,27},{4,2},{5,29},{6,0},{7,31},{8,14},{9,17},... | collective-permute-start | bytes 442376 | tf_op jit(solution)/shard_map/ppermute | solution.py:540
  33.5 24.2 %collective-permute-start.3 = (bf16[48,1536]{1,0:T(8,128)(2,1)}, bf16[48,1536]{1,0:T(8,128)(2,1)}, u32[]{:S(2)}, u32[]{:S(2)}) collective-permute-start(bf16[48,1536]{1,0:T(8,128)(2,1)} %broadcast_add_fusion.9), channel_id=1, source_target_pairs={{0,4},{1,17},{2,6},{3,19},{4,0},{5,21},{6,2},{7,23},{8,12},{9,25},... | collective-permute-start | bytes 442376 | tf_op jit(solution)/shard_map/ppermute | solution.py:540
  34.0 24.2 %collective-permute-start.2 = (bf16[48,1536]{1,0:T(8,128)(2,1)}, bf16[48,1536]{1,0:T(8,128)(2,1)}, u32[]{:S(2)}, u32[]{:S(2)}) collective-permute-start(bf16[48,1536]{1,0:T(8,128)(2,1)} %broadcast_add_fusion.9), channel_id=1, source_target_pairs={{0,2},{1,9},{2,0},{3,11},{4,6},{5,13},{6,4},{7,15},{8,10},{9,1},{1... | collective-permute-start | bytes 442376 | tf_op jit(solution)/shard_map/ppermute | solution.py:540
  35.3 19.7 %collective-permute-start.5 = (bf16[2,2,48,3072]{3,2,1,0:T(8,128)(2,1)}, bf16[2,2,48,3072]{3,2,1,0:T(8,128)(2,1)S(1)}, u32[]{:S(2)}, u32[]{:S(2)}) collective-permute-start(bf16[2,2,48,3072]{3,2,1,0:T(8,128)(2,1)} %pad_maximum_fusion.1), channel_id=1, source_target_pairs={{0,24},{1,7},{2,26},{3,5},{4,28},{5,3},{6,30},{7,1},{8,16},{9,15},... | collective-permute-start | bytes 3538952 | tf_op jit(solution)/shard_map/ppermute | solution.py:540
  39.7 15.9 %collective-permute-start.9 = (bf16[2,2,48,3072]{3,2,1,0:T(8,128)(2,1)}, bf16[2,2,48,3072]{3,2,1,0:T(8,128)(2,1)S(1)}, u32[]{:S(2)}, u32[]{:S(2)}) collective-permute-start(bf16[2,2,48,3072]{3,2,1,0:T(8,128)(2,1)} %pad_maximum_fusion.2), channel_id=1, source_target_pairs={{0,8},{1,3},{2,10},{3,1},{4,12},{5,7},{6,14},{7,5},{8,0},{9,11},{1... | collective-permute-start | bytes 3538952 | tf_op jit(solution)/shard_map/ppermute | solution.py:540
  52.1 42.7 %copy-start.48 = (bf16[512,1536]{1,0:T(8,128)(2,1)}, bf16[512,1536]{1,0:T(8,128)(2,1)S(1)}, u32[]{:S(2)}) copy-start(bf16[512,1536]{1,0:T(8,128)(2,1)S(1)} %get-tuple-element.41.mix_grad.refs_9_.refs_19_) | copy-start | bytes 4718596
  52.1 93.9 %copy-start.11 = (bf16[512,1536]{1,0:T(8,128)(2,1)}, bf16[512,1536]{1,0:T(8,128)(2,1)S(1)}, u32[]{:S(2)}) copy-start(bf16[512,1536]{1,0:T(8,128)(2,1)S(1)} %get-tuple-element.60.refs_17_.refs_10_) | copy-start | bytes 4718596
  55.0 11.6 %collective-permute-start.14 = (bf16[4,48,3072]{2,1,0:T(8,128)(2,1)S(1)}, bf16[4,48,3072]{2,1,0:T(8,128)(2,1)S(1)}, u32[]{:S(2)}, u32[]{:S(2)}) collective-permute-start(bf16[4,48,3072]{2,1,0:T(8,128)(2,1)S(1)} %get-tuple-element.75), channel_id=1, source_target_pairs={{0,1},{1,0},{2,3},{3,2},{4,5},{5,4},{6,7},{7,6},{8,9},{9,8},{10,11... | collective-permute-start | bytes 3538952 | tf_op jit(solution)/shard_map/ppermute | solution.py:540
  55.6 11.1 %collective-permute-start.17 = (bf16[4,48,3072]{2,1,0:T(8,128)(2,1)S(1)}, bf16[4,48,3072]{2,1,0:T(8,128)(2,1)S(1)}, u32[]{:S(2)}, u32[]{:S(2)}) collective-permute-start(bf16[4,48,3072]{2,1,0:T(8,128)(2,1)S(1)} %broadcast_add_fusion.2), channel_id=1, source_target_pairs={{0,1},{1,0},{2,3},{3,2},{4,5},{5,4},{6,7},{7,6},{8,9},{9,8},{10,11... | collective-permute-start | bytes 3538952 | tf_op jit(solution)/shard_map/ppermute | solution.py:540
  57.5 10.1 %collective-permute-start.18 = (bf16[4,48,3072]{2,1,0:T(8,128)(2,1)S(1)}, bf16[4,48,3072]{2,1,0:T(8,128)(2,1)S(1)}, u32[]{:S(2)}, u32[]{:S(2)}) collective-permute-start(bf16[4,48,3072]{2,1,0:T(8,128)(2,1)S(1)} %broadcast_add_fusion.1), channel_id=1, source_target_pairs={{0,1},{1,0},{2,3},{3,2},{4,5},{5,4},{6,7},{7,6},{8,9},{9,8},{10,11... | collective-permute-start | bytes 3538952 | tf_op jit(solution)/shard_map/ppermute | solution.py:540
  57.7 4.6 %collective-permute-start.15 = (bf16[2,48,3072]{2,1,0:T(8,128)(2,1)S(1)}, bf16[2,48,3072]{2,1,0:T(8,128)(2,1)S(1)}, u32[]{:S(2)}, u32[]{:S(2)}) collective-permute-start(bf16[2,48,3072]{2,1,0:T(8,128)(2,1)S(1)} %broadcast_add_fusion.8), channel_id=1, source_target_pairs={{0,1},{1,0},{2,3},{3,2},{4,5},{5,4},{6,7},{7,6},{8,9},{9,8},{10,11... | collective-permute-start | bytes 1769480 | tf_op jit(solution)/shard_map/ppermute | solution.py:540
  58.2 5.4 %collective-permute-start.16 = (bf16[2,48,3072]{2,1,0:T(8,128)(2,1)S(1)}, bf16[2,48,3072]{2,1,0:T(8,128)(2,1)S(1)}, u32[]{:S(2)}, u32[]{:S(2)}) collective-permute-start(bf16[2,48,3072]{2,1,0:T(8,128)(2,1)S(1)} %broadcast_add_fusion.7), channel_id=1, source_target_pairs={{0,1},{1,0},{2,3},{3,2},{4,5},{5,4},{6,7},{7,6},{8,9},{9,8},{10,11... | collective-permute-start | bytes 1769480 | tf_op jit(solution)/shard_map/ppermute | solution.py:540
  61.8 32.9 %copy-start.2 = (bf16[4,48,1536]{2,1,0:T(8,128)(2,1)}, bf16[4,48,1536]{2,1,0:T(8,128)(2,1)S(1)}, u32[]{:S(2)}) copy-start(bf16[4,48,1536]{2,1,0:T(8,128)(2,1)S(1)} %maximum_add_fusion.refs_0_) | copy-start | bytes 1769476
  62.3 23.7 %collective-permute-start.10 = (bf16[4,48,1536]{2,1,0:T(8,128)(2,1)S(1)}, bf16[4,48,1536]{2,1,0:T(8,128)(2,1)S(1)}, u32[]{:S(2)}, u32[]{:S(2)}) collective-permute-start(bf16[4,48,1536]{2,1,0:T(8,128)(2,1)S(1)} %maximum_add_fusion.refs_0_), channel_id=1, source_target_pairs={{0,8},{1,3},{2,10},{3,1},{4,12},{5,7},{6,14},{7,5},{8,0},{9,11},{1... | collective-permute-start | bytes 1769480 | tf_op jit(solution)/shard_map/ppermute | solution.py:540
  63.7 22.5 %collective-permute-start.11 = (bf16[4,48,1536]{2,1,0:T(8,128)(2,1)S(1)}, bf16[4,48,1536]{2,1,0:T(8,128)(2,1)S(1)}, u32[]{:S(2)}, u32[]{:S(2)}) collective-permute-start(bf16[4,48,1536]{2,1,0:T(8,128)(2,1)S(1)} %maximum_add_fusion.refs_0_), channel_id=1, source_target_pairs={{0,16},{1,5},{2,18},{3,7},{4,20},{5,1},{6,22},{7,3},{8,24},{9,13},... | collective-permute-start | bytes 1769480 | tf_op jit(solution)/shard_map/ppermute | solution.py:540
  66.6 20.1 %collective-permute-start.12 = (bf16[4,48,1536]{2,1,0:T(8,128)(2,1)S(1)}, bf16[4,48,1536]{2,1,0:T(8,128)(2,1)S(1)}, u32[]{:S(2)}, u32[]{:S(2)}) collective-permute-start(bf16[4,48,1536]{2,1,0:T(8,128)(2,1)S(1)} %maximum_add_fusion.refs_0_), channel_id=1, source_target_pairs={{0,24},{1,7},{2,26},{3,5},{4,28},{5,3},{6,30},{7,1},{8,16},{9,15},... | collective-permute-start | bytes 1769480 | tf_op jit(solution)/shard_map/ppermute | solution.py:540
  66.7 28.0 %collective-permute-start.13 = (bf16[4,48,1536]{2,1,0:T(8,128)(2,1)S(1)}, bf16[4,48,1536]{2,1,0:T(8,128)(2,1)S(1)}, u32[]{:S(2)}, u32[]{:S(2)}) collective-permute-start(bf16[4,48,1536]{2,1,0:T(8,128)(2,1)S(1)} %maximum_add_fusion.refs_0_), channel_id=1, source_target_pairs={{0,1},{1,0},{2,3},{3,2},{4,5},{5,4},{6,7},{7,6},{8,9},{9,8},{10,11... | collective-permute-start | bytes 1769480 | tf_op jit(solution)/shard_map/ppermute | solution.py:540
  86.0 8.7 %collective-permute-start.19 = (bf16[4,48,1536]{2,1,0:T(8,128)(2,1)S(1)}, bf16[4,48,1536]{2,1,0:T(8,128)(2,1)S(1)}, u32[]{:S(2)}, u32[]{:S(2)}) collective-permute-start(bf16[4,48,1536]{2,1,0:T(8,128)(2,1)S(1)} %broadcast_add_fusion.6), channel_id=1, source_target_pairs={{0,1},{1,0},{2,3},{3,2},{4,5},{5,4},{6,7},{7,6},{8,9},{9,8},{10,11... | collective-permute-start | bytes 1769480 | tf_op jit(solution)/shard_map/ppermute | solution.py:540
  86.2 8.5 %collective-permute-start.20 = (bf16[4,48,1536]{2,1,0:T(8,128)(2,1)S(1)}, bf16[4,48,1536]{2,1,0:T(8,128)(2,1)S(1)}, u32[]{:S(2)}, u32[]{:S(2)}) collective-permute-start(bf16[4,48,1536]{2,1,0:T(8,128)(2,1)S(1)} %broadcast_add_fusion.5), channel_id=1, source_target_pairs={{0,1},{1,0},{2,3},{3,2},{4,5},{5,4},{6,7},{7,6},{8,9},{9,8},{10,11... | collective-permute-start | bytes 1769480 | tf_op jit(solution)/shard_map/ppermute | solution.py:540
  86.8 7.9 %collective-permute-start.21 = (bf16[4,48,1536]{2,1,0:T(8,128)(2,1)S(1)}, bf16[4,48,1536]{2,1,0:T(8,128)(2,1)S(1)}, u32[]{:S(2)}, u32[]{:S(2)}) collective-permute-start(bf16[4,48,1536]{2,1,0:T(8,128)(2,1)S(1)} %broadcast_add_fusion.4), channel_id=1, source_target_pairs={{0,1},{1,0},{2,3},{3,2},{4,5},{5,4},{6,7},{7,6},{8,9},{9,8},{10,11... | collective-permute-start | bytes 1769480 | tf_op jit(solution)/shard_map/ppermute | solution.py:540
  94.2 14.9 %collective-permute-start.22 = (bf16[16,48,1536]{2,1,0:T(8,128)(2,1)S(1)}, bf16[16,48,1536]{2,1,0:T(8,128)(2,1)S(1)}, u32[]{:S(2)}, u32[]{:S(2)}) collective-permute-start(bf16[16,48,1536]{2,1,0:T(8,128)(2,1)S(1)} %get-tuple-element.43), channel_id=1, source_target_pairs={{0,1},{1,0},{2,3},{3,2},{4,5},{5,4},{6,7},{7,6},{8,9},{9,8},{10,11... | collective-permute-start | bytes 7077896 | tf_op jit(solution)/shard_map/ppermute | solution.py:540
  109.7 21.9 %collective-permute-start.24 = (bf16[4,48,1536]{2,1,0:T(8,128)(2,1)S(1)}, bf16[4,48,1536]{2,1,0:T(8,128)(2,1)S(1)}, u32[]{:S(2)}, u32[]{:S(2)}) collective-permute-start(bf16[4,48,1536]{2,1,0:T(8,128)(2,1)S(1)} %get-tuple-element.71.unused_1), channel_id=1, source_target_pairs={{0,2},{1,9},{2,0},{3,11},{4,6},{5,13},{6,4},{7,15},{8,10},{9,1},{1... | collective-permute-start | bytes 1769480 | tf_op jit(solution)/shard_map/ppermute | solution.py:540
  109.8 22.4 %collective-permute-start.25 = (bf16[4,48,1536]{2,1,0:T(8,128)(2,1)S(1)}, bf16[4,48,1536]{2,1,0:T(8,128)(2,1)S(1)}, u32[]{:S(2)}, u32[]{:S(2)}) collective-permute-start(bf16[4,48,1536]{2,1,0:T(8,128)(2,1)S(1)} %get-tuple-element.70.unused_2), channel_id=1, source_target_pairs={{0,4},{1,17},{2,6},{3,19},{4,0},{5,21},{6,2},{7,23},{8,12},{9,25},... | collective-permute-start | bytes 1769480 | tf_op jit(solution)/shard_map/ppermute | solution.py:540
  112.4 21.6 %collective-permute-start.26 = (bf16[4,48,1536]{2,1,0:T(8,128)(2,1)S(1)}, bf16[4,48,1536]{2,1,0:T(8,128)(2,1)S(1)}, u32[]{:S(2)}, u32[]{:S(2)}) collective-permute-start(bf16[4,48,1536]{2,1,0:T(8,128)(2,1)S(1)} %get-tuple-element.69.unused_3), channel_id=1, source_target_pairs={{0,6},{1,25},{2,4},{3,27},{4,2},{5,29},{6,0},{7,31},{8,14},{9,17},... | collective-permute-start | bytes 1769480 | tf_op jit(solution)/shard_map/ppermute | solution.py:540
  125.3 14.4 %collective-permute-start.23 = (bf16[16,48,2048]{2,1,0:T(8,128)(2,1)S(1)}, bf16[16,48,2048]{2,1,0:T(8,128)(2,1)S(1)}, u32[]{:S(2)}, u32[]{:S(2)}) collective-permute-start(bf16[16,48,2048]{2,1,0:T(8,128)(2,1)S(1)} %get-tuple-element.49), channel_id=1, source_target_pairs={{0,1},{1,0},{2,3},{3,2},{4,5},{5,4},{6,7},{7,6},{8,9},{9,8},{10,11... | collective-permute-start | bytes 9437192 | tf_op jit(solution)/shard_map/ppermute | solution.py:540
  135.4 4.3 %collective-permute-start.27 = (bf16[16,48,1024]{2,1,0:T(8,128)(2,1)S(1)}, bf16[16,48,1024]{2,1,0:T(8,128)(2,1)S(1)}, u32[]{:S(2)}, u32[]{:S(2)}) collective-permute-start(bf16[16,48,1024]{2,1,0:T(8,128)(2,1)S(1)} %broadcast_add_fusion), channel_id=1, source_target_pairs={{0,1},{1,0},{2,3},{3,2},{4,5},{5,4},{6,7},{7,6},{8,9},{9,8},{10,11... | collective-permute-start | bytes 4718600 | tf_op jit(solution)/shard_map/ppermute | solution.py:540
  135.6 3.5 %collective-permute-start.31 = (f32[16,1536]{1,0:T(8,128)S(1)}, f32[16,1536]{1,0:T(8,128)S(1)}, u32[]{:S(2)}, u32[]{:S(2)}) collective-permute-start(f32[16,1536]{1,0:T(8,128)S(1)} %broadcast_select_fusion), channel_id=1, source_target_pairs={{0,1},{1,0},{2,3},{3,2},{4,5},{5,4},{6,7},{7,6},{8,9},{9,8},{10,11... | collective-permute-start | bytes 294920 | tf_op jit(solution)/shard_map/ppermute | solution.py:540
  142.7 21.1 %copy-start.17 = (bf16[4,48,3072]{2,1,0:T(8,128)(2,1)}, bf16[4,48,3072]{2,1,0:T(8,128)(2,1)S(1)}, u32[]{:S(2)}) copy-start(bf16[4,48,3072]{2,1,0:T(8,128)(2,1)S(1)} %get-tuple-element.52) | copy-start | bytes 3538948
  142.7 29.5 %collective-permute-start.30 = (bf16[4,48,3072]{2,1,0:T(8,128)(2,1)}, bf16[4,48,3072]{2,1,0:T(8,128)(2,1)}, u32[]{:S(2)}, u32[]{:S(2)}) collective-permute-start(bf16[4,48,3072]{2,1,0:T(8,128)(2,1)} %get-tuple-element.55.refs_16_), channel_id=1, source_target_pairs={{0,6},{1,25},{2,4},{3,27},{4,2},{5,29},{6,0},{7,31},{8,14},{9,17},... | collective-permute-start | bytes 3538952 | tf_op jit(solution)/shard_map/ppermute | solution.py:540
  144.2 28.0 %collective-permute-start.29 = (bf16[4,48,3072]{2,1,0:T(8,128)(2,1)}, bf16[4,48,3072]{2,1,0:T(8,128)(2,1)}, u32[]{:S(2)}, u32[]{:S(2)}) collective-permute-start(bf16[4,48,3072]{2,1,0:T(8,128)(2,1)} %get-tuple-element.54.refs_15_), channel_id=1, source_target_pairs={{0,4},{1,17},{2,6},{3,19},{4,0},{5,21},{6,2},{7,23},{8,12},{9,25},... | collective-permute-start | bytes 3538952 | tf_op jit(solution)/shard_map/ppermute | solution.py:540
  144.3 28.6 %collective-permute-start.28 = (bf16[4,48,3072]{2,1,0:T(8,128)(2,1)}, bf16[4,48,3072]{2,1,0:T(8,128)(2,1)}, u32[]{:S(2)}, u32[]{:S(2)}) collective-permute-start(bf16[4,48,3072]{2,1,0:T(8,128)(2,1)} %get-tuple-element.53.refs_14_), channel_id=1, source_target_pairs={{0,2},{1,9},{2,0},{3,11},{4,6},{5,13},{6,4},{7,15},{8,10},{9,1},{1... | collective-permute-start | bytes 3538952 | tf_op jit(solution)/shard_map/ppermute | solution.py:540
  177.1 17.8 %collective-permute-start.34 = (bf16[56,4608]{1,0:T(8,128)(2,1)}, bf16[56,4608]{1,0:T(8,128)(2,1)S(1)}, u32[]{:S(2)}, u32[]{:S(2)}) collective-permute-start(bf16[56,4608]{1,0:T(8,128)(2,1)} %get-tuple-element.73), channel_id=1, source_target_pairs={{0,24},{1,7},{2,26},{3,5},{4,28},{5,3},{6,30},{7,1},{8,16},{9,15},... | collective-permute-start | bytes 1548296 | tf_op jit(solution)/shard_map/ppermute | solution.py:540
  180.0 14.9 %collective-permute-start.33 = (bf16[56,4608]{1,0:T(8,128)(2,1)}, bf16[56,4608]{1,0:T(8,128)(2,1)}, u32[]{:S(2)}, u32[]{:S(2)}) collective-permute-start(bf16[56,4608]{1,0:T(8,128)(2,1)} %get-tuple-element.74), channel_id=1, source_target_pairs={{0,16},{1,5},{2,18},{3,7},{4,20},{5,1},{6,22},{7,3},{8,24},{9,13},... | collective-permute-start | bytes 1548296 | tf_op jit(solution)/shard_map/ppermute | solution.py:540
  180.0 14.9 %collective-permute-start.32 = (bf16[56,4608]{1,0:T(8,128)(2,1)S(1)}, bf16[56,4608]{1,0:T(8,128)(2,1)}, u32[]{:S(2)}, u32[]{:S(2)}) collective-permute-start(bf16[56,4608]{1,0:T(8,128)(2,1)S(1)} %get-tuple-element.72), channel_id=1, source_target_pairs={{0,8},{1,3},{2,10},{3,1},{4,12},{5,7},{6,14},{7,5},{8,0},{9,11},{1... | collective-permute-start | bytes 1548296 | tf_op jit(solution)/shard_map/ppermute | solution.py:540
  196.5 7.1 %collective-permute-start.37 = (bf16[56,2304]{1,0:T(8,128)(2,1)S(1)}, bf16[56,2304]{1,0:T(8,128)(2,1)S(1)}, u32[]{:S(2)}, u32[]{:S(2)}) collective-permute-start(bf16[56,2304]{1,0:T(8,128)(2,1)S(1)} %get-tuple-element.83), channel_id=1, source_target_pairs={{0,96},{1,97},{2,98},{3,99},{4,100},{5,101},{6,102},{7,103},{8,104... | collective-permute-start | bytes 774152 | tf_op jit(solution)/shard_map/ppermute | solution.py:540
  199.0 5.6 %collective-permute-start.35 = (bf16[56,2304]{1,0:T(8,128)(2,1)S(1)}, bf16[56,2304]{1,0:T(8,128)(2,1)S(1)}, u32[]{:S(2)}, u32[]{:S(2)}) collective-permute-start(bf16[56,2304]{1,0:T(8,128)(2,1)S(1)} %get-tuple-element.84), channel_id=1, source_target_pairs={{0,32},{1,33},{2,34},{3,35},{4,36},{5,37},{6,38},{7,39},{8,40},{9,... | collective-permute-start | bytes 774152 | tf_op jit(solution)/shard_map/ppermute | solution.py:540
  204.7 6.5 %collective-permute-start.36 = (bf16[56,2304]{1,0:T(8,128)(2,1)S(1)}, bf16[56,2304]{1,0:T(8,128)(2,1)S(1)}, u32[]{:S(2)}, u32[]{:S(2)}) collective-permute-start(bf16[56,2304]{1,0:T(8,128)(2,1)S(1)} %get-tuple-element.82), channel_id=1, source_target_pairs={{0,96},{1,97},{2,98},{3,99},{4,100},{5,101},{6,102},{7,103},{8,104... | collective-permute-start | bytes 774152 | tf_op jit(solution)/shard_map/ppermute | solution.py:540
  206.3 5.2 %collective-permute-start.38 = (bf16[56,2304]{1,0:T(8,128)(2,1)S(1)}, bf16[56,2304]{1,0:T(8,128)(2,1)S(1)}, u32[]{:S(2)}, u32[]{:S(2)}) collective-permute-start(bf16[56,2304]{1,0:T(8,128)(2,1)S(1)} %get-tuple-element.81), channel_id=1, source_target_pairs={{0,32},{1,33},{2,34},{3,35},{4,36},{5,37},{6,38},{7,39},{8,40},{9,... | collective-permute-start | bytes 774152 | tf_op jit(solution)/shard_map/ppermute | solution.py:540
  211.5 5.3 %collective-permute-start.41 = (f32[18,1536]{1,0:T(8,128)S(1)}, f32[18,1536]{1,0:T(8,128)S(1)}, u32[]{:S(2)}, u32[]{:S(2)}) collective-permute-start(f32[18,1536]{1,0:T(8,128)S(1)} %fusion.5), channel_id=1, source_target_pairs={{0,6},{1,25},{2,4},{3,27},{4,2},{5,29},{6,0},{7,31},{8,14},{9,17},... | collective-permute-start | bytes 331784 | tf_op jit(solution)/shard_map/ppermute | solution.py:540
  213.0 5.5 %collective-permute-start.40 = (f32[18,1536]{1,0:T(8,128)S(1)}, f32[18,1536]{1,0:T(8,128)S(1)}, u32[]{:S(2)}, u32[]{:S(2)}) collective-permute-start(f32[18,1536]{1,0:T(8,128)S(1)} %fusion.5), channel_id=1, source_target_pairs={{0,4},{1,17},{2,6},{3,19},{4,0},{5,21},{6,2},{7,23},{8,12},{9,25},... | collective-permute-start | bytes 331784 | tf_op jit(solution)/shard_map/ppermute | solution.py:540
  213.0 5.9 %collective-permute-start.39 = (f32[18,1536]{1,0:T(8,128)S(1)}, f32[18,1536]{1,0:T(8,128)S(1)}, u32[]{:S(2)}, u32[]{:S(2)}) collective-permute-start(f32[18,1536]{1,0:T(8,128)S(1)} %fusion.5), channel_id=1, source_target_pairs={{0,2},{1,9},{2,0},{3,11},{4,6},{5,13},{6,4},{7,15},{8,10},{9,1},{1... | collective-permute-start | bytes 331784 | tf_op jit(solution)/shard_map/ppermute | solution.py:540
  219.0 7.5 %collective-permute-start.42 = (f32[18,1536]{1,0:T(8,128)S(1)}, f32[18,1536]{1,0:T(8,128)S(1)}, u32[]{:S(2)}, u32[]{:S(2)}) collective-permute-start(f32[18,1536]{1,0:T(8,128)S(1)} %add_add_fusion), channel_id=1, source_target_pairs={{0,1},{1,0},{2,3},{3,2},{4,5},{5,4},{6,7},{7,6},{8,9},{9,8},{10,11... | collective-permute-start | bytes 331784 | tf_op jit(solution)/shard_map/ppermute | solution.py:540
  (74 other events, 474.1 us)

commit v4 on v3

--- a/solution.py
+++ b/solution.py
@@ -360,16 +360,16 @@
     assemble(offsets, pieces, held, sems)
 
     def product(n, carry):
-        cols = pl.ds(pl.multiple_of(n * CB, CB), CB)
+        cols = pl.ds(pl.multiple_of(n * 2 * CB, 2 * CB), 2 * CB)
         mixed = mm(swished[...], held[:, cols])
         for u in range(NU):
             rows = slice(u * UTT, (u + 1) * UTT)
             total = embedded[rows, cols].astype(F32) + mixed[rows]
-            valid = keep(frames_of[u] // PATCH, (UTT, CB))
+            valid = keep(frames_of[u] // PATCH, (UTT, 2 * CB))
             output[rows, cols] = jnp.where(valid, total, 0.0).astype(BF16)
         return carry
 
-    lax.fori_loop(0, NB, product, 0)
+    lax.fori_loop(0, NB // 2, product, 0)
 
 
 def chip_sum_kernel(mine_1, other_1, mine_2, other_2, *groups):
@@ -635,7 +635,8 @@
 
 
 def finish_small(values, rows, c):
-    values = total_of([values] + [send(values, along_first(r)) for r in (1, 2, 3)])
+    narrow = values.astype(BF16)
+    values = total_of([values] + [send(narrow, along_first(r)) for r in (1, 2, 3)])
     other = send(values, other_core())
     mine, late = values[:rows], values[rows:] + other[rows:]
     other = other[:rows]

time: 229 us -> 228 us (level)
  transfers between devices with their start and end apart: 44 -> 44, of which waited for: 15 -> 14; matrix products, arithmetic and copies ran while one was open for 11% -> 11% of each run, Pallas kernels for 37% -> 37%
where the time goes in v4:
time: 228 us; the launch traced here: 227 us
  Pallas kernels  86.1 us (38%)
  starting transfers between devices  60.8 us (27%)
  waiting for transfers between devices  25.3 us (11%)
  local copies, waits for them, and re-layouts  24.7 us (11%)
  other arithmetic  20.6 us (9%)
  between operations  9.75 us (4%)
    pallas_call x9, Pallas kernels, call(): pl.pallas_call(kernel, name=name, out_shape=outs, in_specs=in_specs, out_...  86.1 us
    ppermute x43, starting transfers between devices, send(): return lax.ppermute(values, ALL, where)  52.7 us
    ppermute x43, waiting for transfers between devices, send(): return lax.ppermute(values, ALL, where)  23.5 us
    unnamed x167, local copies, waits for them, and re-layouts  12.8 us
    all_to_all x1, starting transfers between devices, body(): lax.all_to_all(outgoing, ALL, split_axis=0, concat_axis=0, tiled=True)  8.13 us
    slice x11, local copies, waits for them, and re-layouts, zero_of(): return values[(0,) * values.ndim] * 0  6.42 us
    convert_element_type x2, other arithmetic, body(): (total_of(term) + follow).astype(BF16)  5.13 us
  transfers between devices with their start and end apart: 44, of which 14 were waited for; matrix products, arithmetic and copies ran while one was open for 11% of the time, Pallas kernels for 37%

profile of v4, /device:TPU:1, one launch (start us, length us, event | category | flops | bytes accessed | tf_op | source)
XLA Modules:
  0.0 227.3 jit_solution(6500786035664638928)
XLA Ops:
  0.7 2.2 collective-permute-start
  2.9 1.9 collective-permute-start.7
  8.2 1.3 broadcast_select_fusion.4
  10.4 1.6 collective-permute-start.1
  12.1 1.2 collective-permute-done.6
  14.2 3.5 %collective-permute-start.8 = (bf16[2,48,3072]{2,1,0:T(8,128)(2,1)}, bf16[2,48,3072]{2,1,0:T(8,128)(2,1)S(1)}, u32[]{:S(2)}, u32[]{:S(2)}) collective-permute-start(bf16[2,48,3072]{2,1,0:T(8,128)(2,1)} %get-tuple-element.80), channel_id=1, source_target_pairs={{0,24},{1,7},{2,26},{3,5},{4,28},{5,3},{6,30},{7,1},{8,16},{9,15},... | collective-permute-start | bytes 1769480 | tf_op jit(solution)/shard_map/ppermute | solution.py:540
  19.9 8.1 %all-to-all-start = ((bf16[128,16,128]{2,1,0:T(8,128)(2,1)}), bf16[128,16,128]{2,1,0:T(8,128)(2,1)}, u32[]{:S(2)}, u32[]{:S(2)}) async-start(bf16[128,16,128]{2,1,0:T(8,128)(2,1)} %select_add_fusion), calls=%async_computation | async-start | bytes 1048576 | tf_op jit(solution)/shard_map/all_to_all | solution.py:658
  29.2 1.6 broadcast_add_fusion.9
  30.8 2.6 %collective-permute-start.4 = (bf16[48,1536]{1,0:T(8,128)(2,1)}, bf16[48,1536]{1,0:T(8,128)(2,1)}, u32[]{:S(2)}, u32[]{:S(2)}) collective-permute-start(bf16[48,1536]{1,0:T(8,128)(2,1)} %broadcast_add_fusion.9), channel_id=1, source_target_pairs={{0,6},{1,25},{2,4},{3,27},{4,2},{5,29},{6,0},{7,31},{8,14},{9,17},... | collective-permute-start | bytes 442376 | tf_op jit(solution)/shard_map/ppermute | solution.py:540
  34.1 1.2 pad_maximum_fusion.1
  35.3 3.3 %collective-permute-start.5 = (bf16[2,2,48,3072]{3,2,1,0:T(8,128)(2,1)}, bf16[2,2,48,3072]{3,2,1,0:T(8,128)(2,1)S(1)}, u32[]{:S(2)}, u32[]{:S(2)}) collective-permute-start(bf16[2,2,48,3072]{3,2,1,0:T(8,128)(2,1)} %pad_maximum_fusion.1), channel_id=1, source_target_pairs={{0,24},{1,7},{2,26},{3,5},{4,28},{5,3},{6,30},{7,1},{8,16},{9,15},... | collective-permute-start | bytes 3538952 | tf_op jit(solution)/shard_map/ppermute | solution.py:540
  39.7 1.8 all-to-all-done
  41.5 1.4 copy-done.28
  44.7 5.7 %stem.1 = (f32[512,1536]{1,0:T(8,128)S(1)}, bf16[512,1536]{1,0:T(8,128)(2,1)S(1)}, bf16[512,1536]{1,0:T(8,128)(2,1)S(1)}, bf16[1536,512]{1,0:T(8,128)(2,1)S(1)},...) custom-call(bf16[2,48,3072]{2,1,0:T(8,128)(2,1)S(1)} %collective-permute-done.1.unused.refs_1_,, ...), custom_call_target="tpu_custom_call" | custom-call | flops 805306368 | bytes 14680064 | tf_op jit(solution)/shard_map/stem/pallas_call | solution.py:393
  50.4 1.7 copy-done.47
  55.6 1.6 collective-permute-start.17
  62.2 1.2 collective-permute-start.10
  63.6 3.0 %collective-permute-start.11 = (bf16[4,48,1536]{2,1,0:T(8,128)(2,1)S(1)}, bf16[4,48,1536]{2,1,0:T(8,128)(2,1)S(1)}, u32[]{:S(2)}, u32[]{:S(2)}) collective-permute-start(bf16[4,48,1536]{2,1,0:T(8,128)(2,1)S(1)} %maximum_add_fusion.refs_0_), channel_id=1, source_target_pairs={{0,16},{1,5},{2,18},{3,7},{4,20},{5,1},{6,22},{7,3},{8,24},{9,13},... | collective-permute-start | bytes 1769480 | tf_op jit(solution)/shard_map/ppermute | solution.py:540
  67.6 13.7 %gate.1 = (f32[512,1536]{1,0:T(8,128)S(1)}, f32[512,1536]{1,0:T(8,128)S(1)}, f32[512,1536]{1,0:T(8,128)S(1)}) custom-call(s32[32]{0:T(128)S(1)} %pad_add_fusion.offsets, s32[4]{0:T(128)S(1)} %copy-done.27, bf16[4,48,3072]{2,1,0:T(8,128)(2,1)S(1)} %get-tuple-element.78.refs_0_, bf16[2,48,3072]{2,1,0:T(8,128)(2,1)S(1)} %collective-permute-done.1.unused.refs_1_, ...), custom_call_target="tpu_custom_call" | custom-call | flops 4831838208 | bytes 23068672 | tf_op jit(solution)/shard_map/gate/pallas_call | solution.py:393
  81.4 1.7 copy-done.51
  83.1 1.7 copy-done.53
  86.9 6.1 %out_grad.1 = (bf16[16,48,1536]{2,1,0:T(8,128)(2,1)S(1)}, bf16[16,48,1536]{2,1,0:T(8,128)(2,1)S(1)}, bf16[512,1536]{1,0:T(8,128)(2,1)S(1)}) custom-call(s32[33]{0:T(128)S(1)} %pad_add_fusion.1.slots, bf16[4,48,1536]{2,1,0:T(8,128)(2,1)S(1)} %collective-permute-done.10.unused_1.refs_1_, bf16[4,48,1536]{2,1,0:T(8,128)(2,1)S(1)} %collective-permute-done.11.unused_2.refs_2_, ...), custom_call_target="tpu_custom_call" | custom-call | flops 38654705664 | bytes 184549376 | tf_op jit(solution)/shard_map/out_grad/pallas_call | solution.py:393
  94.8 14.3 %middle.1 = (f32[512,1536]{1,0:T(8,128)S(1)}, f32[1,1536]{1,0:T(1,128)S(1)}) custom-call(s32[32]{0:T(128)S(1)} %pad_add_fusion.offsets, bf16[4,48,1536]{2,1,0:T(8,128)(2,1)S(1)} %maximum_add_fusion.refs_0_, bf16[4,48,1536]{2,1,0:T(8,128)(2,1)S(1)} %collective-permute-done.10.unused_1.refs_1_, ...), custom_call_target="tpu_custom_call" | custom-call | flops 38654705664 | bytes 218103808 | tf_op jit(solution)/shard_map/middle/pallas_call | solution.py:393
  109.8 2.6 %collective-permute-start.25 = (bf16[4,48,1536]{2,1,0:T(8,128)(2,1)S(1)}, bf16[4,48,1536]{2,1,0:T(8,128)(2,1)S(1)}, u32[]{:S(2)}, u32[]{:S(2)}) collective-permute-start(bf16[4,48,1536]{2,1,0:T(8,128)(2,1)S(1)} %get-tuple-element.72.unused_2), channel_id=1, source_target_pairs={{0,4},{1,17},{2,6},{3,19},{4,0},{5,21},{6,2},{7,23},{8,12},{9,25},... | collective-permute-start | bytes 1769480 | tf_op jit(solution)/shard_map/ppermute | solution.py:540
  112.4 1.2 collective-permute-start.26
  113.7 1.9 copy-done.54
  115.6 9.8 %conv_back.2 = (bf16[512,1024]{1,0:T(8,128)(2,1)S(1)}, bf16[512,1024]{1,0:T(8,128)(2,1)S(1)}, bf16[16,48,2048]{2,1,0:T(8,128)(2,1)S(1)}, bf16[16,48,2048]{2,1,0:T(8,128)(2,1)S(1)}, f32[32,1024]{1,0:T(8,128)S(1)}) custom-call(s32[33]{0:T(128)S(1)} %pad_add_fusion.1.slots, s32[4]{0:T(128)S(1)} %copy-done.27, ...), custom_call_target="tpu_custom_call" | custom-call | flops 51539607552 | bytes 246065824 | tf_op jit(solution)/shard_map/conv_back/pallas_call | solution.py:393
  126.5 5.0 %conv_back.3 = (bf16[512,512]{1,0:T(8,128)(2,1)S(1)}, bf16[512,512]{1,0:T(8,128)(2,1)S(1)}, bf16[16,48,1024]{2,1,0:T(8,128)(2,1)S(1)}, bf16[16,48,1024]{2,1,0:T(8,128)(2,1)S(1)}, f32[32,512]{1,0:T(8,128)S(1)}) custom-call(s32[33]{0:T(128)S(1)} %pad_add_fusion.1.slots, s32[4]{0:T(128)S(1)} %copy-done.27, bf16[4,48,1536]{2,1,0:T(8,128)(2,1)S(1)} %get-tuple-element.73.unused_1, ...), custom_call_target="tpu_custom_call" | custom-call | flops 25769803776 | bytes 123032912 | tf_op jit(solution)/shard_map/conv_back/pallas_call | solution.py:393
  136.1 2.9 %collective-permute-done.31 = f32[16,1536]{1,0:T(8,128)S(1)} collective-permute-done((f32[16,1536]{1,0:T(8,128)S(1)}, f32[16,1536]{1,0:T(8,128)S(1)}, u32[]{:S(2)}, u32[]{:S(2)}) %collective-permute-start.31) | collective-permute-done | bytes 98336 | tf_op jit(solution)/shard_map/ppermute | solution.py:540
  139.8 3.0 %chip_sum.1 = (bf16[4,48,3072]{2,1,0:T(8,128)(2,1)S(1)}, bf16[4,48,3072]{2,1,0:T(8,128)(2,1)}, bf16[4,48,3072]{2,1,0:T(8,128)(2,1)}, bf16[4,48,3072]{2,1,0:T(8,128)(2,1)}) custom-call(bf16[4,4,48,2048]{3,2,1,0:T(8,128)(2,1)S(1)} %bitcast.53, bf16[4,4,48,2048]{3,2,1,0:T(8,128)(2,1)S(1)} %bitcast.54, bf16[4,4,48,1024]{3,2,1,0:T(8,128)(2,1)S(1)} %bitcast.57, ...), custom_call_target="tpu_custom_call" | custom-call | flops 2359296 | bytes 14680064 | tf_op jit(solution)/shard_map/chip_sum/pallas_call | solution.py:393
  142.8 1.5 collective-permute-start.30
  144.3 1.7 collective-permute-start.28
  147.2 16.7 %stem_back.1 = (f32[1,1536]{1,0:T(1,128)S(1)}, f32[16,48]{1,0:T(8,128)S(1)}) custom-call(s32[32]{0:T(128)S(1)} %pad_add_fusion.offsets, s32[4]{0:T(128)S(1)} %copy-done.27, bf16[4,48,3072]{2,1,0:T(8,128)(2,1)S(1)} %copy-done.16, bf16[2,48,3072]{2,1,0:T(8,128)(2,1)S(1)} %collective-permute-done.1.unused.refs_1_, ...), custom_call_target="tpu_custom_call" | custom-call | flops 77309411328 | bytes 335544320 | tf_op jit(solution)/shard_map/stem_back/pallas_call | solution.py:393
  166.0 2.3 %add_convert_fusion.1 = bf16[4,48,1536]{2,1,0:T(8,128)(2,1)S(1)} fusion(bf16[4,48,1536]{2,1,0:T(8,128)(2,1)} %copy-done.71, bf16[4,48,1536]{2,1,0:T(8,128)(2,1)} %copy-done.70, bf16[4,48,1536]{2,1,0:T(8,128)(2,1)} %copy-done.69, bf16[16,48,1536]{2,1,0:T(8,128)(2,1)} %copy-done.59, f32[]{:T(128)} %bitcast.29, bf16[16,48,1536]{2,1,0:T(8,128)(2,1)} %copy-done.10), kind=kLoop, calls=%fused_computation.6 | loop fusion | flops 3833856 | bytes 3538948 | tf_op jit(solution)/shard_map/convert_element_type | solution.py:691
  168.3 4.0 %collective-permute-done.30 = bf16[4,48,3072]{2,1,0:T(8,128)(2,1)} collective-permute-done((bf16[4,48,3072]{2,1,0:T(8,128)(2,1)}, bf16[4,48,3072]{2,1,0:T(8,128)(2,1)}, u32[]{:S(2)}, u32[]{:S(2)}) %collective-permute-start.30) | collective-permute-done | bytes 1179680 | tf_op jit(solution)/shard_map/ppermute | solution.py:540
  172.9 2.8 %add_convert_fusion = bf16[4,48,3072]{2,1,0:T(8,128)(2,1)S(1)} fusion(bf16[4,48,3072]{2,1,0:T(8,128)(2,1)} %collective-permute-done.30, bf16[4,48,3072]{2,1,0:T(8,128)(2,1)} %collective-permute-done.29, bf16[4,48,3072]{2,1,0:T(8,128)(2,1)} %collective-permute-done.28, bf16[4,48,3072]{2,1,0:T(8,128)(2,1)S(1)} %copy-done.18, f32[]{:T(128)} %bitcast.29), kind=kLoop, calls=%fused_computation.1 | loop fusion | flops 5308416 | bytes 5898244 | tf_op jit(solution)/shard_map/convert_element_type | solution.py:691
  177.1 2.9 %collective-permute-start.34 = (bf16[56,4608]{1,0:T(8,128)(2,1)}, bf16[56,4608]{1,0:T(8,128)(2,1)S(1)}, u32[]{:S(2)}, u32[]{:S(2)}) collective-permute-start(bf16[56,4608]{1,0:T(8,128)(2,1)} %get-tuple-element.75), channel_id=1, source_target_pairs={{0,24},{1,7},{2,26},{3,5},{4,28},{5,3},{6,30},{7,1},{8,16},{9,15},... | collective-permute-start | bytes 1548296 | tf_op jit(solution)/shard_map/ppermute | solution.py:540
  180.7 11.7 %mixed.1 = bf16[512,1536]{1,0:T(8,128)(2,1)} custom-call(s32[32]{0:T(128)S(1)} %pad_add_fusion.offsets, s32[4]{0:T(128)S(1)} %copy-done.27, bf16[4,48,1536]{2,1,0:T(8,128)(2,1)S(1)} %copy-done.3, bf16[4,48,1536]{2,1,0:T(8,128)(2,1)S(1)} %copy-done.5, bf16[4,48,1536]{2,1,0:T(8,128)(2,1)S(1)} %copy-done.7, bf16[4,48,1536]{2,1,0:T(8,128)(2,1)S(1)} %copy-done.9, ...), custom_call_target="tpu_custom_call" | custom-call | flops 2415919104 | bytes 10485760 | tf_op jit(solution)/shard_map/mixed/pallas_call | solution.py:393
  192.5 1.2 slice.283
  194.4 1.5 fusion.3
  195.9 2.5 %collective-permute-start.37 = (bf16[56,2304]{1,0:T(8,128)(2,1)S(1)}, bf16[56,2304]{1,0:T(8,128)(2,1)S(1)}, u32[]{:S(2)}, u32[]{:S(2)}) collective-permute-start(bf16[56,2304]{1,0:T(8,128)(2,1)S(1)} %get-tuple-element.85), channel_id=1, source_target_pairs={{0,96},{1,97},{2,98},{3,99},{4,100},{5,101},{6,102},{7,103},{8,104... | collective-permute-start | bytes 774152 | tf_op jit(solution)/shard_map/ppermute | solution.py:540
  198.4 4.6 %collective-permute-done.37 = bf16[56,2304]{1,0:T(8,128)(2,1)S(1)} collective-permute-done((bf16[56,2304]{1,0:T(8,128)(2,1)S(1)}, bf16[56,2304]{1,0:T(8,128)(2,1)S(1)}, u32[]{:S(2)}, u32[]{:S(2)}) %collective-permute-start.37) | collective-permute-done | bytes 258080 | tf_op jit(solution)/shard_map/ppermute | solution.py:540
  204.1 1.6 collective-permute-start.36
  205.7 4.9 %collective-permute-done.36 = bf16[56,2304]{1,0:T(8,128)(2,1)S(1)} collective-permute-done((bf16[56,2304]{1,0:T(8,128)(2,1)S(1)}, bf16[56,2304]{1,0:T(8,128)(2,1)S(1)}, u32[]{:S(2)}, u32[]{:S(2)}) %collective-permute-start.36) | collective-permute-done | bytes 258080 | tf_op jit(solution)/shard_map/ppermute | solution.py:540
  211.0 1.5 collective-permute-start.41
  212.5 1.8 collective-permute-start.39
  215.5 1.7 collective-permute-done.40
  217.3 7.0 %collective-permute-start.42 = (f32[18,1536]{1,0:T(8,128)S(1)}, f32[18,1536]{1,0:T(8,128)S(1)}, u32[]{:S(2)}, u32[]{:S(2)}) collective-permute-start(f32[18,1536]{1,0:T(8,128)S(1)} %convert_add_fusion.3), channel_id=1, source_target_pairs={{0,1},{1,0},{2,3},{3,2},{4,5},{5,4},{6,7},{7,6},{8,9},{9,8},{10,11... | collective-permute-start | bytes 331784 | tf_op jit(solution)/shard_map/ppermute | solution.py:540
  (284 shorter events, 36.5 us)
Async XLA Ops:
  0.7 8.9 %collective-permute-start = (bf16[48,3072]{1,0:T(8,128)(2,1)}, bf16[48,3072]{1,0:T(8,128)(2,1)S(1)}, u32[]{:S(2)}, u32[]{:S(2)}) collective-permute-start(bf16[48,3072]{1,0:T(8,128)(2,1)} %param.25), channel_id=1, source_target_pairs={{0,2},{1,9},{2,0},{3,11},{4,6},{5,13},{6,4},{7,15},{8,10},{9,1},{1... | collective-permute-start | bytes 884744 | tf_op jit(solution)/shard_map/ppermute | solution.py:540
  2.9 9.2 %collective-permute-start.7 = (bf16[48,3072]{1,0:T(8,128)(2,1)}, bf16[48,3072]{1,0:T(8,128)(2,1)S(1)}, u32[]{:S(2)}, u32[]{:S(2)}) collective-permute-start(bf16[48,3072]{1,0:T(8,128)(2,1)} %param.25), channel_id=1, source_target_pairs={{0,6},{1,25},{2,4},{3,27},{4,2},{5,29},{6,0},{7,31},{8,14},{9,17},... | collective-permute-start | bytes 884744 | tf_op jit(solution)/shard_map/ppermute | solution.py:540
  4.8 8.5 %collective-permute-start.6 = (bf16[48,3072]{1,0:T(8,128)(2,1)}, bf16[48,3072]{1,0:T(8,128)(2,1)S(1)}, u32[]{:S(2)}, u32[]{:S(2)}) collective-permute-start(bf16[48,3072]{1,0:T(8,128)(2,1)} %param.25), channel_id=1, source_target_pairs={{0,4},{1,17},{2,6},{3,19},{4,0},{5,21},{6,2},{7,23},{8,12},{9,25},... | collective-permute-start | bytes 884744 | tf_op jit(solution)/shard_map/ppermute | solution.py:540
  10.4 17.6 %collective-permute-start.1 = (bf16[2,48,3072]{2,1,0:T(8,128)(2,1)}, bf16[2,48,3072]{2,1,0:T(8,128)(2,1)S(1)}, u32[]{:S(2)}, u32[]{:S(2)}) collective-permute-start(bf16[2,48,3072]{2,1,0:T(8,128)(2,1)} %get-tuple-element.82), channel_id=1, source_target_pairs={{0,8},{1,3},{2,10},{3,1},{4,12},{5,7},{6,14},{7,5},{8,0},{9,11},{1... | collective-permute-start | bytes 1769480 | tf_op jit(solution)/shard_map/ppermute | solution.py:540
  14.2 24.4 %collective-permute-start.8 = (bf16[2,48,3072]{2,1,0:T(8,128)(2,1)}, bf16[2,48,3072]{2,1,0:T(8,128)(2,1)S(1)}, u32[]{:S(2)}, u32[]{:S(2)}) collective-permute-start(bf16[2,48,3072]{2,1,0:T(8,128)(2,1)} %get-tuple-element.80), channel_id=1, source_target_pairs={{0,24},{1,7},{2,26},{3,5},{4,28},{5,3},{6,30},{7,1},{8,16},{9,15},... | collective-permute-start | bytes 1769480 | tf_op jit(solution)/shard_map/ppermute | solution.py:540
  19.9 21.6 %all-to-all-start = ((bf16[128,16,128]{2,1,0:T(8,128)(2,1)}), bf16[128,16,128]{2,1,0:T(8,128)(2,1)}, u32[]{:S(2)}, u32[]{:S(2)}) async-start(bf16[128,16,128]{2,1,0:T(8,128)(2,1)} %select_add_fusion), calls=%async_computation | async-start | bytes 1048576 | tf_op jit(solution)/shard_map/all_to_all | solution.py:658
  30.8 26.7 %collective-permute-start.4 = (bf16[48,1536]{1,0:T(8,128)(2,1)}, bf16[48,1536]{1,0:T(8,128)(2,1)}, u32[]{:S(2)}, u32[]{:S(2)}) collective-permute-start(bf16[48,1536]{1,0:T(8,128)(2,1)} %broadcast_add_fusion.9), channel_id=1, source_target_pairs={{0,6},{1,25},{2,4},{3,27},{4,2},{5,29},{6,0},{7,31},{8,14},{9,17},... | collective-permute-start | bytes 442376 | tf_op jit(solution)/shard_map/ppermute | solution.py:540
  33.5 24.2 %collective-permute-start.3 = (bf16[48,1536]{1,0:T(8,128)(2,1)}, bf16[48,1536]{1,0:T(8,128)(2,1)}, u32[]{:S(2)}, u32[]{:S(2)}) collective-permute-start(bf16[48,1536]{1,0:T(8,128)(2,1)} %broadcast_add_fusion.9), channel_id=1, source_target_pairs={{0,4},{1,17},{2,6},{3,19},{4,0},{5,21},{6,2},{7,23},{8,12},{9,25},... | collective-permute-start | bytes 442376 | tf_op jit(solution)/shard_map/ppermute | solution.py:540
  34.0 24.2 %collective-permute-start.2 = (bf16[48,1536]{1,0:T(8,128)(2,1)}, bf16[48,1536]{1,0:T(8,128)(2,1)}, u32[]{:S(2)}, u32[]{:S(2)}) collective-permute-start(bf16[48,1536]{1,0:T(8,128)(2,1)} %broadcast_add_fusion.9), channel_id=1, source_target_pairs={{0,2},{1,9},{2,0},{3,11},{4,6},{5,13},{6,4},{7,15},{8,10},{9,1},{1... | collective-permute-start | bytes 442376 | tf_op jit(solution)/shard_map/ppermute | solution.py:540
  35.3 19.7 %collective-permute-start.5 = (bf16[2,2,48,3072]{3,2,1,0:T(8,128)(2,1)}, bf16[2,2,48,3072]{3,2,1,0:T(8,128)(2,1)S(1)}, u32[]{:S(2)}, u32[]{:S(2)}) collective-permute-start(bf16[2,2,48,3072]{3,2,1,0:T(8,128)(2,1)} %pad_maximum_fusion.1), channel_id=1, source_target_pairs={{0,24},{1,7},{2,26},{3,5},{4,28},{5,3},{6,30},{7,1},{8,16},{9,15},... | collective-permute-start | bytes 3538952 | tf_op jit(solution)/shard_map/ppermute | solution.py:540
  39.7 15.9 %collective-permute-start.9 = (bf16[2,2,48,3072]{3,2,1,0:T(8,128)(2,1)}, bf16[2,2,48,3072]{3,2,1,0:T(8,128)(2,1)S(1)}, u32[]{:S(2)}, u32[]{:S(2)}) collective-permute-start(bf16[2,2,48,3072]{3,2,1,0:T(8,128)(2,1)} %pad_maximum_fusion.2), channel_id=1, source_target_pairs={{0,8},{1,3},{2,10},{3,1},{4,12},{5,7},{6,14},{7,5},{8,0},{9,11},{1... | collective-permute-start | bytes 3538952 | tf_op jit(solution)/shard_map/ppermute | solution.py:540
  52.1 42.7 %copy-start.48 = (bf16[512,1536]{1,0:T(8,128)(2,1)}, bf16[512,1536]{1,0:T(8,128)(2,1)S(1)}, u32[]{:S(2)}) copy-start(bf16[512,1536]{1,0:T(8,128)(2,1)S(1)} %get-tuple-element.41.mix_grad.refs_9_.refs_19_) | copy-start | bytes 4718596
  52.1 94.0 %copy-start.11 = (bf16[512,1536]{1,0:T(8,128)(2,1)}, bf16[512,1536]{1,0:T(8,128)(2,1)S(1)}, u32[]{:S(2)}) copy-start(bf16[512,1536]{1,0:T(8,128)(2,1)S(1)} %get-tuple-element.60.refs_17_.refs_10_) | copy-start | bytes 4718596
  55.0 11.6 %collective-permute-start.14 = (bf16[4,48,3072]{2,1,0:T(8,128)(2,1)S(1)}, bf16[4,48,3072]{2,1,0:T(8,128)(2,1)S(1)}, u32[]{:S(2)}, u32[]{:S(2)}) collective-permute-start(bf16[4,48,3072]{2,1,0:T(8,128)(2,1)S(1)} %get-tuple-element.77), channel_id=1, source_target_pairs={{0,1},{1,0},{2,3},{3,2},{4,5},{5,4},{6,7},{7,6},{8,9},{9,8},{10,11... | collective-permute-start | bytes 3538952 | tf_op jit(solution)/shard_map/ppermute | solution.py:540
  55.6 11.1 %collective-permute-start.17 = (bf16[4,48,3072]{2,1,0:T(8,128)(2,1)S(1)}, bf16[4,48,3072]{2,1,0:T(8,128)(2,1)S(1)}, u32[]{:S(2)}, u32[]{:S(2)}) collective-permute-start(bf16[4,48,3072]{2,1,0:T(8,128)(2,1)S(1)} %broadcast_add_fusion.2), channel_id=1, source_target_pairs={{0,1},{1,0},{2,3},{3,2},{4,5},{5,4},{6,7},{7,6},{8,9},{9,8},{10,11... | collective-permute-start | bytes 3538952 | tf_op jit(solution)/shard_map/ppermute | solution.py:540
  57.5 10.1 %collective-permute-start.18 = (bf16[4,48,3072]{2,1,0:T(8,128)(2,1)S(1)}, bf16[4,48,3072]{2,1,0:T(8,128)(2,1)S(1)}, u32[]{:S(2)}, u32[]{:S(2)}) collective-permute-start(bf16[4,48,3072]{2,1,0:T(8,128)(2,1)S(1)} %broadcast_add_fusion.1), channel_id=1, source_target_pairs={{0,1},{1,0},{2,3},{3,2},{4,5},{5,4},{6,7},{7,6},{8,9},{9,8},{10,11... | collective-permute-start | bytes 3538952 | tf_op jit(solution)/shard_map/ppermute | solution.py:540
  57.7 4.6 %collective-permute-start.15 = (bf16[2,48,3072]{2,1,0:T(8,128)(2,1)S(1)}, bf16[2,48,3072]{2,1,0:T(8,128)(2,1)S(1)}, u32[]{:S(2)}, u32[]{:S(2)}) collective-permute-start(bf16[2,48,3072]{2,1,0:T(8,128)(2,1)S(1)} %broadcast_add_fusion.8), channel_id=1, source_target_pairs={{0,1},{1,0},{2,3},{3,2},{4,5},{5,4},{6,7},{7,6},{8,9},{9,8},{10,11... | collective-permute-start | bytes 1769480 | tf_op jit(solution)/shard_map/ppermute | solution.py:540
  58.2 5.4 %collective-permute-start.16 = (bf16[2,48,3072]{2,1,0:T(8,128)(2,1)S(1)}, bf16[2,48,3072]{2,1,0:T(8,128)(2,1)S(1)}, u32[]{:S(2)}, u32[]{:S(2)}) collective-permute-start(bf16[2,48,3072]{2,1,0:T(8,128)(2,1)S(1)} %broadcast_add_fusion.7), channel_id=1, source_target_pairs={{0,1},{1,0},{2,3},{3,2},{4,5},{5,4},{6,7},{7,6},{8,9},{9,8},{10,11... | collective-permute-start | bytes 1769480 | tf_op jit(solution)/shard_map/ppermute | solution.py:540
  61.8 32.9 %copy-start.2 = (bf16[4,48,1536]{2,1,0:T(8,128)(2,1)}, bf16[4,48,1536]{2,1,0:T(8,128)(2,1)S(1)}, u32[]{:S(2)}) copy-start(bf16[4,48,1536]{2,1,0:T(8,128)(2,1)S(1)} %maximum_add_fusion.refs_0_) | copy-start | bytes 1769476
  62.2 23.7 %collective-permute-start.10 = (bf16[4,48,1536]{2,1,0:T(8,128)(2,1)S(1)}, bf16[4,48,1536]{2,1,0:T(8,128)(2,1)S(1)}, u32[]{:S(2)}, u32[]{:S(2)}) collective-permute-start(bf16[4,48,1536]{2,1,0:T(8,128)(2,1)S(1)} %maximum_add_fusion.refs_0_), channel_id=1, source_target_pairs={{0,8},{1,3},{2,10},{3,1},{4,12},{5,7},{6,14},{7,5},{8,0},{9,11},{1... | collective-permute-start | bytes 1769480 | tf_op jit(solution)/shard_map/ppermute | solution.py:540
  63.6 22.5 %collective-permute-start.11 = (bf16[4,48,1536]{2,1,0:T(8,128)(2,1)S(1)}, bf16[4,48,1536]{2,1,0:T(8,128)(2,1)S(1)}, u32[]{:S(2)}, u32[]{:S(2)}) collective-permute-start(bf16[4,48,1536]{2,1,0:T(8,128)(2,1)S(1)} %maximum_add_fusion.refs_0_), channel_id=1, source_target_pairs={{0,16},{1,5},{2,18},{3,7},{4,20},{5,1},{6,22},{7,3},{8,24},{9,13},... | collective-permute-start | bytes 1769480 | tf_op jit(solution)/shard_map/ppermute | solution.py:540
  66.6 20.1 %collective-permute-start.12 = (bf16[4,48,1536]{2,1,0:T(8,128)(2,1)S(1)}, bf16[4,48,1536]{2,1,0:T(8,128)(2,1)S(1)}, u32[]{:S(2)}, u32[]{:S(2)}) collective-permute-start(bf16[4,48,1536]{2,1,0:T(8,128)(2,1)S(1)} %maximum_add_fusion.refs_0_), channel_id=1, source_target_pairs={{0,24},{1,7},{2,26},{3,5},{4,28},{5,3},{6,30},{7,1},{8,16},{9,15},... | collective-permute-start | bytes 1769480 | tf_op jit(solution)/shard_map/ppermute | solution.py:540
  66.7 28.0 %collective-permute-start.13 = (bf16[4,48,1536]{2,1,0:T(8,128)(2,1)S(1)}, bf16[4,48,1536]{2,1,0:T(8,128)(2,1)S(1)}, u32[]{:S(2)}, u32[]{:S(2)}) collective-permute-start(bf16[4,48,1536]{2,1,0:T(8,128)(2,1)S(1)} %maximum_add_fusion.refs_0_), channel_id=1, source_target_pairs={{0,1},{1,0},{2,3},{3,2},{4,5},{5,4},{6,7},{7,6},{8,9},{9,8},{10,11... | collective-permute-start | bytes 1769480 | tf_op jit(solution)/shard_map/ppermute | solution.py:540
  86.0 8.7 %collective-permute-start.19 = (bf16[4,48,1536]{2,1,0:T(8,128)(2,1)S(1)}, bf16[4,48,1536]{2,1,0:T(8,128)(2,1)S(1)}, u32[]{:S(2)}, u32[]{:S(2)}) collective-permute-start(bf16[4,48,1536]{2,1,0:T(8,128)(2,1)S(1)} %broadcast_add_fusion.6), channel_id=1, source_target_pairs={{0,1},{1,0},{2,3},{3,2},{4,5},{5,4},{6,7},{7,6},{8,9},{9,8},{10,11... | collective-permute-start | bytes 1769480 | tf_op jit(solution)/shard_map/ppermute | solution.py:540
  86.2 8.5 %collective-permute-start.20 = (bf16[4,48,1536]{2,1,0:T(8,128)(2,1)S(1)}, bf16[4,48,1536]{2,1,0:T(8,128)(2,1)S(1)}, u32[]{:S(2)}, u32[]{:S(2)}) collective-permute-start(bf16[4,48,1536]{2,1,0:T(8,128)(2,1)S(1)} %broadcast_add_fusion.5), channel_id=1, source_target_pairs={{0,1},{1,0},{2,3},{3,2},{4,5},{5,4},{6,7},{7,6},{8,9},{9,8},{10,11... | collective-permute-start | bytes 1769480 | tf_op jit(solution)/shard_map/ppermute | solution.py:540
  86.8 7.9 %collective-permute-start.21 = (bf16[4,48,1536]{2,1,0:T(8,128)(2,1)S(1)}, bf16[4,48,1536]{2,1,0:T(8,128)(2,1)S(1)}, u32[]{:S(2)}, u32[]{:S(2)}) collective-permute-start(bf16[4,48,1536]{2,1,0:T(8,128)(2,1)S(1)} %broadcast_add_fusion.4), channel_id=1, source_target_pairs={{0,1},{1,0},{2,3},{3,2},{4,5},{5,4},{6,7},{7,6},{8,9},{9,8},{10,11... | collective-permute-start | bytes 1769480 | tf_op jit(solution)/shard_map/ppermute | solution.py:540
  94.2 14.9 %collective-permute-start.22 = (bf16[16,48,1536]{2,1,0:T(8,128)(2,1)S(1)}, bf16[16,48,1536]{2,1,0:T(8,128)(2,1)S(1)}, u32[]{:S(2)}, u32[]{:S(2)}) collective-permute-start(bf16[16,48,1536]{2,1,0:T(8,128)(2,1)S(1)} %get-tuple-element.43), channel_id=1, source_target_pairs={{0,1},{1,0},{2,3},{3,2},{4,5},{5,4},{6,7},{7,6},{8,9},{9,8},{10,11... | collective-permute-start | bytes 7077896 | tf_op jit(solution)/shard_map/ppermute | solution.py:540
  109.7 21.9 %collective-permute-start.24 = (bf16[4,48,1536]{2,1,0:T(8,128)(2,1)S(1)}, bf16[4,48,1536]{2,1,0:T(8,128)(2,1)S(1)}, u32[]{:S(2)}, u32[]{:S(2)}) collective-permute-start(bf16[4,48,1536]{2,1,0:T(8,128)(2,1)S(1)} %get-tuple-element.73.unused_1), channel_id=1, source_target_pairs={{0,2},{1,9},{2,0},{3,11},{4,6},{5,13},{6,4},{7,15},{8,10},{9,1},{1... | collective-permute-start | bytes 1769480 | tf_op jit(solution)/shard_map/ppermute | solution.py:540
  109.8 22.4 %collective-permute-start.25 = (bf16[4,48,1536]{2,1,0:T(8,128)(2,1)S(1)}, bf16[4,48,1536]{2,1,0:T(8,128)(2,1)S(1)}, u32[]{:S(2)}, u32[]{:S(2)}) collective-permute-start(bf16[4,48,1536]{2,1,0:T(8,128)(2,1)S(1)} %get-tuple-element.72.unused_2), channel_id=1, source_target_pairs={{0,4},{1,17},{2,6},{3,19},{4,0},{5,21},{6,2},{7,23},{8,12},{9,25},... | collective-permute-start | bytes 1769480 | tf_op jit(solution)/shard_map/ppermute | solution.py:540
  112.4 21.6 %collective-permute-start.26 = (bf16[4,48,1536]{2,1,0:T(8,128)(2,1)S(1)}, bf16[4,48,1536]{2,1,0:T(8,128)(2,1)S(1)}, u32[]{:S(2)}, u32[]{:S(2)}) collective-permute-start(bf16[4,48,1536]{2,1,0:T(8,128)(2,1)S(1)} %get-tuple-element.71.unused_3), channel_id=1, source_target_pairs={{0,6},{1,25},{2,4},{3,27},{4,2},{5,29},{6,0},{7,31},{8,14},{9,17},... | collective-permute-start | bytes 1769480 | tf_op jit(solution)/shard_map/ppermute | solution.py:540
  125.3 14.4 %collective-permute-start.23 = (bf16[16,48,2048]{2,1,0:T(8,128)(2,1)S(1)}, bf16[16,48,2048]{2,1,0:T(8,128)(2,1)S(1)}, u32[]{:S(2)}, u32[]{:S(2)}) collective-permute-start(bf16[16,48,2048]{2,1,0:T(8,128)(2,1)S(1)} %get-tuple-element.49), channel_id=1, source_target_pairs={{0,1},{1,0},{2,3},{3,2},{4,5},{5,4},{6,7},{7,6},{8,9},{9,8},{10,11... | collective-permute-start | bytes 9437192 | tf_op jit(solution)/shard_map/ppermute | solution.py:540
  135.4 4.3 %collective-permute-start.27 = (bf16[16,48,1024]{2,1,0:T(8,128)(2,1)S(1)}, bf16[16,48,1024]{2,1,0:T(8,128)(2,1)S(1)}, u32[]{:S(2)}, u32[]{:S(2)}) collective-permute-start(bf16[16,48,1024]{2,1,0:T(8,128)(2,1)S(1)} %broadcast_add_fusion), channel_id=1, source_target_pairs={{0,1},{1,0},{2,3},{3,2},{4,5},{5,4},{6,7},{7,6},{8,9},{9,8},{10,11... | collective-permute-start | bytes 4718600 | tf_op jit(solution)/shard_map/ppermute | solution.py:540
  135.6 3.5 %collective-permute-start.31 = (f32[16,1536]{1,0:T(8,128)S(1)}, f32[16,1536]{1,0:T(8,128)S(1)}, u32[]{:S(2)}, u32[]{:S(2)}) collective-permute-start(f32[16,1536]{1,0:T(8,128)S(1)} %broadcast_select_fusion), channel_id=1, source_target_pairs={{0,1},{1,0},{2,3},{3,2},{4,5},{5,4},{6,7},{7,6},{8,9},{9,8},{10,11... | collective-permute-start | bytes 294920 | tf_op jit(solution)/shard_map/ppermute | solution.py:540
  142.8 21.1 %copy-start.17 = (bf16[4,48,3072]{2,1,0:T(8,128)(2,1)}, bf16[4,48,3072]{2,1,0:T(8,128)(2,1)S(1)}, u32[]{:S(2)}) copy-start(bf16[4,48,3072]{2,1,0:T(8,128)(2,1)S(1)} %get-tuple-element.52) | copy-start | bytes 3538948
  142.8 29.5 %collective-permute-start.30 = (bf16[4,48,3072]{2,1,0:T(8,128)(2,1)}, bf16[4,48,3072]{2,1,0:T(8,128)(2,1)}, u32[]{:S(2)}, u32[]{:S(2)}) collective-permute-start(bf16[4,48,3072]{2,1,0:T(8,128)(2,1)} %get-tuple-element.55.refs_16_), channel_id=1, source_target_pairs={{0,6},{1,25},{2,4},{3,27},{4,2},{5,29},{6,0},{7,31},{8,14},{9,17},... | collective-permute-start | bytes 3538952 | tf_op jit(solution)/shard_map/ppermute | solution.py:540
  144.3 28.0 %collective-permute-start.29 = (bf16[4,48,3072]{2,1,0:T(8,128)(2,1)}, bf16[4,48,3072]{2,1,0:T(8,128)(2,1)}, u32[]{:S(2)}, u32[]{:S(2)}) collective-permute-start(bf16[4,48,3072]{2,1,0:T(8,128)(2,1)} %get-tuple-element.54.refs_15_), channel_id=1, source_target_pairs={{0,4},{1,17},{2,6},{3,19},{4,0},{5,21},{6,2},{7,23},{8,12},{9,25},... | collective-permute-start | bytes 3538952 | tf_op jit(solution)/shard_map/ppermute | solution.py:540
  144.3 28.6 %collective-permute-start.28 = (bf16[4,48,3072]{2,1,0:T(8,128)(2,1)}, bf16[4,48,3072]{2,1,0:T(8,128)(2,1)}, u32[]{:S(2)}, u32[]{:S(2)}) collective-permute-start(bf16[4,48,3072]{2,1,0:T(8,128)(2,1)} %get-tuple-element.53.refs_14_), channel_id=1, source_target_pairs={{0,2},{1,9},{2,0},{3,11},{4,6},{5,13},{6,4},{7,15},{8,10},{9,1},{1... | collective-permute-start | bytes 3538952 | tf_op jit(solution)/shard_map/ppermute | solution.py:540
  177.1 17.2 %collective-permute-start.34 = (bf16[56,4608]{1,0:T(8,128)(2,1)}, bf16[56,4608]{1,0:T(8,128)(2,1)S(1)}, u32[]{:S(2)}, u32[]{:S(2)}) collective-permute-start(bf16[56,4608]{1,0:T(8,128)(2,1)} %get-tuple-element.75), channel_id=1, source_target_pairs={{0,24},{1,7},{2,26},{3,5},{4,28},{5,3},{6,30},{7,1},{8,16},{9,15},... | collective-permute-start | bytes 1548296 | tf_op jit(solution)/shard_map/ppermute | solution.py:540
  180.1 14.3 %collective-permute-start.33 = (bf16[56,4608]{1,0:T(8,128)(2,1)}, bf16[56,4608]{1,0:T(8,128)(2,1)}, u32[]{:S(2)}, u32[]{:S(2)}) collective-permute-start(bf16[56,4608]{1,0:T(8,128)(2,1)} %get-tuple-element.76), channel_id=1, source_target_pairs={{0,16},{1,5},{2,18},{3,7},{4,20},{5,1},{6,22},{7,3},{8,24},{9,13},... | collective-permute-start | bytes 1548296 | tf_op jit(solution)/shard_map/ppermute | solution.py:540
  180.1 14.3 %collective-permute-start.32 = (bf16[56,4608]{1,0:T(8,128)(2,1)S(1)}, bf16[56,4608]{1,0:T(8,128)(2,1)}, u32[]{:S(2)}, u32[]{:S(2)}) collective-permute-start(bf16[56,4608]{1,0:T(8,128)(2,1)S(1)} %get-tuple-element.74), channel_id=1, source_target_pairs={{0,8},{1,3},{2,10},{3,1},{4,12},{5,7},{6,14},{7,5},{8,0},{9,11},{1... | collective-permute-start | bytes 1548296 | tf_op jit(solution)/shard_map/ppermute | solution.py:540
  195.9 7.1 %collective-permute-start.37 = (bf16[56,2304]{1,0:T(8,128)(2,1)S(1)}, bf16[56,2304]{1,0:T(8,128)(2,1)S(1)}, u32[]{:S(2)}, u32[]{:S(2)}) collective-permute-start(bf16[56,2304]{1,0:T(8,128)(2,1)S(1)} %get-tuple-element.85), channel_id=1, source_target_pairs={{0,96},{1,97},{2,98},{3,99},{4,100},{5,101},{6,102},{7,103},{8,104... | collective-permute-start | bytes 774152 | tf_op jit(solution)/shard_map/ppermute | solution.py:540
  198.4 5.6 %collective-permute-start.35 = (bf16[56,2304]{1,0:T(8,128)(2,1)S(1)}, bf16[56,2304]{1,0:T(8,128)(2,1)S(1)}, u32[]{:S(2)}, u32[]{:S(2)}) collective-permute-start(bf16[56,2304]{1,0:T(8,128)(2,1)S(1)} %get-tuple-element.86), channel_id=1, source_target_pairs={{0,32},{1,33},{2,34},{3,35},{4,36},{5,37},{6,38},{7,39},{8,40},{9,... | collective-permute-start | bytes 774152 | tf_op jit(solution)/shard_map/ppermute | solution.py:540
  204.1 6.5 %collective-permute-start.36 = (bf16[56,2304]{1,0:T(8,128)(2,1)S(1)}, bf16[56,2304]{1,0:T(8,128)(2,1)S(1)}, u32[]{:S(2)}, u32[]{:S(2)}) collective-permute-start(bf16[56,2304]{1,0:T(8,128)(2,1)S(1)} %get-tuple-element.84), channel_id=1, source_target_pairs={{0,96},{1,97},{2,98},{3,99},{4,100},{5,101},{6,102},{7,103},{8,104... | collective-permute-start | bytes 774152 | tf_op jit(solution)/shard_map/ppermute | solution.py:540
  205.7 5.2 %collective-permute-start.38 = (bf16[56,2304]{1,0:T(8,128)(2,1)S(1)}, bf16[56,2304]{1,0:T(8,128)(2,1)S(1)}, u32[]{:S(2)}, u32[]{:S(2)}) collective-permute-start(bf16[56,2304]{1,0:T(8,128)(2,1)S(1)} %get-tuple-element.83), channel_id=1, source_target_pairs={{0,32},{1,33},{2,34},{3,35},{4,36},{5,37},{6,38},{7,39},{8,40},{9,... | collective-permute-start | bytes 774152 | tf_op jit(solution)/shard_map/ppermute | solution.py:540
  211.0 4.5 %collective-permute-start.41 = (bf16[18,1536]{1,0:T(8,128)(2,1)S(1)}, bf16[18,1536]{1,0:T(8,128)(2,1)S(1)}, u32[]{:S(2)}, u32[]{:S(2)}) collective-permute-start(bf16[18,1536]{1,0:T(8,128)(2,1)S(1)} %get-tuple-element.69), channel_id=1, source_target_pairs={{0,6},{1,25},{2,4},{3,27},{4,2},{5,29},{6,0},{7,31},{8,14},{9,17},... | collective-permute-start | bytes 165896 | tf_op jit(solution)/shard_map/ppermute | solution.py:540
  212.5 4.7 %collective-permute-start.40 = (bf16[18,1536]{1,0:T(8,128)(2,1)S(1)}, bf16[18,1536]{1,0:T(8,128)(2,1)S(1)}, u32[]{:S(2)}, u32[]{:S(2)}) collective-permute-start(bf16[18,1536]{1,0:T(8,128)(2,1)S(1)} %get-tuple-element.69), channel_id=1, source_target_pairs={{0,4},{1,17},{2,6},{3,19},{4,0},{5,21},{6,2},{7,23},{8,12},{9,25},... | collective-permute-start | bytes 165896 | tf_op jit(solution)/shard_map/ppermute | solution.py:540
  212.5 4.7 %collective-permute-start.39 = (bf16[18,1536]{1,0:T(8,128)(2,1)S(1)}, bf16[18,1536]{1,0:T(8,128)(2,1)S(1)}, u32[]{:S(2)}, u32[]{:S(2)}) collective-permute-start(bf16[18,1536]{1,0:T(8,128)(2,1)S(1)} %get-tuple-element.69), channel_id=1, source_target_pairs={{0,2},{1,9},{2,0},{3,11},{4,6},{5,13},{6,4},{7,15},{8,10},{9,1},{1... | collective-permute-start | bytes 165896 | tf_op jit(solution)/shard_map/ppermute | solution.py:540
  217.3 8.0 %collective-permute-start.42 = (f32[18,1536]{1,0:T(8,128)S(1)}, f32[18,1536]{1,0:T(8,128)S(1)}, u32[]{:S(2)}, u32[]{:S(2)}) collective-permute-start(f32[18,1536]{1,0:T(8,128)S(1)} %convert_add_fusion.3), channel_id=1, source_target_pairs={{0,1},{1,0},{2,3},{3,2},{4,5},{5,4},{6,7},{7,6},{8,9},{9,8},{10,11... | collective-permute-start | bytes 331784 | tf_op jit(solution)/shard_map/ppermute | solution.py:540
  (74 other events, 473.5 us)

commit v5 on v4

--- a/solution.py
+++ b/solution.py
@@ -506,6 +506,18 @@
     )
 
 
+def nothing(*refs):
+    pass
+
+
+def after(value, *before):
+    return pl.pallas_call(
+        nothing, name="after", out_shape=shaped(value.shape, value.dtype),
+        in_specs=[ANY] * (1 + len(before)), out_specs=ANY, input_output_aliases={0: 0},
+        compiler_params=pltpu.CompilerParams(vmem_limit_bytes=MIB),
+    )(value, *before)
+
+
 def place(x, y, z, c):
     return ((x % 4 * 4 + y % 4) * 4 + z % 4) * 2 + c
 
@@ -620,8 +632,8 @@
 
 
 def scatter_rest(near, follow):
-    close = total_of([near[0]] + [send(near[r], along_second(r)) for r in (1, 2, 3)]) + follow
-    close = close.astype(BF16)
+    got = [send(near[r], along_second(r)) for r in (1, 2, 3)]
+    close = total_of([near[0], after(got[0], follow), *got[1:]]).astype(BF16)
     wide = close.shape[1] // 2
     halves = []
     for half, order in ((close[:, :wide], (1, 3)), (close[:, wide:], (3, 1))):
@@ -676,7 +688,7 @@
         )
         grads.append((value_grad, gate_grad))
         if begin:
-            other = other + sum(zero_of(group) for group in out_groups[1:])
+            other = after(other, *out_groups[1:])
         nears.append((mine, send(other, other_core())))
         convs.append(conv_grad[:TAPS])
     gate_groups = chip_sums(nears)
@@ -694,7 +706,7 @@
     small = jnp.concatenate([small[:8], small[8:16], small[16:]], axis=1).astype(BF16)
     near = jnp.concatenate([near, jnp.broadcast_to(small[None], (4, *small.shape))], axis=1)
     output = mixed_out(offsets, utterance_frames, out_pieces, near, swished, embedded)
-    sums = scatter_rest(near, zero_of(output).astype(F32))
+    sums = scatter_rest(near, output)
     small = sums[ROWS:]
     early, late = finish_small(
         jnp.concatenate([small[:, :D], small[:, D : 2 * D], small[:2, 2 * D :]]), 16, c

time: 228 us -> 223 us (0.978)
  waiting for transfers between devices: 25.3 us -> 31.7 us
  local copies, waits for them, and re-layouts: 24.7 us -> 19.6 us
  between operations: 9.75 us -> 7.19 us
    ppermute x43, waiting for transfers between devices: 23.5 us -> 29.5 us  [send(): return lax.ppermute(values, ALL, where)]
    add x5, other arithmetic: 0.59 us -> 2.98 us  [gather_pieces(): return own + [send(piece + after, other_core()) for piece in own]]
    unnamed x167 -> x155, local copies, waits for them, and re-layouts: 12.8 us -> 10.9 us
    slice x11 -> x7, local copies, waits for them, and re-layouts: 6.42 us -> 4.94 us  [zero_of(): return values[(0,) * values.ndim] * 0]
  transfers between devices with their start and end apart: 44 -> 44, of which waited for: 14 -> 13; matrix products, arithmetic and copies ran while one was open for 11% -> 10% of each run, Pallas kernels for 37% -> 37%
where the time goes in v5:
time: 223 us
  Pallas kernels  85.2 us (38%)
  starting transfers between devices  58.9 us (26%)
  waiting for transfers between devices  31.7 us (14%)
  other arithmetic  20.1 us (9%)
  local copies, waits for them, and re-layouts  19.6 us (9%)
  between operations  7.19 us (3%)
    pallas_call x9, Pallas kernels, call(): pl.pallas_call(kernel, name=name, out_shape=outs, in_specs=in_specs, out_...  85.2 us
    ppermute x43, starting transfers between devices, send(): return lax.ppermute(values, ALL, where)  51.2 us
    ppermute x43, waiting for transfers between devices, send(): return lax.ppermute(values, ALL, where)  29.5 us
    unnamed x155, local copies, waits for them, and re-layouts  10.9 us
    all_to_all x1, starting transfers between devices, body(): lax.all_to_all(outgoing, ALL, split_axis=0, concat_axis=0, tiled=True)  7.68 us
    slice x7, local copies, waits for them, and re-layouts, zero_of(): return values[(0,) * values.ndim] * 0  4.94 us
    convert_element_type x2, other arithmetic, body(): (total_of(term) + follow).astype(BF16)  4.5 us
  transfers between devices with their start and end apart: 44, of which 13 were waited for; matrix products, arithmetic and copies ran while one was open for 10% of the time, Pallas kernels for 37%

profile of v5, /device:TPU:1, one launch (start us, length us, event | category | flops | bytes accessed | tf_op | source)
XLA Modules:
  0.0 222.7 jit_solution(16728808298893596047)
XLA Ops:
  0.7 2.2 collective-permute-start
  2.9 1.9 collective-permute-start.7
  8.2 1.2 broadcast_select_fusion.4
  10.4 1.6 collective-permute-start.1
  12.0 1.3 collective-permute-done.6
  14.2 3.5 %collective-permute-start.8 = (bf16[2,48,3072]{2,1,0:T(8,128)(2,1)}, bf16[2,48,3072]{2,1,0:T(8,128)(2,1)S(1)}, u32[]{:S(2)}, u32[]{:S(2)}) collective-permute-start(bf16[2,48,3072]{2,1,0:T(8,128)(2,1)} %get-tuple-element.80), channel_id=1, source_target_pairs={{0,24},{1,7},{2,26},{3,5},{4,28},{5,3},{6,30},{7,1},{8,16},{9,15},... | collective-permute-start | bytes 1769480 | tf_op jit(solution)/shard_map/ppermute | solution.py:552
  19.9 7.7 %all-to-all-start = ((bf16[128,16,128]{2,1,0:T(8,128)(2,1)}), bf16[128,16,128]{2,1,0:T(8,128)(2,1)S(1)}, u32[]{:S(2)}, u32[]{:S(2)}) async-start(bf16[128,16,128]{2,1,0:T(8,128)(2,1)} %select_add_fusion), calls=%async_computation | async-start | bytes 1048576 | tf_op jit(solution)/shard_map/all_to_all | solution.py:670
  28.8 1.6 broadcast_add_fusion.8
  30.4 2.6 %collective-permute-start.4 = (bf16[48,1536]{1,0:T(8,128)(2,1)}, bf16[48,1536]{1,0:T(8,128)(2,1)}, u32[]{:S(2)}, u32[]{:S(2)}) collective-permute-start(bf16[48,1536]{1,0:T(8,128)(2,1)} %broadcast_add_fusion.8), channel_id=1, source_target_pairs={{0,6},{1,25},{2,4},{3,27},{4,2},{5,29},{6,0},{7,31},{8,14},{9,17},... | collective-permute-start | bytes 442376 | tf_op jit(solution)/shard_map/ppermute | solution.py:552
  34.8 3.3 %collective-permute-start.5 = (bf16[2,2,48,3072]{3,2,1,0:T(8,128)(2,1)}, bf16[2,2,48,3072]{3,2,1,0:T(8,128)(2,1)}, u32[]{:S(2)}, u32[]{:S(2)}) collective-permute-start(bf16[2,2,48,3072]{3,2,1,0:T(8,128)(2,1)} %pad_maximum_fusion.1), channel_id=1, source_target_pairs={{0,24},{1,7},{2,26},{3,5},{4,28},{5,3},{6,30},{7,1},{8,16},{9,15},... | collective-permute-start | bytes 3538952 | tf_op jit(solution)/shard_map/ppermute | solution.py:552
  39.2 2.2 %all-to-all-done = bf16[128,16,128]{2,1,0:T(8,128)(2,1)S(1)} async-done(((bf16[128,16,128]{2,1,0:T(8,128)(2,1)}), bf16[128,16,128]{2,1,0:T(8,128)(2,1)S(1)}, u32[]{:S(2)}, u32[]{:S(2)}) %all-to-all-start) | async-done | bytes 524320 | tf_op jit(solution)/shard_map/all_to_all | solution.py:670
  41.5 1.4 copy-done.33
  42.9 5.2 %stem.1 = (f32[512,1536]{1,0:T(8,128)S(1)}, bf16[512,1536]{1,0:T(8,128)(2,1)S(1)}, bf16[512,1536]{1,0:T(8,128)(2,1)S(1)}, bf16[1536,512]{1,0:T(8,128)(2,1)S(1)},...) custom-call(bf16[2,48,3072]{2,1,0:T(8,128)(2,1)S(1)} %collective-permute-done.1.unused.refs_1_,, ...), custom_call_target="tpu_custom_call" | custom-call | flops 805306368 | bytes 14680064 | tf_op jit(solution)/shard_map/stem/pallas_call | solution.py:393
  50.5 4.3 %collective-permute-done.5 = bf16[2,2,48,3072]{3,2,1,0:T(8,128)(2,1)} collective-permute-done((bf16[2,2,48,3072]{3,2,1,0:T(8,128)(2,1)}, bf16[2,2,48,3072]{3,2,1,0:T(8,128)(2,1)}, u32[]{:S(2)}, u32[]{:S(2)}) %collective-permute-start.5) | collective-permute-done | bytes 1179680 | tf_op jit(solution)/shard_map/ppermute | solution.py:552
  54.8 1.4 broadcast_add_fusion.1
  56.9 1.3 broadcast_add_fusion
  59.1 1.2 slice.251
  64.0 1.3 collective-permute-start.10
  65.4 3.0 %collective-permute-start.11 = (bf16[4,48,1536]{2,1,0:T(8,128)(2,1)S(1)}, bf16[4,48,1536]{2,1,0:T(8,128)(2,1)S(1)}, u32[]{:S(2)}, u32[]{:S(2)}) collective-permute-start(bf16[4,48,1536]{2,1,0:T(8,128)(2,1)S(1)} %maximum_add_fusion.refs_0_), channel_id=1, source_target_pairs={{0,16},{1,5},{2,18},{3,7},{4,20},{5,1},{6,22},{7,3},{8,24},{9,13},... | collective-permute-start | bytes 1769480 | tf_op jit(solution)/shard_map/ppermute | solution.py:552
  69.4 13.6 %gate.1 = (f32[512,1536]{1,0:T(8,128)S(1)}, f32[512,1536]{1,0:T(8,128)S(1)}, f32[512,1536]{1,0:T(8,128)S(1)}) custom-call(s32[32]{0:T(128)S(1)} %pad_add_fusion.offsets, s32[4]{0:T(128)S(1)} %copy-done.32, bf16[4,48,3072]{2,1,0:T(8,128)(2,1)S(1)} %get-tuple-element.78.refs_0_, bf16[2,48,3072]{2,1,0:T(8,128)(2,1)S(1)} %collective-permute-done.1.unused.refs_1_, ...), custom_call_target="tpu_custom_call" | custom-call | flops 4831838208 | bytes 23068672 | tf_op jit(solution)/shard_map/gate/pallas_call | solution.py:393
  83.0 1.8 copy-done.54
  84.8 1.7 copy-done.56
  88.6 6.1 %out_grad.1 = (bf16[16,48,1536]{2,1,0:T(8,128)(2,1)S(1)}, bf16[16,48,1536]{2,1,0:T(8,128)(2,1)S(1)}, bf16[512,1536]{1,0:T(8,128)(2,1)S(1)}) custom-call(s32[33]{0:T(128)S(1)} %pad_add_fusion.1.slots, bf16[4,48,1536]{2,1,0:T(8,128)(2,1)S(1)} %collective-permute-done.10.unused_1.refs_1_, bf16[4,48,1536]{2,1,0:T(8,128)(2,1)S(1)} %collective-permute-done.11.unused_2.refs_2_, ...), custom_call_target="tpu_custom_call" | custom-call | flops 38654705664 | bytes 184549376 | tf_op jit(solution)/shard_map/out_grad/pallas_call | solution.py:393
  96.5 14.1 %middle.1 = (f32[512,1536]{1,0:T(8,128)S(1)}, f32[1,1536]{1,0:T(1,128)S(1)}) custom-call(s32[32]{0:T(128)S(1)} %pad_add_fusion.offsets, bf16[4,48,1536]{2,1,0:T(8,128)(2,1)S(1)} %maximum_add_fusion.refs_0_, bf16[4,48,1536]{2,1,0:T(8,128)(2,1)S(1)} %collective-permute-done.10.unused_1.refs_1_, ...), custom_call_target="tpu_custom_call" | custom-call | flops 38654705664 | bytes 218103808 | tf_op jit(solution)/shard_map/middle/pallas_call | solution.py:393
  111.4 2.7 %collective-permute-start.25 = (bf16[4,48,1536]{2,1,0:T(8,128)(2,1)S(1)}, bf16[4,48,1536]{2,1,0:T(8,128)(2,1)S(1)}, u32[]{:S(2)}, u32[]{:S(2)}) collective-permute-start(bf16[4,48,1536]{2,1,0:T(8,128)(2,1)S(1)} %get-tuple-element.72.unused_2), channel_id=1, source_target_pairs={{0,4},{1,17},{2,6},{3,19},{4,0},{5,21},{6,2},{7,23},{8,12},{9,25},... | collective-permute-start | bytes 1769480 | tf_op jit(solution)/shard_map/ppermute | solution.py:552
  114.1 1.2 collective-permute-start.26
  115.3 1.9 copy-done.57
  117.1 9.7 %conv_back.2 = (bf16[512,1024]{1,0:T(8,128)(2,1)S(1)}, bf16[512,1024]{1,0:T(8,128)(2,1)S(1)}, bf16[16,48,2048]{2,1,0:T(8,128)(2,1)S(1)}, bf16[16,48,2048]{2,1,0:T(8,128)(2,1)S(1)}, f32[32,1024]{1,0:T(8,128)S(1)}) custom-call(s32[33]{0:T(128)S(1)} %pad_add_fusion.1.slots, s32[4]{0:T(128)S(1)} %copy-done.32, ...), custom_call_target="tpu_custom_call" | custom-call | flops 51539607552 | bytes 246065824 | tf_op jit(solution)/shard_map/conv_back/pallas_call | solution.py:393
  128.0 5.0 %conv_back.3 = (bf16[512,512]{1,0:T(8,128)(2,1)S(1)}, bf16[512,512]{1,0:T(8,128)(2,1)S(1)}, bf16[16,48,1024]{2,1,0:T(8,128)(2,1)S(1)}, bf16[16,48,1024]{2,1,0:T(8,128)(2,1)S(1)}, f32[32,512]{1,0:T(8,128)S(1)}) custom-call(s32[33]{0:T(128)S(1)} %pad_add_fusion.1.slots, s32[4]{0:T(128)S(1)} %copy-done.32, bf16[4,48,1536]{2,1,0:T(8,128)(2,1)S(1)} %get-tuple-element.73.unused_1, ...), custom_call_target="tpu_custom_call" | custom-call | flops 25769803776 | bytes 123032912 | tf_op jit(solution)/shard_map/conv_back/pallas_call | solution.py:393
  133.7 2.9 %collective-permute-done.31 = f32[16,1536]{1,0:T(8,128)S(1)} collective-permute-done((f32[16,1536]{1,0:T(8,128)S(1)}, f32[16,1536]{1,0:T(8,128)S(1)}, u32[]{:S(2)}, u32[]{:S(2)}) %collective-permute-start.31) | collective-permute-done | bytes 98336 | tf_op jit(solution)/shard_map/ppermute | solution.py:552
  136.8 3.0 %chip_sum.1 = (bf16[4,48,3072]{2,1,0:T(8,128)(2,1)S(1)}, bf16[4,48,3072]{2,1,0:T(8,128)(2,1)}, bf16[4,48,3072]{2,1,0:T(8,128)(2,1)}, bf16[4,48,3072]{2,1,0:T(8,128)(2,1)}) custom-call(bf16[4,4,48,2048]{3,2,1,0:T(8,128)(2,1)S(1)} %bitcast.50, bf16[4,4,48,2048]{3,2,1,0:T(8,128)(2,1)S(1)} %bitcast.51, bf16[4,4,48,1024]{3,2,1,0:T(8,128)(2,1)S(1)} %bitcast.54, ...), custom_call_target="tpu_custom_call" | custom-call | flops 2359296 | bytes 14680064 | tf_op jit(solution)/shard_map/chip_sum/pallas_call | solution.py:393
  140.9 1.5 collective-permute-start.30
  142.4 1.7 collective-permute-start.28
  144.2 16.7 %stem_back.1 = (f32[1,1536]{1,0:T(1,128)S(1)}, f32[16,48]{1,0:T(8,128)S(1)}) custom-call(s32[32]{0:T(128)S(1)} %pad_add_fusion.offsets, s32[4]{0:T(128)S(1)} %copy-done.32, bf16[4,48,3072]{2,1,0:T(8,128)(2,1)S(1)} %copy-done.19, bf16[2,48,3072]{2,1,0:T(8,128)(2,1)S(1)} %copy-done.12, bf16[2,48,3072]{2,1,0:T(8,128)(2,1)S(1)} %copy-done.14, ...), custom_call_target="tpu_custom_call" | custom-call | flops 77309411328 | bytes 335544320 | tf_op jit(solution)/shard_map/stem_back/pallas_call | solution.py:393
  162.3 1.7 add_convert_fusion.1
  164.0 6.4 %collective-permute-done.30 = bf16[4,48,3072]{2,1,0:T(8,128)(2,1)} collective-permute-done((bf16[4,48,3072]{2,1,0:T(8,128)(2,1)}, bf16[4,48,3072]{2,1,0:T(8,128)(2,1)}, u32[]{:S(2)}, u32[]{:S(2)}) %collective-permute-start.30) | collective-permute-done | bytes 1179680 | tf_op jit(solution)/shard_map/ppermute | solution.py:552
  171.1 2.8 %add_convert_fusion = bf16[4,48,3072]{2,1,0:T(8,128)(2,1)S(1)} fusion(bf16[4,48,3072]{2,1,0:T(8,128)(2,1)} %collective-permute-done.30, bf16[4,48,3072]{2,1,0:T(8,128)(2,1)} %collective-permute-done.29, bf16[4,48,3072]{2,1,0:T(8,128)(2,1)} %collective-permute-done.28, bf16[4,48,3072]{2,1,0:T(8,128)(2,1)S(1)} %copy-done.21, f32[]{:T(128)} %bitcast.28), kind=kLoop, calls=%fused_computation.1 | loop fusion | flops 5308416 | bytes 5898244 | tf_op jit(solution)/shard_map/convert_element_type | solution.py:703
  174.7 2.6 %collective-permute-start.34 = (bf16[56,4608]{1,0:T(8,128)(2,1)S(1)}, bf16[56,4608]{1,0:T(8,128)(2,1)S(1)}, u32[]{:S(2)}, u32[]{:S(2)}) collective-permute-start(bf16[56,4608]{1,0:T(8,128)(2,1)S(1)} %get-tuple-element.75), channel_id=1, source_target_pairs={{0,24},{1,7},{2,26},{3,5},{4,28},{5,3},{6,30},{7,1},{8,16},{9,15},... | collective-permute-start | bytes 1548296 | tf_op jit(solution)/shard_map/ppermute | solution.py:552
  178.5 11.8 %mixed.1.refs_1_ = bf16[512,1536]{1,0:T(8,128)(2,1)} custom-call(s32[32]{0:T(128)S(1)} %pad_add_fusion.offsets, s32[4]{0:T(128)S(1)} %copy-done.32, bf16[4,48,1536]{2,1,0:T(8,128)(2,1)S(1)} %copy-done.4, bf16[4,48,1536]{2,1,0:T(8,128)(2,1)S(1)} %copy-done.6, bf16[4,48,1536]{2,1,0:T(8,128)(2,1)S(1)} %copy-done.8, bf16[4,48,1536]{2,1,0:T(8,128)(2,1)S(1)} %copy-done.10, ...), custom_call_target="tpu_custom_call" | custom-call | flops 2415919104 | bytes 10485760 | tf_op jit(solution)/shard_map/mixed/pallas_call | solution.py:393
  190.3 1.4 copy-done.2
  192.0 2.5 %collective-permute-start.37 = (bf16[56,2304]{1,0:T(8,128)(2,1)S(1)}, bf16[56,2304]{1,0:T(8,128)(2,1)S(1)}, u32[]{:S(2)}, u32[]{:S(2)}) collective-permute-start(bf16[56,2304]{1,0:T(8,128)(2,1)S(1)} %get-tuple-element.85), channel_id=1, source_target_pairs={{0,96},{1,97},{2,98},{3,99},{4,100},{5,101},{6,102},{7,103},{8,104... | collective-permute-start | bytes 774152 | tf_op jit(solution)/shard_map/ppermute | solution.py:552
  194.5 5.0 %collective-permute-done.37 = bf16[56,2304]{1,0:T(8,128)(2,1)S(1)} collective-permute-done((bf16[56,2304]{1,0:T(8,128)(2,1)S(1)}, bf16[56,2304]{1,0:T(8,128)(2,1)S(1)}, u32[]{:S(2)}, u32[]{:S(2)}) %collective-permute-start.37) | collective-permute-done | bytes 258080 | tf_op jit(solution)/shard_map/ppermute | solution.py:552
  200.6 1.6 collective-permute-start.36
  202.2 4.9 %collective-permute-done.36 = bf16[56,2304]{1,0:T(8,128)(2,1)S(1)} collective-permute-done((bf16[56,2304]{1,0:T(8,128)(2,1)S(1)}, bf16[56,2304]{1,0:T(8,128)(2,1)S(1)}, u32[]{:S(2)}, u32[]{:S(2)}) %collective-permute-start.36) | collective-permute-done | bytes 258080 | tf_op jit(solution)/shard_map/ppermute | solution.py:552
  207.5 1.4 collective-permute-start.41
  208.8 2.0 collective-permute-start.39
  211.9 1.6 collective-permute-done.40
  213.6 6.1 %collective-permute-start.42 = (f32[18,1536]{1,0:T(8,128)S(1)}, f32[18,1536]{1,0:T(8,128)S(1)}, u32[]{:S(2)}, u32[]{:S(2)}) collective-permute-start(f32[18,1536]{1,0:T(8,128)S(1)} %convert_add_fusion.3), channel_id=1, source_target_pairs={{0,1},{1,0},{2,3},{3,2},{4,5},{5,4},{6,7},{7,6},{8,9},{9,8},{10,11... | collective-permute-start | bytes 331784 | tf_op jit(solution)/shard_map/ppermute | solution.py:552
  (269 shorter events, 32.1 us)
Async XLA Ops:
  0.7 8.8 %collective-permute-start = (bf16[48,3072]{1,0:T(8,128)(2,1)}, bf16[48,3072]{1,0:T(8,128)(2,1)S(1)}, u32[]{:S(2)}, u32[]{:S(2)}) collective-permute-start(bf16[48,3072]{1,0:T(8,128)(2,1)} %param.25), channel_id=1, source_target_pairs={{0,2},{1,9},{2,0},{3,11},{4,6},{5,13},{6,4},{7,15},{8,10},{9,1},{1... | collective-permute-start | bytes 884744 | tf_op jit(solution)/shard_map/ppermute | solution.py:552
  2.9 9.1 %collective-permute-start.7 = (bf16[48,3072]{1,0:T(8,128)(2,1)}, bf16[48,3072]{1,0:T(8,128)(2,1)S(1)}, u32[]{:S(2)}, u32[]{:S(2)}) collective-permute-start(bf16[48,3072]{1,0:T(8,128)(2,1)} %param.25), channel_id=1, source_target_pairs={{0,6},{1,25},{2,4},{3,27},{4,2},{5,29},{6,0},{7,31},{8,14},{9,17},... | collective-permute-start | bytes 884744 | tf_op jit(solution)/shard_map/ppermute | solution.py:552
  4.8 8.5 %collective-permute-start.6 = (bf16[48,3072]{1,0:T(8,128)(2,1)}, bf16[48,3072]{1,0:T(8,128)(2,1)S(1)}, u32[]{:S(2)}, u32[]{:S(2)}) collective-permute-start(bf16[48,3072]{1,0:T(8,128)(2,1)} %param.25), channel_id=1, source_target_pairs={{0,4},{1,17},{2,6},{3,19},{4,0},{5,21},{6,2},{7,23},{8,12},{9,25},... | collective-permute-start | bytes 884744 | tf_op jit(solution)/shard_map/ppermute | solution.py:552
  7.5 33.9 %copy-start.30 = (f32[1,1536]{1,0:T(1,128)}, f32[1,1536]{1,0:T(1,128)S(1)}, u32[]{:S(2)}) copy-start(f32[1,1536]{1,0:T(1,128)S(1)} %broadcast_in_dim.30.first_gain.refs_20_) | copy-start | bytes 18436
  10.4 17.2 %collective-permute-start.1 = (bf16[2,48,3072]{2,1,0:T(8,128)(2,1)}, bf16[2,48,3072]{2,1,0:T(8,128)(2,1)S(1)}, u32[]{:S(2)}, u32[]{:S(2)}) collective-permute-start(bf16[2,48,3072]{2,1,0:T(8,128)(2,1)} %get-tuple-element.82), channel_id=1, source_target_pairs={{0,8},{1,3},{2,10},{3,1},{4,12},{5,7},{6,14},{7,5},{8,0},{9,11},{1... | collective-permute-start | bytes 1769480 | tf_op jit(solution)/shard_map/ppermute | solution.py:552
  14.2 23.9 %collective-permute-start.8 = (bf16[2,48,3072]{2,1,0:T(8,128)(2,1)}, bf16[2,48,3072]{2,1,0:T(8,128)(2,1)S(1)}, u32[]{:S(2)}, u32[]{:S(2)}) collective-permute-start(bf16[2,48,3072]{2,1,0:T(8,128)(2,1)} %get-tuple-element.80), channel_id=1, source_target_pairs={{0,24},{1,7},{2,26},{3,5},{4,28},{5,3},{6,30},{7,1},{8,16},{9,15},... | collective-permute-start | bytes 1769480 | tf_op jit(solution)/shard_map/ppermute | solution.py:552
  19.9 21.6 %all-to-all-start = ((bf16[128,16,128]{2,1,0:T(8,128)(2,1)}), bf16[128,16,128]{2,1,0:T(8,128)(2,1)S(1)}, u32[]{:S(2)}, u32[]{:S(2)}) async-start(bf16[128,16,128]{2,1,0:T(8,128)(2,1)} %select_add_fusion), calls=%async_computation | async-start | bytes 1048576 | tf_op jit(solution)/shard_map/all_to_all | solution.py:670
  27.6 41.8 %copy-start.11 = (bf16[2,48,3072]{2,1,0:T(8,128)(2,1)}, bf16[2,48,3072]{2,1,0:T(8,128)(2,1)S(1)}, u32[]{:S(2)}) copy-start(bf16[2,48,3072]{2,1,0:T(8,128)(2,1)S(1)} %collective-permute-done.1.unused.refs_1_) | copy-start | bytes 1769476
  30.4 27.9 %collective-permute-start.4 = (bf16[48,1536]{1,0:T(8,128)(2,1)}, bf16[48,1536]{1,0:T(8,128)(2,1)}, u32[]{:S(2)}, u32[]{:S(2)}) collective-permute-start(bf16[48,1536]{1,0:T(8,128)(2,1)} %broadcast_add_fusion.8), channel_id=1, source_target_pairs={{0,6},{1,25},{2,4},{3,27},{4,2},{5,29},{6,0},{7,31},{8,14},{9,17},... | collective-permute-start | bytes 442376 | tf_op jit(solution)/shard_map/ppermute | solution.py:552
  33.0 25.4 %collective-permute-start.3 = (bf16[48,1536]{1,0:T(8,128)(2,1)}, bf16[48,1536]{1,0:T(8,128)(2,1)}, u32[]{:S(2)}, u32[]{:S(2)}) collective-permute-start(bf16[48,1536]{1,0:T(8,128)(2,1)} %broadcast_add_fusion.8), channel_id=1, source_target_pairs={{0,4},{1,17},{2,6},{3,19},{4,0},{5,21},{6,2},{7,23},{8,12},{9,25},... | collective-permute-start | bytes 442376 | tf_op jit(solution)/shard_map/ppermute | solution.py:552
  33.6 25.4 %collective-permute-start.2 = (bf16[48,1536]{1,0:T(8,128)(2,1)}, bf16[48,1536]{1,0:T(8,128)(2,1)}, u32[]{:S(2)}, u32[]{:S(2)}) collective-permute-start(bf16[48,1536]{1,0:T(8,128)(2,1)} %broadcast_add_fusion.8), channel_id=1, source_target_pairs={{0,2},{1,9},{2,0},{3,11},{4,6},{5,13},{6,4},{7,15},{8,10},{9,1},{1... | collective-permute-start | bytes 442376 | tf_op jit(solution)/shard_map/ppermute | solution.py:552
  34.8 20.0 %collective-permute-start.5 = (bf16[2,2,48,3072]{3,2,1,0:T(8,128)(2,1)}, bf16[2,2,48,3072]{3,2,1,0:T(8,128)(2,1)}, u32[]{:S(2)}, u32[]{:S(2)}) collective-permute-start(bf16[2,2,48,3072]{3,2,1,0:T(8,128)(2,1)} %pad_maximum_fusion.1), channel_id=1, source_target_pairs={{0,24},{1,7},{2,26},{3,5},{4,28},{5,3},{6,30},{7,1},{8,16},{9,15},... | collective-permute-start | bytes 3538952 | tf_op jit(solution)/shard_map/ppermute | solution.py:552
  39.2 16.9 %collective-permute-start.9 = (bf16[2,2,48,3072]{3,2,1,0:T(8,128)(2,1)}, bf16[2,2,48,3072]{3,2,1,0:T(8,128)(2,1)}, u32[]{:S(2)}, u32[]{:S(2)}) collective-permute-start(bf16[2,2,48,3072]{3,2,1,0:T(8,128)(2,1)} %pad_maximum_fusion.2), channel_id=1, source_target_pairs={{0,8},{1,3},{2,10},{3,1},{4,12},{5,7},{6,14},{7,5},{8,0},{9,11},{1... | collective-permute-start | bytes 3538952 | tf_op jit(solution)/shard_map/ppermute | solution.py:552
  48.1 48.4 %copy-start.53 = (bf16[512,1536]{1,0:T(8,128)(2,1)}, bf16[512,1536]{1,0:T(8,128)(2,1)S(1)}, u32[]{:S(2)}) copy-start(bf16[512,1536]{1,0:T(8,128)(2,1)S(1)} %get-tuple-element.41.mix_grad.refs_9_.refs_19_) | copy-start | bytes 4718596
  54.8 13.6 %collective-permute-start.14 = (bf16[4,48,3072]{2,1,0:T(8,128)(2,1)S(1)}, bf16[4,48,3072]{2,1,0:T(8,128)(2,1)S(1)}, u32[]{:S(2)}, u32[]{:S(2)}) collective-permute-start(bf16[4,48,3072]{2,1,0:T(8,128)(2,1)S(1)} %get-tuple-element.77), channel_id=1, source_target_pairs={{0,1},{1,0},{2,3},{3,2},{4,5},{5,4},{6,7},{7,6},{8,9},{9,8},{10,11... | collective-permute-start | bytes 3538952 | tf_op jit(solution)/shard_map/ppermute | solution.py:552
  56.1 12.3 %collective-permute-start.17 = (bf16[4,48,3072]{2,1,0:T(8,128)(2,1)S(1)}, bf16[4,48,3072]{2,1,0:T(8,128)(2,1)S(1)}, u32[]{:S(2)}, u32[]{:S(2)}) collective-permute-start(bf16[4,48,3072]{2,1,0:T(8,128)(2,1)S(1)} %broadcast_add_fusion.1), channel_id=1, source_target_pairs={{0,1},{1,0},{2,3},{3,2},{4,5},{5,4},{6,7},{7,6},{8,9},{9,8},{10,11... | collective-permute-start | bytes 3538952 | tf_op jit(solution)/shard_map/ppermute | solution.py:552
  58.3 11.1 %collective-permute-start.18 = (bf16[4,48,3072]{2,1,0:T(8,128)(2,1)S(1)}, bf16[4,48,3072]{2,1,0:T(8,128)(2,1)S(1)}, u32[]{:S(2)}, u32[]{:S(2)}) collective-permute-start(bf16[4,48,3072]{2,1,0:T(8,128)(2,1)S(1)} %broadcast_add_fusion), channel_id=1, source_target_pairs={{0,1},{1,0},{2,3},{3,2},{4,5},{5,4},{6,7},{7,6},{8,9},{9,8},{10,11... | collective-permute-start | bytes 3538952 | tf_op jit(solution)/shard_map/ppermute | solution.py:552
  58.4 5.5 %collective-permute-start.15 = (bf16[2,48,3072]{2,1,0:T(8,128)(2,1)S(1)}, bf16[2,48,3072]{2,1,0:T(8,128)(2,1)S(1)}, u32[]{:S(2)}, u32[]{:S(2)}) collective-permute-start(bf16[2,48,3072]{2,1,0:T(8,128)(2,1)S(1)} %broadcast_add_fusion.7), channel_id=1, source_target_pairs={{0,1},{1,0},{2,3},{3,2},{4,5},{5,4},{6,7},{7,6},{8,9},{9,8},{10,11... | collective-permute-start | bytes 1769480 | tf_op jit(solution)/shard_map/ppermute | solution.py:552
  59.0 6.4 %collective-permute-start.16 = (bf16[2,48,3072]{2,1,0:T(8,128)(2,1)S(1)}, bf16[2,48,3072]{2,1,0:T(8,128)(2,1)S(1)}, u32[]{:S(2)}, u32[]{:S(2)}) collective-permute-start(bf16[2,48,3072]{2,1,0:T(8,128)(2,1)S(1)} %broadcast_add_fusion.6), channel_id=1, source_target_pairs={{0,1},{1,0},{2,3},{3,2},{4,5},{5,4},{6,7},{7,6},{8,9},{9,8},{10,11... | collective-permute-start | bytes 1769480 | tf_op jit(solution)/shard_map/ppermute | solution.py:552
  63.9 32.6 %copy-start.3 = (bf16[4,48,1536]{2,1,0:T(8,128)(2,1)}, bf16[4,48,1536]{2,1,0:T(8,128)(2,1)S(1)}, u32[]{:S(2)}) copy-start(bf16[4,48,1536]{2,1,0:T(8,128)(2,1)S(1)} %maximum_add_fusion.refs_0_) | copy-start | bytes 1769476
  64.0 23.7 %collective-permute-start.10 = (bf16[4,48,1536]{2,1,0:T(8,128)(2,1)S(1)}, bf16[4,48,1536]{2,1,0:T(8,128)(2,1)S(1)}, u32[]{:S(2)}, u32[]{:S(2)}) collective-permute-start(bf16[4,48,1536]{2,1,0:T(8,128)(2,1)S(1)} %maximum_add_fusion.refs_0_), channel_id=1, source_target_pairs={{0,8},{1,3},{2,10},{3,1},{4,12},{5,7},{6,14},{7,5},{8,0},{9,11},{1... | collective-permute-start | bytes 1769480 | tf_op jit(solution)/shard_map/ppermute | solution.py:552
  65.4 22.5 %collective-permute-start.11 = (bf16[4,48,1536]{2,1,0:T(8,128)(2,1)S(1)}, bf16[4,48,1536]{2,1,0:T(8,128)(2,1)S(1)}, u32[]{:S(2)}, u32[]{:S(2)}) collective-permute-start(bf16[4,48,1536]{2,1,0:T(8,128)(2,1)S(1)} %maximum_add_fusion.refs_0_), channel_id=1, source_target_pairs={{0,16},{1,5},{2,18},{3,7},{4,20},{5,1},{6,22},{7,3},{8,24},{9,13},... | collective-permute-start | bytes 1769480 | tf_op jit(solution)/shard_map/ppermute | solution.py:552
  68.4 20.1 %collective-permute-start.12 = (bf16[4,48,1536]{2,1,0:T(8,128)(2,1)S(1)}, bf16[4,48,1536]{2,1,0:T(8,128)(2,1)S(1)}, u32[]{:S(2)}, u32[]{:S(2)}) collective-permute-start(bf16[4,48,1536]{2,1,0:T(8,128)(2,1)S(1)} %maximum_add_fusion.refs_0_), channel_id=1, source_target_pairs={{0,24},{1,7},{2,26},{3,5},{4,28},{5,3},{6,30},{7,1},{8,16},{9,15},... | collective-permute-start | bytes 1769480 | tf_op jit(solution)/shard_map/ppermute | solution.py:552
  68.4 28.0 %collective-permute-start.13 = (bf16[4,48,1536]{2,1,0:T(8,128)(2,1)S(1)}, bf16[4,48,1536]{2,1,0:T(8,128)(2,1)S(1)}, u32[]{:S(2)}, u32[]{:S(2)}) collective-permute-start(bf16[4,48,1536]{2,1,0:T(8,128)(2,1)S(1)} %maximum_add_fusion.refs_0_), channel_id=1, source_target_pairs={{0,1},{1,0},{2,3},{3,2},{4,5},{5,4},{6,7},{7,6},{8,9},{9,8},{10,11... | collective-permute-start | bytes 1769480 | tf_op jit(solution)/shard_map/ppermute | solution.py:552
  87.8 8.7 %collective-permute-start.19 = (bf16[4,48,1536]{2,1,0:T(8,128)(2,1)S(1)}, bf16[4,48,1536]{2,1,0:T(8,128)(2,1)S(1)}, u32[]{:S(2)}, u32[]{:S(2)}) collective-permute-start(bf16[4,48,1536]{2,1,0:T(8,128)(2,1)S(1)} %broadcast_add_fusion.5), channel_id=1, source_target_pairs={{0,1},{1,0},{2,3},{3,2},{4,5},{5,4},{6,7},{7,6},{8,9},{9,8},{10,11... | collective-permute-start | bytes 1769480 | tf_op jit(solution)/shard_map/ppermute | solution.py:552
  87.9 8.5 %collective-permute-start.20 = (bf16[4,48,1536]{2,1,0:T(8,128)(2,1)S(1)}, bf16[4,48,1536]{2,1,0:T(8,128)(2,1)S(1)}, u32[]{:S(2)}, u32[]{:S(2)}) collective-permute-start(bf16[4,48,1536]{2,1,0:T(8,128)(2,1)S(1)} %broadcast_add_fusion.4), channel_id=1, source_target_pairs={{0,1},{1,0},{2,3},{3,2},{4,5},{5,4},{6,7},{7,6},{8,9},{9,8},{10,11... | collective-permute-start | bytes 1769480 | tf_op jit(solution)/shard_map/ppermute | solution.py:552
  88.5 7.9 %collective-permute-start.21 = (bf16[4,48,1536]{2,1,0:T(8,128)(2,1)S(1)}, bf16[4,48,1536]{2,1,0:T(8,128)(2,1)S(1)}, u32[]{:S(2)}, u32[]{:S(2)}) collective-permute-start(bf16[4,48,1536]{2,1,0:T(8,128)(2,1)S(1)} %broadcast_add_fusion.3), channel_id=1, source_target_pairs={{0,1},{1,0},{2,3},{3,2},{4,5},{5,4},{6,7},{7,6},{8,9},{9,8},{10,11... | collective-permute-start | bytes 1769480 | tf_op jit(solution)/shard_map/ppermute | solution.py:552
  95.9 14.8 %collective-permute-start.22 = (bf16[16,48,1536]{2,1,0:T(8,128)(2,1)S(1)}, bf16[16,48,1536]{2,1,0:T(8,128)(2,1)S(1)}, u32[]{:S(2)}, u32[]{:S(2)}) collective-permute-start(bf16[16,48,1536]{2,1,0:T(8,128)(2,1)S(1)} %get-tuple-element.43), channel_id=1, source_target_pairs={{0,1},{1,0},{2,3},{3,2},{4,5},{5,4},{6,7},{7,6},{8,9},{9,8},{10,11... | collective-permute-start | bytes 7077896 | tf_op jit(solution)/shard_map/ppermute | solution.py:552
  111.3 21.7 %collective-permute-start.24 = (bf16[4,48,1536]{2,1,0:T(8,128)(2,1)S(1)}, bf16[4,48,1536]{2,1,0:T(8,128)(2,1)S(1)}, u32[]{:S(2)}, u32[]{:S(2)}) collective-permute-start(bf16[4,48,1536]{2,1,0:T(8,128)(2,1)S(1)} %get-tuple-element.73.unused_1), channel_id=1, source_target_pairs={{0,2},{1,9},{2,0},{3,11},{4,6},{5,13},{6,4},{7,15},{8,10},{9,1},{1... | collective-permute-start | bytes 1769480 | tf_op jit(solution)/shard_map/ppermute | solution.py:552
  111.4 21.7 %collective-permute-start.25 = (bf16[4,48,1536]{2,1,0:T(8,128)(2,1)S(1)}, bf16[4,48,1536]{2,1,0:T(8,128)(2,1)S(1)}, u32[]{:S(2)}, u32[]{:S(2)}) collective-permute-start(bf16[4,48,1536]{2,1,0:T(8,128)(2,1)S(1)} %get-tuple-element.72.unused_2), channel_id=1, source_target_pairs={{0,4},{1,17},{2,6},{3,19},{4,0},{5,21},{6,2},{7,23},{8,12},{9,25},... | collective-permute-start | bytes 1769480 | tf_op jit(solution)/shard_map/ppermute | solution.py:552
  114.1 19.0 %collective-permute-start.26 = (bf16[4,48,1536]{2,1,0:T(8,128)(2,1)S(1)}, bf16[4,48,1536]{2,1,0:T(8,128)(2,1)S(1)}, u32[]{:S(2)}, u32[]{:S(2)}) collective-permute-start(bf16[4,48,1536]{2,1,0:T(8,128)(2,1)S(1)} %get-tuple-element.71.unused_3), channel_id=1, source_target_pairs={{0,6},{1,25},{2,4},{3,27},{4,2},{5,29},{6,0},{7,31},{8,14},{9,17},... | collective-permute-start | bytes 1769480 | tf_op jit(solution)/shard_map/ppermute | solution.py:552
  126.8 9.9 %collective-permute-start.23 = (bf16[16,48,2048]{2,1,0:T(8,128)(2,1)S(1)}, bf16[16,48,2048]{2,1,0:T(8,128)(2,1)S(1)}, u32[]{:S(2)}, u32[]{:S(2)}) collective-permute-start(bf16[16,48,2048]{2,1,0:T(8,128)(2,1)S(1)} %get-tuple-element.49), channel_id=1, source_target_pairs={{0,1},{1,0},{2,3},{3,2},{4,5},{5,4},{6,7},{7,6},{8,9},{9,8},{10,11... | collective-permute-start | bytes 9437192 | tf_op jit(solution)/shard_map/ppermute | solution.py:552
  133.1 3.7 %collective-permute-start.27 = (bf16[16,48,1024]{2,1,0:T(8,128)(2,1)S(1)}, bf16[16,48,1024]{2,1,0:T(8,128)(2,1)S(1)}, u32[]{:S(2)}, u32[]{:S(2)}) collective-permute-start(bf16[16,48,1024]{2,1,0:T(8,128)(2,1)S(1)} %after.2), channel_id=1, source_target_pairs={{0,1},{1,0},{2,3},{3,2},{4,5},{5,4},{6,7},{7,6},{8,9},{9,8},{10,11... | collective-permute-start | bytes 4718600 | tf_op jit(solution)/shard_map/ppermute | solution.py:552
  133.5 3.2 %collective-permute-start.31 = (f32[16,1536]{1,0:T(8,128)S(1)}, f32[16,1536]{1,0:T(8,128)S(1)}, u32[]{:S(2)}, u32[]{:S(2)}) collective-permute-start(f32[16,1536]{1,0:T(8,128)S(1)} %broadcast_select_fusion), channel_id=1, source_target_pairs={{0,1},{1,0},{2,3},{3,2},{4,5},{5,4},{6,7},{7,6},{8,9},{9,8},{10,11... | collective-permute-start | bytes 294920 | tf_op jit(solution)/shard_map/ppermute | solution.py:552
  140.9 29.5 %collective-permute-start.30 = (bf16[4,48,3072]{2,1,0:T(8,128)(2,1)}, bf16[4,48,3072]{2,1,0:T(8,128)(2,1)}, u32[]{:S(2)}, u32[]{:S(2)}) collective-permute-start(bf16[4,48,3072]{2,1,0:T(8,128)(2,1)} %get-tuple-element.55.refs_16_), channel_id=1, source_target_pairs={{0,6},{1,25},{2,4},{3,27},{4,2},{5,29},{6,0},{7,31},{8,14},{9,17},... | collective-permute-start | bytes 3538952 | tf_op jit(solution)/shard_map/ppermute | solution.py:552
  142.4 28.0 %collective-permute-start.29 = (bf16[4,48,3072]{2,1,0:T(8,128)(2,1)}, bf16[4,48,3072]{2,1,0:T(8,128)(2,1)}, u32[]{:S(2)}, u32[]{:S(2)}) collective-permute-start(bf16[4,48,3072]{2,1,0:T(8,128)(2,1)} %get-tuple-element.54.refs_15_), channel_id=1, source_target_pairs={{0,4},{1,17},{2,6},{3,19},{4,0},{5,21},{6,2},{7,23},{8,12},{9,25},... | collective-permute-start | bytes 3538952 | tf_op jit(solution)/shard_map/ppermute | solution.py:552
  142.4 28.6 %collective-permute-start.28 = (bf16[4,48,3072]{2,1,0:T(8,128)(2,1)}, bf16[4,48,3072]{2,1,0:T(8,128)(2,1)}, u32[]{:S(2)}, u32[]{:S(2)}) collective-permute-start(bf16[4,48,3072]{2,1,0:T(8,128)(2,1)} %get-tuple-element.53.refs_14_), channel_id=1, source_target_pairs={{0,2},{1,9},{2,0},{3,11},{4,6},{5,13},{6,4},{7,15},{8,10},{9,1},{1... | collective-permute-start | bytes 3538952 | tf_op jit(solution)/shard_map/ppermute | solution.py:552
  174.2 16.1 %collective-permute-start.32 = (bf16[56,4608]{1,0:T(8,128)(2,1)S(1)}, bf16[56,4608]{1,0:T(8,128)(2,1)S(1)}, u32[]{:S(2)}, u32[]{:S(2)}) collective-permute-start(bf16[56,4608]{1,0:T(8,128)(2,1)S(1)} %get-tuple-element.74), channel_id=1, source_target_pairs={{0,8},{1,3},{2,10},{3,1},{4,12},{5,7},{6,14},{7,5},{8,0},{9,11},{1... | collective-permute-start | bytes 1548296 | tf_op jit(solution)/shard_map/ppermute | solution.py:552
  174.7 16.9 %collective-permute-start.34 = (bf16[56,4608]{1,0:T(8,128)(2,1)S(1)}, bf16[56,4608]{1,0:T(8,128)(2,1)S(1)}, u32[]{:S(2)}, u32[]{:S(2)}) collective-permute-start(bf16[56,4608]{1,0:T(8,128)(2,1)S(1)} %get-tuple-element.75), channel_id=1, source_target_pairs={{0,24},{1,7},{2,26},{3,5},{4,28},{5,3},{6,30},{7,1},{8,16},{9,15},... | collective-permute-start | bytes 1548296 | tf_op jit(solution)/shard_map/ppermute | solution.py:552
  177.3 14.4 %collective-permute-start.33 = (bf16[56,4608]{1,0:T(8,128)(2,1)S(1)}, bf16[56,4608]{1,0:T(8,128)(2,1)S(1)}, u32[]{:S(2)}, u32[]{:S(2)}) collective-permute-start(bf16[56,4608]{1,0:T(8,128)(2,1)S(1)} %get-tuple-element.76), channel_id=1, source_target_pairs={{0,16},{1,5},{2,18},{3,7},{4,20},{5,1},{6,22},{7,3},{8,24},{9,13},... | collective-permute-start | bytes 1548296 | tf_op jit(solution)/shard_map/ppermute | solution.py:552
  192.0 7.6 %collective-permute-start.37 = (bf16[56,2304]{1,0:T(8,128)(2,1)S(1)}, bf16[56,2304]{1,0:T(8,128)(2,1)S(1)}, u32[]{:S(2)}, u32[]{:S(2)}) collective-permute-start(bf16[56,2304]{1,0:T(8,128)(2,1)S(1)} %get-tuple-element.85), channel_id=1, source_target_pairs={{0,96},{1,97},{2,98},{3,99},{4,100},{5,101},{6,102},{7,103},{8,104... | collective-permute-start | bytes 774152 | tf_op jit(solution)/shard_map/ppermute | solution.py:552
  194.5 6.0 %collective-permute-start.35 = (bf16[56,2304]{1,0:T(8,128)(2,1)S(1)}, bf16[56,2304]{1,0:T(8,128)(2,1)S(1)}, u32[]{:S(2)}, u32[]{:S(2)}) collective-permute-start(bf16[56,2304]{1,0:T(8,128)(2,1)S(1)} %get-tuple-element.86), channel_id=1, source_target_pairs={{0,32},{1,33},{2,34},{3,35},{4,36},{5,37},{6,38},{7,39},{8,40},{9,... | collective-permute-start | bytes 774152 | tf_op jit(solution)/shard_map/ppermute | solution.py:552
  200.6 6.5 %collective-permute-start.36 = (bf16[56,2304]{1,0:T(8,128)(2,1)S(1)}, bf16[56,2304]{1,0:T(8,128)(2,1)S(1)}, u32[]{:S(2)}, u32[]{:S(2)}) collective-permute-start(bf16[56,2304]{1,0:T(8,128)(2,1)S(1)} %get-tuple-element.84), channel_id=1, source_target_pairs={{0,96},{1,97},{2,98},{3,99},{4,100},{5,101},{6,102},{7,103},{8,104... | collective-permute-start | bytes 774152 | tf_op jit(solution)/shard_map/ppermute | solution.py:552
  202.2 5.2 %collective-permute-start.38 = (bf16[56,2304]{1,0:T(8,128)(2,1)S(1)}, bf16[56,2304]{1,0:T(8,128)(2,1)S(1)}, u32[]{:S(2)}, u32[]{:S(2)}) collective-permute-start(bf16[56,2304]{1,0:T(8,128)(2,1)S(1)} %get-tuple-element.83), channel_id=1, source_target_pairs={{0,32},{1,33},{2,34},{3,35},{4,36},{5,37},{6,38},{7,39},{8,40},{9,... | collective-permute-start | bytes 774152 | tf_op jit(solution)/shard_map/ppermute | solution.py:552
  207.5 4.5 %collective-permute-start.41 = (bf16[18,1536]{1,0:T(8,128)(2,1)S(1)}, bf16[18,1536]{1,0:T(8,128)(2,1)S(1)}, u32[]{:S(2)}, u32[]{:S(2)}) collective-permute-start(bf16[18,1536]{1,0:T(8,128)(2,1)S(1)} %get-tuple-element.69), channel_id=1, source_target_pairs={{0,6},{1,25},{2,4},{3,27},{4,2},{5,29},{6,0},{7,31},{8,14},{9,17},... | collective-permute-start | bytes 165896 | tf_op jit(solution)/shard_map/ppermute | solution.py:552
  208.8 4.7 %collective-permute-start.40 = (bf16[18,1536]{1,0:T(8,128)(2,1)S(1)}, bf16[18,1536]{1,0:T(8,128)(2,1)S(1)}, u32[]{:S(2)}, u32[]{:S(2)}) collective-permute-start(bf16[18,1536]{1,0:T(8,128)(2,1)S(1)} %get-tuple-element.69), channel_id=1, source_target_pairs={{0,4},{1,17},{2,6},{3,19},{4,0},{5,21},{6,2},{7,23},{8,12},{9,25},... | collective-permute-start | bytes 165896 | tf_op jit(solution)/shard_map/ppermute | solution.py:552
  208.8 4.7 %collective-permute-start.39 = (bf16[18,1536]{1,0:T(8,128)(2,1)S(1)}, bf16[18,1536]{1,0:T(8,128)(2,1)S(1)}, u32[]{:S(2)}, u32[]{:S(2)}) collective-permute-start(bf16[18,1536]{1,0:T(8,128)(2,1)S(1)} %get-tuple-element.69), channel_id=1, source_target_pairs={{0,2},{1,9},{2,0},{3,11},{4,6},{5,13},{6,4},{7,15},{8,10},{9,1},{1... | collective-permute-start | bytes 165896 | tf_op jit(solution)/shard_map/ppermute | solution.py:552
  213.6 7.1 %collective-permute-start.42 = (f32[18,1536]{1,0:T(8,128)S(1)}, f32[18,1536]{1,0:T(8,128)S(1)}, u32[]{:S(2)}, u32[]{:S(2)}) collective-permute-start(f32[18,1536]{1,0:T(8,128)S(1)} %convert_add_fusion.3), channel_id=1, source_target_pairs={{0,1},{1,0},{2,3},{3,2},{4,5},{5,4},{6,7},{7,6},{8,9},{9,8},{10,11... | collective-permute-start | bytes 331784 | tf_op jit(solution)/shard_map/ppermute | solution.py:552
  (68 other events, 494.9 us)
